TPU v7x, 128 devices: a whole 4x4x4 slice. The times are simulated.
128 devices in a mesh: ctx: 16 (over z, y_lo, core), tp: 8 (over y_hi, x).
Axes of the slice: x: 4, y: 4 (y_hi: 2, y_lo: 2; y = y_hi * 2 + y_lo), z: 4, core: 2. Of those that a mesh axis runs over, the one named last changes fastest.
Arguments:
- query_in: bfloat16 [4096, 8192], P('ctx', 'tp'), may hold values from -6 to 6
- key_in: bfloat16 [4096, 8192], P('ctx', 'tp'), may hold values from -6 to 6
- value_in: bfloat16 [4096, 8192], P('ctx', 'tp'), may hold values from -6 to 6
- short_filter: float32 [3, 7, 8192], P(None, None, 'tp'), may hold values from -2 to 2
- long_filter: bfloat16 [128, 512], P(None, 'tp'), may hold values from -0.5 to 0.5
- skip_gain: float32 [8192], P('tp'), may hold values from 0.5 to 1.5
- out_weight: bfloat16 [8192, 8192], P('tp'), may hold values from -0.09375 to 0.09375
- grad_output: bfloat16 [4096, 8192], P('ctx', 'tp'), may hold values from -6 to 6
Outputs:
- output: bfloat16 [4096, 8192], P('ctx', 'tp')
- grad_query: bfloat16 [4096, 8192], P('ctx', 'tp')
- grad_key: bfloat16 [4096, 8192], P('ctx', 'tp')
- grad_value: bfloat16 [4096, 8192], P('ctx', 'tp')
- weight_grad: bfloat16 [8192, 8192], P('tp', 'ctx')
All inputs are finite; a program needn't handle non-finite values.
Results may differ from a plain program's by a relative error of at most 0.023.
Values may be sent and summed in bfloat16 or wider, within the bound.
No kernel may reach another device: no remote copies, remote signals or barrier semaphores. Data moves between devices by JAX's collectives and lax.ppermute only.
A program may use at most 192 MiB of HBM per device.

v0:
```python
import jax
import jax.numpy as jnp
from jax import lax
from jax.sharding import PartitionSpec as P


def passed_along(block, axis, distance):
    devices = range(lax.axis_size(axis))
    route = [(i - distance, i) for i in devices if i - distance in devices]
    return lax.ppermute(block, axis, route)


def short_rows(extended, coeffs, row_count):
    short_len = coeffs.shape[0]
    running = jnp.zeros((row_count, extended.shape[1]), jnp.float32)
    for offset in range(short_len):
        first_row = short_len - 1 - offset
        running = running + coeffs[offset] * extended[first_row : first_row + row_count].astype(
            jnp.float32
        )
    return running


def short_back(extended, coeffs, row_count):
    running = jnp.zeros((row_count, extended.shape[1]), jnp.float32)
    for offset in range(coeffs.shape[0]):
        running = running + coeffs[offset] * extended[offset : offset + row_count]
    return running


def toeplitz_table(long_filter):
    taps_len = long_filter.shape[0]
    shape_all = (taps_len, 2 * taps_len, taps_len)
    row_ids = lax.broadcasted_iota(jnp.int32, shape_all, 0)
    col_ids = lax.broadcasted_iota(jnp.int32, shape_all, 1)
    tap_ids = lax.broadcasted_iota(jnp.int32, shape_all, 2)
    selector = (tap_ids == row_ids + taps_len - col_ids).astype(jnp.bfloat16)
    selector = selector.reshape(2 * taps_len * taps_len, taps_len)
    spread = jnp.dot(selector, long_filter, preferred_element_type=jnp.float32)
    return spread.astype(jnp.bfloat16).reshape(taps_len, 2 * taps_len, long_filter.shape[1])


def causal_blocks(extended, toeplitz):
    taps_len = toeplitz.shape[0]
    groups = toeplitz.shape[2]
    channels = extended.shape[1]
    padded = jnp.concatenate([jnp.zeros((1, channels), extended.dtype), extended], axis=0)
    blocks = padded.shape[0] // taps_len - 1
    lower_half = padded[: blocks * taps_len].reshape(blocks, taps_len, groups, channels // groups)
    upper_half = padded[taps_len:].reshape(blocks, taps_len, groups, channels // groups)
    window = jnp.concatenate([lower_half, upper_half], axis=1)
    result = jnp.einsum("ijg,bjgc->bigc", toeplitz, window, preferred_element_type=jnp.float32)
    return result.reshape(blocks * taps_len, channels)


def anti_blocks(values, rim_after, toeplitz):
    joined = jnp.flip(jnp.concatenate([values, rim_after], axis=0), 0)
    return jnp.flip(causal_blocks(joined, toeplitz), 0)


def on_device(
    query_in, key_in, value_in, short_filter, long_filter, skip_gain, out_weight, grad_output
):
    tok_rows, channels = query_in.shape
    taps_len = long_filter.shape[0]
    long_reach = taps_len - 1
    short_reach = short_filter.shape[1] - 1
    toeplitz = toeplitz_table(long_filter)
    stacked = jnp.stack([query_in, key_in, value_in])
    inner_rows = [
        short_rows(stacked[member], short_filter[member], tok_rows - short_reach)
        for member in range(3)
    ]
    inner_product = (inner_rows[1] * inner_rows[2]).astype(jnp.bfloat16)
    tail_rows = stacked[:, tok_rows - short_reach :]
    product_tail = inner_product[inner_product.shape[0] - long_reach :]
    tail_rim, product_rim = passed_along((tail_rows, product_tail), "ctx", 1)
    head_conv = [
        short_rows(
            jnp.concatenate([tail_rim[member], stacked[member, :short_reach]], axis=0),
            short_filter[member],
            short_reach,
        )
        for member in range(3)
    ]
    query_conv = jnp.concatenate([head_conv[0], inner_rows[0]], axis=0)
    key_conv = jnp.concatenate([head_conv[1], inner_rows[1]], axis=0)
    value_conv = jnp.concatenate([head_conv[2], inner_rows[2]], axis=0)
    kv_product = jnp.concatenate(
        [(head_conv[1] * head_conv[2]).astype(jnp.bfloat16), inner_product], axis=0
    )
    kv_wide = kv_product.astype(jnp.float32)
    carried = (
        causal_blocks(jnp.concatenate([product_rim, kv_product], axis=0), toeplitz)
        + skip_gain * kv_wide
    )
    query_gated = (query_conv * carried).astype(jnp.bfloat16)
    columns = out_weight
    projected = lax.psum_scatter(
        lax.dot_general(
            columns, query_gated, (((0,), (1,)), ((), ())), preferred_element_type=jnp.float32
        ).astype(jnp.bfloat16),
        "tp",
        scatter_dimension=0,
        tiled=True,
    ).astype(jnp.float32)
    output = projected.T.astype(jnp.bfloat16)
    full_grad = lax.all_gather(grad_output, "tp", axis=1, tiled=True)
    grad_gated = lax.dot_general(
        full_grad, out_weight, (((1,), (1,)), ((), ())), preferred_element_type=jnp.float32
    )
    grad_carried = (grad_gated * query_conv).astype(jnp.bfloat16)
    grad_query_conv = grad_gated * carried
    zero_rim = jnp.zeros((long_reach, channels), jnp.bfloat16)
    local_grad = anti_blocks(grad_carried, zero_rim, toeplitz) + skip_gain * grad_carried.astype(
        jnp.float32
    )
    head_grads = jnp.stack(
        [
            grad_query_conv[:short_reach],
            local_grad[:short_reach] * value_conv[:short_reach],
            local_grad[:short_reach] * key_conv[:short_reach],
        ]
    )
    carried_head = grad_carried[:long_reach].astype(jnp.float32)
    carried_rim, head_rim = (
        passed_along(carried_head.astype(jnp.bfloat16), "ctx", -1).astype(carried_head.dtype),
        passed_along(head_grads.astype(jnp.bfloat16), "ctx", -1).astype(head_grads.dtype),
    )
    correction = anti_blocks(
        jnp.zeros((taps_len, channels), jnp.bfloat16), carried_rim.astype(jnp.bfloat16), toeplitz
    )
    split_row = tok_rows - taps_len
    grad_products = jnp.concatenate(
        [local_grad[:split_row], local_grad[split_row:] + correction], axis=0
    )
    conv_grads = [grad_query_conv, grad_products * value_conv, grad_products * key_conv]
    input_grads = [
        short_back(
            jnp.concatenate([conv_grads[member], head_rim[member]], axis=0),
            short_filter[member],
            tok_rows,
        ).astype(jnp.bfloat16)
        for member in range(3)
    ]
    grad_scale = float(tok_rows * lax.axis_size("ctx")) ** (-0.5)
    columns = full_grad
    weight_grad = (
        lax.psum_scatter(
            (
                lax.dot_general(
                    columns,
                    query_gated,
                    (((0,), (0,)), ((), ())),
                    preferred_element_type=jnp.float32,
                )
                * grad_scale
            ).astype(jnp.bfloat16),
            "ctx",
            scatter_dimension=0,
            tiled=True,
        )
        .astype(jnp.float32)
        .T.astype(jnp.bfloat16)
    )
    return (output, input_grads[0], input_grads[1], input_grads[2], weight_grad)


def solution(mesh):
    return jax.shard_map(
        on_device,
        mesh=mesh,
        in_specs=(
            P("ctx", "tp"),
            P("ctx", "tp"),
            P("ctx", "tp"),
            P(None, None, "tp"),
            P(None, "tp"),
            P("tp"),
            P("tp", None),
            P("ctx", "tp"),
        ),
        out_specs=(P("ctx", "tp"), P("ctx", "tp"), P("ctx", "tp"), P("ctx", "tp"), P("tp", "ctx")),
        check_vma=False,
    )
```

profile of v0, /device:TPU:0, one launch (start us, length us, event | category | flops | bytes accessed | tf_op | source)
XLA Modules:
  0.0 416.6 jit_solution(15570839581660005858)
XLA Ops:
  8.8 1.3 collective-permute-start
  10.9 1.4 fusion.96
  12.5 2.9 multiply_convert_fusion.3
  15.5 4.3 %collective-permute-start.1 = (bf16[127,1024]{1,0:T(8,128)(2,1)S(1)}, bf16[127,1024]{1,0:T(8,128)(2,1)S(1)}, u32[]{:S(2)}, u32[]{:S(2)}) collective-permute-start(bf16[127,1024]{1,0:T(8,128)(2,1)S(1)} %slice.488), channel_id=1, source_target_pairs={{0,8},{8,16},{16,24},{24,32},{32,40},{40,48},{48,56},{56,64},{64,7... | collective-permute-start | bytes 780296 | tf_op jit(solution)/shard_map/ppermute | solution.py:10
  20.0 8.3 %convolution_convert_fusion = bf16[32768,64]{0,1:T(8,128)(2,1)S(1)} fusion(bf16[128,64]{0,1:T(8,128)(2,1)S(1)} %copy-done, s32[32768]{0:T(1024)S(1)} %bitcast.135), kind=kOutput, calls=%fused_computation | convolution fusion | flops 543162368 | bytes 4341760 | tf_op jit(solution)/shard_map/dot_general | solution.py:39
  29.9 3.1 copy.34
  33.2 51.2 %all-gather.2.cloned.1.call-done = bf16[256,8192]{1,0:T(8,128)(2,1)} async-done(((bf16[256,1024]{1,0:T(8,128)(2,1)}), bf16[256,8192]{1,0:T(8,128)(2,1)}) %all-gather.2.cloned.1.call-update) | async-done | bytes 4194320 | tf_op jit(solution)/shard_map/all_gather | solution.py:108
  84.4 12.5 %multiply_convert_fusion.1 = (bf16[256,1024]{1,0:T(8,128)(2,1)S(1)}, f32[256,1024]{1,0:T(8,128)}) fusion(f32[250,1024]{1,0:T(8,128)S(1)} %multiply_add_fusion.4, f32[6,1024]{1,0:T(8,128)S(1)} %multiply_add_fusion.7, bf16[256,8192]{1,0:T(8,128)(2,1)} %all-gather.2.cloned.1.call-done, bf16[1024,8192]{1,0:T(8,128)(2,1)} %param.14), kind=kOutput, calls=%fused_computation.107 | convolution fusion | flops 4295753728 | bytes 23592960 | tf_op jit(solution)/shard_map/dot_general | solution.py:109
  98.2 2.4 rev.16
  101.1 3.7 fusion.10
  105.4 1.3 copy.29
  106.8 7.0 %rev.17 = f32[256,1024]{1,0:T(8,128)S(1)} reverse(f32[256,1024]{1,0:T(8,128)} %copy.29), dimensions={0} | reverse | bytes 2097152 | tf_op jit(solution)/shard_map/jit(_flip)/rev | solution.py:58
  115.4 1.4 pad_maximum_fusion.5
  117.4 0.9 reshape.91
  118.3 1.1 copy.21
  119.5 3.7 fusion.7
  123.7 1.0 copy.41
  124.8 2.5 copy.23
  127.3 2.3 fusion.73
  130.4 11.9 %fusion.1 = bf16[8192,256]{0,1:T(8,128)(2,1)} fusion(bf16[256,1024]{1,0:T(8,128)(2,1)S(1)} %get-tuple-element.13, bf16[1024,8192]{1,0:T(8,128)(2,1)} %param.14), kind=kOutput, calls=%fused_computation.5 | convolution fusion | flops 4297064448 | bytes 21495808 | tf_op jit(solution)/shard_map/dot_general | solution.py:100
  142.3 1.0 copy-done.9
  143.3 10.4 %fusion = bf16[8192,1024]{0,1:T(8,128)(2,1)} fusion(bf16[256,1024]{1,0:T(8,128)(2,1)S(1)} %copy-done.9, bf16[256,8192]{1,0:T(8,128)(2,1)} %all-gather.2.cloned.1.call-done), kind=kOutput, calls=%fused_computation.3 | convolution fusion | flops 4311744512 | bytes 21495808 | tf_op jit(solution)/shard_map/dot_general | solution.py:151
  154.4 1.3 collective-permute-start.2
  155.8 1.3 collective-permute-start.3
  157.7 1.7 fusion.51
  159.9 2.0 rev.18
  162.1 3.5 fusion.74
  166.3 1.6 maximum_multiply_fusion.1
  168.0 1.7 fusion.34
  169.7 1.7 fusion.17
  171.4 54.3 %reduce-scatter.3.cloned.1.call-done = bf16[1024,256]{0,1:T(8,128)(2,1)} async-done(((bf16[8192,256]{0,1:T(8,128)(2,1)}), bf16[1024,256]{0,1:T(8,128)(2,1)}) %reduce-scatter.3.cloned.1.call-update) | async-done | bytes 524304 | tf_op jit(solution)/shard_map/reduce_scatter | solution.py:99
  225.7 184.4 %reduce-scatter.5.cloned.1.call-done = bf16[512,1024]{0,1:T(8,128)(2,1)} async-done(((bf16[8192,1024]{0,1:T(8,128)(2,1)}), bf16[512,1024]{0,1:T(8,128)(2,1)}) %reduce-scatter.5.cloned.1.call-update) | async-done | bytes 1048592 | tf_op jit(solution)/shard_map/reduce_scatter | solution.py:149
  (134 shorter events, 12.6 us)
Async XLA Ops:
  7.2 12.9 %copy-start = (bf16[128,64]{0,1:T(8,128)(2,1)S(1)}, bf16[128,64]{0,1:T(8,128)(2,1)}, u32[]{:S(2)}) copy-start(bf16[128,64]{0,1:T(8,128)(2,1)} %param.12) | copy-start | bytes 49156
  7.2 5.3 %copy-start.4 = (bf16[256,1024]{1,0:T(8,128)(2,1)S(1)}, bf16[256,1024]{1,0:T(8,128)(2,1)}, u32[]{:S(2)}) copy-start(bf16[256,1024]{1,0:T(8,128)(2,1)} %param.10) | copy-start | bytes 1572868
  7.2 5.3 %copy-start.2 = (bf16[256,1024]{1,0:T(8,128)(2,1)S(1)}, bf16[256,1024]{1,0:T(8,128)(2,1)}, u32[]{:S(2)}) copy-start(bf16[256,1024]{1,0:T(8,128)(2,1)} %param.9) | copy-start | bytes 1572868
  7.2 77.2 %all-gather.2.cloned.1.call-start = ((), (), s32[]{:S(2)}) async-start(), calls=%async_computation.3 | async-start | bytes 4718592 | tf_op jit(solution)/shard_map/all_gather | solution.py:108
  7.9 217.7 %reduce-scatter.3.cloned.1.call-start = ((), (), s32[]{:S(2)}) async-start(), calls=%async_computation.2 | async-start | bytes 4718592 | tf_op jit(solution)/shard_map/reduce_scatter | solution.py:99
  8.8 24.3 %collective-permute-start = (bf16[3,6,1024]{2,1,0:T(8,128)(2,1)S(1)}, bf16[3,6,1024]{2,1,0:T(8,128)(2,1)S(1)}, u32[]{:S(2)}, u32[]{:S(2)}) collective-permute-start(bf16[3,6,1024]{2,1,0:T(8,128)(2,1)S(1)} %pad_maximum_fusion.9), channel_id=1, source_target_pairs={{0,8},{8,16},{16,24},{24,32},{32,40},{40,48},{48,56},{56,64},{64,7... | collective-permute-start | bytes 110600 | tf_op jit(solution)/shard_map/ppermute | solution.py:10
  10.9 103.8 %copy-start.18 = (f32[1,1,1024]{2,1,0:T(1,128)}, f32[1,1,1024]{2,1,0:T(1,128)S(1)}, u32[]{:S(2)}) copy-start(f32[1,1,1024]{2,1,0:T(1,128)S(1)} %get-tuple-element.42) | copy-start | bytes 12292
  10.9 103.8 %copy-start.20 = (f32[1,1,1024]{2,1,0:T(1,128)}, f32[1,1,1024]{2,1,0:T(1,128)S(1)}, u32[]{:S(2)}) copy-start(f32[1,1,1024]{2,1,0:T(1,128)S(1)} %get-tuple-element.43) | copy-start | bytes 12292
  12.4 20.7 %copy-start.24 = (f32[1,1,1024]{2,1,0:T(1,128)}, f32[1,1,1024]{2,1,0:T(1,128)S(1)}, u32[]{:S(2)}) copy-start(f32[1,1,1024]{2,1,0:T(1,128)S(1)} %get-tuple-element.35) | copy-start | bytes 12292
  12.4 20.7 %copy-start.26 = (f32[1,1,1024]{2,1,0:T(1,128)}, f32[1,1,1024]{2,1,0:T(1,128)S(1)}, u32[]{:S(2)}) copy-start(f32[1,1,1024]{2,1,0:T(1,128)S(1)} %get-tuple-element.36) | copy-start | bytes 12292
  12.4 20.7 %copy-start.28 = (f32[1,1,1024]{2,1,0:T(1,128)}, f32[1,1,1024]{2,1,0:T(1,128)S(1)}, u32[]{:S(2)}) copy-start(f32[1,1,1024]{2,1,0:T(1,128)S(1)} %get-tuple-element.37) | copy-start | bytes 12292
  12.4 20.7 %copy-start.30 = (f32[1,1,1024]{2,1,0:T(1,128)}, f32[1,1,1024]{2,1,0:T(1,128)S(1)}, u32[]{:S(2)}) copy-start(f32[1,1,1024]{2,1,0:T(1,128)S(1)} %get-tuple-element.38) | copy-start | bytes 12292
  12.4 20.7 %copy-start.32 = (f32[1,1,1024]{2,1,0:T(1,128)}, f32[1,1,1024]{2,1,0:T(1,128)S(1)}, u32[]{:S(2)}) copy-start(f32[1,1,1024]{2,1,0:T(1,128)S(1)} %get-tuple-element.39) | copy-start | bytes 12292
  12.4 20.7 %copy-start.34 = (f32[1,1,1024]{2,1,0:T(1,128)}, f32[1,1,1024]{2,1,0:T(1,128)S(1)}, u32[]{:S(2)}) copy-start(f32[1,1,1024]{2,1,0:T(1,128)S(1)} %get-tuple-element.40) | copy-start | bytes 12292
  12.4 20.7 %copy-start.36 = (f32[1,1,1024]{2,1,0:T(1,128)}, f32[1,1,1024]{2,1,0:T(1,128)S(1)}, u32[]{:S(2)}) copy-start(f32[1,1,1024]{2,1,0:T(1,128)S(1)} %get-tuple-element.41) | copy-start | bytes 12292
  12.4 101.6 %copy-start.10 = (f32[1,1,1024]{2,1,0:T(1,128)}, f32[1,1,1024]{2,1,0:T(1,128)S(1)}, u32[]{:S(2)}) copy-start(f32[1,1,1024]{2,1,0:T(1,128)S(1)} %get-tuple-element.31) | copy-start | bytes 12292
  12.4 101.6 %copy-start.12 = (f32[1,1,1024]{2,1,0:T(1,128)}, f32[1,1,1024]{2,1,0:T(1,128)S(1)}, u32[]{:S(2)}) copy-start(f32[1,1,1024]{2,1,0:T(1,128)S(1)} %get-tuple-element.32) | copy-start | bytes 12292
  12.4 101.6 %copy-start.14 = (f32[1,1,1024]{2,1,0:T(1,128)}, f32[1,1,1024]{2,1,0:T(1,128)S(1)}, u32[]{:S(2)}) copy-start(f32[1,1,1024]{2,1,0:T(1,128)S(1)} %get-tuple-element.33) | copy-start | bytes 12292
  12.5 101.6 %copy-start.16 = (f32[1,1,1024]{2,1,0:T(1,128)}, f32[1,1,1024]{2,1,0:T(1,128)S(1)}, u32[]{:S(2)}) copy-start(f32[1,1,1024]{2,1,0:T(1,128)S(1)} %get-tuple-element.34) | copy-start | bytes 12292
  12.5 7.5 %copy-start.3 = (bf16[256,1024]{1,0:T(8,128)(2,1)S(1)}, bf16[256,1024]{1,0:T(8,128)(2,1)}, u32[]{:S(2)}) copy-start(bf16[256,1024]{1,0:T(8,128)(2,1)} %param.8) | copy-start | bytes 1572868
  15.4 13.9 %copy-start.7 = (bf16[250,1024]{1,0:T(8,128)(2,1)}, bf16[250,1024]{1,0:T(8,128)(2,1)S(1)}, u32[]{:S(2)}) copy-start(bf16[250,1024]{1,0:T(8,128)(2,1)S(1)} %get-tuple-element.9) | copy-start | bytes 1536004
  15.5 99.9 %collective-permute-start.1 = (bf16[127,1024]{1,0:T(8,128)(2,1)S(1)}, bf16[127,1024]{1,0:T(8,128)(2,1)S(1)}, u32[]{:S(2)}, u32[]{:S(2)}) collective-permute-start(bf16[127,1024]{1,0:T(8,128)(2,1)S(1)} %slice.488), channel_id=1, source_target_pairs={{0,8},{8,16},{16,24},{24,32},{32,40},{40,48},{48,56},{56,64},{64,7... | collective-permute-start | bytes 780296 | tf_op jit(solution)/shard_map/ppermute | solution.py:10
  29.3 55.1 %copy-start.5 = (f32[250,1024]{1,0:T(8,128)}, f32[250,1024]{1,0:T(8,128)S(1)}, u32[]{:S(2)}) copy-start(f32[250,1024]{1,0:T(8,128)S(1)} %multiply_add_fusion.4) | copy-start | bytes 3072004
  104.8 9.0 %copy-start.38 = (f32[1024]{0:T(1024)S(1)}, f32[1024]{0:T(1024)}, u32[]{:S(2)}) copy-start(f32[1024]{0:T(1024)} %param.13) | copy-start | bytes 12292
  123.2 4.2 copy-start.39
  142.3 267.7 %reduce-scatter.5.cloned.1.call-start = ((), (), s32[]{:S(2)}) async-start(), calls=%async_computation.4 | async-start | bytes 17825792 | tf_op jit(solution)/shard_map/reduce_scatter | solution.py:149
  153.7 3.9 copy-start.29
  153.7 3.9 copy-start.31
  154.4 3.1 collective-permute-start.2
  155.8 4.1 collective-permute-start.3
  162.1 4.2 %copy-start.6 = (f32[250,1024]{1,0:T(8,128)S(1)}, f32[250,1024]{1,0:T(8,128)}, u32[]{:S(2)}) copy-start(f32[250,1024]{1,0:T(8,128)} %get-tuple-element.10) | copy-start | bytes 3072004
  166.3 243.7 %copy-start.1 = (bf16[128,64]{0,1:T(8,128)(2,1)S(1)}, bf16[128,64]{0,1:T(8,128)(2,1)}, u32[]{:S(2)}) copy-start(bf16[128,64]{0,1:T(8,128)(2,1)} %param.12) | copy-start | bytes 49156
  (15 other events, 37.2 us)
Sparse Core Ops, SparseCore 0:
  10.4 74.0 all-gather.1
  142.4 83.1 reduce-scatter.2
  228.6 181.3 reduce-scatter.4
where the time goes:
time: 418 us; the launch traced here: 417 us
  waiting for transfers between devices  292 us (70%)
  matrix products  54.1 us (13%)
  local copies, waits for them, and re-layouts  31.3 us (7%)
  other arithmetic  16.7 us (4%)
  between operations  14.6 us (3%)
  starting transfers between devices  8.3 us (2%)
    reduce_scatter x1, waiting for transfers between devices, on_device(): lax.psum_scatter((lax.dot_general(columns, query_gated, (((0,), (0,)), ((...  184 us
    reduce_scatter x1, waiting for transfers between devices, on_device(): lax.psum_scatter(lax.dot_general(columns, query_gated, (((0,), (1,)), (()...  54.3 us
    all_gather x1, waiting for transfers between devices, on_device(): full_grad = lax.all_gather(grad_output, 'tp', axis=1, tiled=True)  51.2 us
    dot_general x1, matrix products, on_device(): lax.dot_general(full_grad, out_weight, (((1,), (1,)), ((), ())), preferre...  12.5 us
    dot_general x1, matrix products, on_device(): lax.dot_general(columns, query_gated, (((0,), (1,)), ((), ())), preferred...  11.9 us
    dot_general x3, matrix products, causal_blocks(): jnp.einsum('ijg,bjgc->bigc', toeplitz, window, preferred_element_type=jnp...  10.9 us
    dot_general x1, matrix products, on_device(): lax.dot_general(columns, query_gated, (((0,), (0,)), ((), ())), preferred...  10.4 us
  transfers between devices with their start and end apart: 7, of which 5 were waited for; matrix products, arithmetic and copies ran while one was open for 18% of the time, Pallas kernels for 0%

commit v1 on v0

v1 whole, which is shorter than its diff:
```python
import functools

import jax
import jax.numpy as jnp
from jax import lax
from jax.experimental import pallas as pl
from jax.experimental.pallas import tpu as pltpu
from jax.sharding import PartitionSpec as P

Z, YL, CORE, YH, X = 4, 2, 2, 2, 4
F32, BF16 = jnp.float32, jnp.bfloat16
HALO = 144
HEAD = 16
LANES = 128
VMEM_LIMIT = 48 * 1024 * 1024


def ctx_pairs(move):
    pairs = []
    for i in range(Z * YL * CORE):
        z, yl, c = move(i // 4, (i // 2) % 2, i % 2)
        pairs.append((i, (z % Z) * 4 + (yl % YL) * 2 + c % CORE))
    return pairs


def tp_pairs(move):
    pairs = []
    for j in range(YH * X):
        yh, x = move(j // 4, j % 4)
        pairs.append((j, (yh % YH) * 4 + x % X))
    return pairs


def along_x(a, d):
    return lax.ppermute(a, "tp", tp_pairs(lambda yh, x: (yh, x + d)))


def across_yh(a):
    return lax.ppermute(a, "tp", tp_pairs(lambda yh, x: (yh + 1, x)))


def along_z(a, d):
    return lax.ppermute(a, "ctx", ctx_pairs(lambda z, yl, c: (z + d, yl, c)))


def across_core(a):
    return lax.ppermute(a, "ctx", ctx_pairs(lambda z, yl, c: (z, yl, c + 1)))


def next_shard(a, d):
    n = Z * YL * CORE
    return lax.ppermute(a, "ctx", [(i, i + d) for i in range(n) if 0 <= i + d < n])


def to_owner_yl(a, phase):
    pairs = []
    for i in range(Z * YL * CORE):
        for j in range(YH * X):
            parity = (j % X + 1 + phase) % 2
            if (i // 2) % 2 != parity:
                pairs.append((i * YH * X + j, (i ^ 2) * YH * X + j))
    return lax.ppermute(a, ("ctx", "tp"), pairs)


def toeplitz_into(table, rows):
    for g in range(8):
        wide = jnp.broadcast_to(rows[g : g + 1, :], (LANES, 2 * LANES))
        table[g * LANES : (g + 1) * LANES, :] = pltpu.roll(
            wide, 0, 1, stride=1, stride_axis=0
        ).astype(BF16)


def pick_groups(res, rows):
    lane_group = (lax.broadcasted_iota(jnp.int32, (rows, res.shape[1]), 1) % LANES) // 16
    out = res[:rows]
    for g in range(1, 8):
        out = jnp.where(lane_group == g, res[g * rows : (g + 1) * rows], out)
    return out


def forward_kernel(q, k, v, hq, hk, hv, sf, taps, gain, qc_o, ca_o, kc_o, vc_o, qg_o, qgt_o, qs, ks, vs, table):
    n = q.shape[0]
    qs[:HEAD] = hq[...].astype(F32)
    qs[HEAD:] = q[...].astype(F32)
    ks[:HALO] = hk[...].astype(F32)
    ks[HALO:] = k[...].astype(F32)
    vs[:HALO] = hv[...].astype(F32)
    vs[HALO:] = v[...].astype(F32)
    toeplitz_into(table, taps[...])

    def short(scr, member, first, rows):
        acc = sf[member, 0:1, :] * scr[pl.ds(first, rows), :]
        for s in range(1, 7):
            acc = acc + sf[member, s : s + 1, :] * scr[pl.ds(first - s, rows), :]
        return acc

    qc = short(qs, 0, HEAD, n)
    kc = short(ks, 1, HALO - LANES, n + LANES)
    vc = short(vs, 2, HALO - LANES, n + LANES)
    kv = (kc * vc).astype(BF16)
    window = jnp.concatenate([kv[: 2 * LANES], kv[LANES:]], axis=1)
    res = pick_groups(jnp.dot(table[...], window, preferred_element_type=F32), LANES)
    carried = jnp.concatenate([res[:, :LANES], res[:, LANES:]], axis=0)
    carried = carried + gain[...] * kv[LANES:].astype(F32)
    qc_o[...] = qc
    ca_o[...] = carried
    kc_o[...] = kc[LANES:]
    vc_o[...] = vc[LANES:]
    gated = qc * carried
    qg_o[...] = gated.astype(BF16)
    qgt_o[...] = gated.T.astype(BF16)


def forward(q, k, v, hq, hk, hv, sf, taps, gain):
    n, ch = q.shape
    col = lambda rows: pl.BlockSpec((rows, LANES), lambda i: (0, i))
    return pl.pallas_call(
        forward_kernel,
        grid=(ch // LANES,),
        in_specs=[
            col(n), col(n), col(n), col(HEAD), col(HALO), col(HALO),
            pl.BlockSpec((3, 7, LANES), lambda i: (0, 0, i)),
            pl.BlockSpec((8, 2 * LANES), lambda i: (i, 0)),
            col(1),
        ],
        out_specs=[col(n)] * 5 + [pl.BlockSpec((LANES, n), lambda i: (i, 0))],
        out_shape=[jax.ShapeDtypeStruct((n, ch), F32)] * 4
        + [jax.ShapeDtypeStruct((n, ch), BF16), jax.ShapeDtypeStruct((ch, n), BF16)],
        scratch_shapes=[
            pltpu.VMEM((HEAD + n, LANES), F32),
            pltpu.VMEM((HALO + n, LANES), F32),
            pltpu.VMEM((HALO + n, LANES), F32),
            pltpu.VMEM((8 * LANES, 2 * LANES), BF16),
        ],
        compiler_params=pltpu.CompilerParams(vmem_limit_bytes=VMEM_LIMIT),
        cost_estimate=pl.CostEstimate(flops=10**9 * 4, bytes_accessed=8 * 2**20, transcendentals=0),
        name="forward",
    )(q, k, v, hq, hk, hv, sf, taps, gain)


def backward_kernel(gc, gq, vc, kc, hgc, hgq, hvc, hkc, sf, taps, gain, dq_o, dk_o, dv_o, gs, qs, ks, vs, table):
    n = gc.shape[0]
    gs[:n] = gc[...]
    gs[n : n + HALO] = hgc[...]
    gs[n + HALO :] = jnp.zeros((gs.shape[0] - n - HALO, LANES), BF16)
    toeplitz_into(table, taps[...])
    window = jnp.concatenate([gs[: 2 * LANES], gs[LANES : 3 * LANES]], axis=1)
    res = pick_groups(jnp.dot(table[...], window, preferred_element_type=F32), LANES)
    small = jnp.concatenate([table[g * LANES : g * LANES + HEAD] for g in range(8)], axis=0)
    tail = pick_groups(jnp.dot(small, gs[2 * LANES :], preferred_element_type=F32), HEAD)
    gp = jnp.concatenate([res[:, :LANES], res[:, LANES:]], axis=0) + gain[...] * gs[:n].astype(F32)
    gp_tail = tail + gain[...] * gs[n : n + HEAD].astype(F32)
    qs[:n] = gq[...]
    qs[n:] = hgq[...].astype(F32)
    ks[:n] = gp * vc[...]
    ks[n:] = gp_tail * hvc[...].astype(F32)
    vs[:n] = gp * kc[...]
    vs[n:] = gp_tail * hkc[...].astype(F32)

    def short(scr, member):
        acc = sf[member, 0:1, :] * scr[pl.ds(0, n), :]
        for s in range(1, 7):
            acc = acc + sf[member, s : s + 1, :] * scr[pl.ds(s, n), :]
        return acc.astype(BF16)

    dq_o[...] = short(qs, 0)
    dk_o[...] = short(ks, 1)
    dv_o[...] = short(vs, 2)


def backward(gc, gq, vc, kc, hgc, hgq, hvc, hkc, sf, taps, gain):
    n, ch = gc.shape
    col = lambda rows: pl.BlockSpec((rows, LANES), lambda i: (0, i))
    return pl.pallas_call(
        backward_kernel,
        grid=(ch // LANES,),
        in_specs=[
            col(n), col(n), col(n), col(n), col(HALO), col(HEAD), col(HEAD), col(HEAD),
            pl.BlockSpec((3, 7, LANES), lambda i: (0, 0, i)),
            pl.BlockSpec((8, 2 * LANES), lambda i: (i, 0)),
            col(1),
        ],
        out_specs=[col(n)] * 3,
        out_shape=[jax.ShapeDtypeStruct((n, ch), BF16)] * 3,
        scratch_shapes=[
            pltpu.VMEM((4 * LANES, LANES), BF16),
            pltpu.VMEM((n + HEAD, LANES), F32),
            pltpu.VMEM((n + HEAD, LANES), F32),
            pltpu.VMEM((n + HEAD, LANES), F32),
            pltpu.VMEM((8 * LANES, 2 * LANES), BF16),
        ],
        compiler_params=pltpu.CompilerParams(vmem_limit_bytes=VMEM_LIMIT),
        cost_estimate=pl.CostEstimate(flops=10**9 * 4, bytes_accessed=6 * 2**20, transcendentals=0),
        name="backward",
    )(gc, gq, vc, kc, hgc, hgq, hvc, hkc, sf, taps, gain)


def grad_kernel(with_start, cols, blocks, w, *refs):
    start, out, acc = refs if with_start else (None,) + refs
    i = pl.program_id(0)
    part = lax.dot_general(blocks[0], w[...], (((1,), (1,)), ((), ())), preferred_element_type=F32)

    @pl.when(i == 0)
    def _():
        acc[...] = part + start[...] if with_start else part

    @pl.when(i > 0)
    def _():
        acc[...] += part

    @pl.when(i == pl.num_programs(0) - 1)
    def _():
        out[...] = acc[...]


def grad_product(cols, blocks, w, start=None):
    n, rows, width = blocks.shape
    ch = w.shape[0]
    whole = pl.BlockSpec((rows, ch), lambda i, s: (0, 0))
    extra = [] if start is None else [start]
    return pl.pallas_call(
        functools.partial(grad_kernel, start is not None),
        grid_spec=pltpu.PrefetchScalarGridSpec(
            num_scalar_prefetch=1,
            grid=(n,),
            in_specs=[
                pl.BlockSpec((1, rows, width), lambda i, s: (i, 0, 0)),
                pl.BlockSpec((ch, width), lambda i, s: (0, s[i])),
            ]
            + [whole] * len(extra),
            out_specs=whole,
            scratch_shapes=[pltpu.VMEM((rows, ch), F32)],
        ),
        out_shape=jax.ShapeDtypeStruct((rows, ch), F32),
        compiler_params=pltpu.CompilerParams(vmem_limit_bytes=VMEM_LIMIT),
        cost_estimate=pl.CostEstimate(
            flops=2 * n * rows * width * ch, bytes_accessed=2 * n * width * ch, transcendentals=0
        ),
        name="grad_product",
    )(cols, blocks, w, *extra)


def project_kernel(n_add, tops, cols, qg, w, *refs):
    adds, out = refs[:n_add], refs[n_add]
    part = jnp.dot(qg[...], w[...], preferred_element_type=F32)
    if n_add == 2:
        part = part + adds[0][0].astype(F32) + adds[1][0].astype(F32)
    if n_add != 1:
        out[0] = part.astype(BF16)
    else:
        half = part.shape[0] // 2
        i = pl.program_id(0)

        @pl.when(i < tops)
        def _():
            out[0, :half] = (part[:half] + adds[0][0].astype(F32)).astype(BF16)
            out[0, half:] = part[half:].astype(BF16)

        @pl.when(i >= tops)
        def _():
            out[0, :half] = part[:half].astype(BF16)
            out[0, half:] = (part[half:] + adds[0][0].astype(F32)).astype(BF16)


def project(cols, qg, w, adds=()):
    n = cols.shape[0]
    rows, ch = qg.shape
    add_spec = [pl.BlockSpec((1,) + a.shape[1:], lambda i, s: (i, 0, 0)) for a in adds]
    return pl.pallas_call(
        functools.partial(project_kernel, len(adds), n // 2),
        grid_spec=pltpu.PrefetchScalarGridSpec(
            num_scalar_prefetch=1,
            grid=(n,),
            in_specs=[
                pl.BlockSpec((rows, ch), lambda i, s: (0, 0)),
                pl.BlockSpec((ch, ch), lambda i, s: (0, s[i])),
            ]
            + add_spec,
            out_specs=pl.BlockSpec((1, rows, ch), lambda i, s: (i, 0, 0)),
        ),
        out_shape=jax.ShapeDtypeStruct((n, rows, ch), BF16),
        compiler_params=pltpu.CompilerParams(vmem_limit_bytes=VMEM_LIMIT),
        cost_estimate=pl.CostEstimate(
            flops=2 * n * rows * ch * ch, bytes_accessed=2 * n * ch * ch, transcendentals=0
        ),
        name="project",
    )(cols, qg, w, *adds)


def on_device(query_in, key_in, value_in, short_filter, long_filter, skip_gain, out_weight, grad_output):
    n, ch = query_in.shape
    half = ch // 2
    ctx, tp = lax.axis_index("ctx"), lax.axis_index("tp")
    z, yl, c = ctx // 4, (ctx // 2) % 2, ctx % 2
    yh, x = tp // 4, tp % 4
    gain = skip_gain.reshape(1, ch)

    keep = lax.dynamic_slice_in_dim(grad_output, c * half, half, 1)
    give = lax.dynamic_slice_in_dim(grad_output, (1 - c) * half, half, 1)
    own = jnp.stack([keep, across_core(give)])
    r1, l1 = along_x(own, 1), along_x(own, -1)
    other = across_yh(own)
    halo = next_shard(
        jnp.concatenate([query_in[n - HEAD :], key_in[n - HALO :], value_in[n - HALO :]], axis=0), 1
    )
    r2, l2 = along_x(other, 1), along_x(other, -1)
    r3 = along_x(jnp.stack([r1[0], r2[0]]), 1)
    l3 = along_x(jnp.stack([l1[1], l2[1]]), -1)

    taps = long_filter.astype(F32).T
    none = jnp.zeros((taps.shape[0], 1), F32)
    pad = jnp.zeros((taps.shape[0], taps.shape[1] - 1), F32)
    taps_fwd = jnp.concatenate([none, taps[:, ::-1], pad], axis=1)
    taps_bwd = jnp.concatenate([taps, none, pad], axis=1)
    query_conv, carried, key_conv, value_conv, gated, gated_t = forward(
        query_in, key_in, value_in,
        halo[:HEAD], halo[HEAD : HEAD + HALO], halo[HEAD + HALO :],
        short_filter, taps_fwd, gain,
    )

    zr, zl = along_z(gated_t, 1), along_z(gated_t, -1)
    zfar = jnp.concatenate([along_z(zr[: ch // 2], 1), along_z(zl[ch // 2 :], -1)], axis=0)
    mine = jnp.concatenate([gated_t, zr, zl, zfar], axis=1)
    theirs = across_core(mine)

    near = jnp.stack([r1, l1, r2, l2])
    far = jnp.stack([own, jnp.stack([r3[0], l3[0]]), other, jnp.stack([r3[1], l3[1]])])

    def block_cols(dys, dxs, parts):
        dy, dx = jnp.array(dys), jnp.array(dxs)
        return (((yh + dy) % YH) * X + (x + dx) % X).astype(jnp.int32) * parts

    near_cols = block_cols([0, 0, 1, 1], [3, 1, 3, 1], 2) + c
    far_cols = block_cols([0, 0, 1, 1], [0, 2, 0, 2], 2) + c
    w = out_weight
    partial_gg = grad_product(near_cols, near.reshape(4, 2 * n, half), w)
    partial_gg = grad_product(far_cols, far.reshape(4, 2 * n, half), w, partial_gg)

    def for_plane(blocks, d, phase):
        plane = (z + d) % Z
        to_x = 2 * (plane % 2) + (x + 1 + phase) % 2
        dy = (plane // 2 + yh) % 2
        dx = (to_x - x) % X
        place = dy * 2 + (dx == 1 + phase).astype(jnp.int32)
        return lax.dynamic_index_in_dim(blocks, place, 0, keepdims=False)

    def weight_part(blocks, phase):
        got = [for_plane(blocks, 0, phase)] + [
            along_z(for_plane(blocks, d, phase), d) for d in (1, -1, 2)
        ]
        return got

    def weight_sum(got):
        rows_own = jnp.concatenate([g[0] for g in got], axis=0)
        rows_their = jnp.concatenate([g[1] for g in got], axis=0)
        total = jnp.dot(mine, rows_own, preferred_element_type=F32)
        total = total + jnp.dot(theirs, rows_their, preferred_element_type=F32)
        return (total * float(n * Z * YL * CORE) ** -0.5).astype(BF16)

    near_got = weight_part(near, 0)
    far_got = weight_part(far, 1)
    sum_a = weight_sum(near_got)
    recv_a = to_owner_yl(sum_a, 0)

    p2 = project(block_cols([0, 1], [2, 2], 1), gated, w)
    h = n // 2
    got_r = along_x(p2[:, :h], 1)
    got_l = along_x(p2[:, h:], -1)
    p1 = project(
        block_cols([0, 1, 0, 1], [1, 1, 3, 3], 1), gated, w, (jnp.concatenate([got_r, got_l], axis=0),)
    )
    from_r = along_x(p1[:2], 1)
    from_l = along_x(p1[2:], -1)
    p0 = project(block_cols([0, 1], [0, 0], 1), gated, w, (from_r, from_l))
    output = (p0[0].astype(F32) + across_yh(p0[1]).astype(F32)).astype(BF16)

    grad_gated = partial_gg[:n] + across_core(partial_gg[n:].astype(BF16)).astype(F32)
    grad_carried = (grad_gated * query_conv).astype(BF16)
    grad_query_conv = grad_gated * carried
    rim = next_shard(
        jnp.concatenate(
            [
                grad_carried[:HALO],
                grad_query_conv[:HEAD].astype(BF16),
                value_conv[:HEAD].astype(BF16),
                key_conv[:HEAD].astype(BF16),
            ],
            axis=0,
        ),
        -1,
    )
    a, b, d = HALO, HALO + HEAD, HALO + 2 * HEAD
    grad_query, grad_key, grad_value = backward(
        grad_carried, grad_query_conv, value_conv, key_conv,
        rim[:a], rim[a:b], rim[b:d], rim[d:],
        short_filter, taps_bwd, gain,
    )

    sum_b = weight_sum(far_got)
    recv_b = to_owner_yl(sum_b, 1)
    here = jnp.where(yl == (x + 1) % 2, sum_a, sum_b).astype(F32)
    weight_grad = (here + recv_a.astype(F32) + recv_b.astype(F32)).astype(BF16)
    return output, grad_query, grad_key, grad_value, weight_grad


def solution(mesh):
    return jax.shard_map(
        on_device,
        mesh=mesh,
        in_specs=(
            P("ctx", "tp"),
            P("ctx", "tp"),
            P("ctx", "tp"),
            P(None, None, "tp"),
            P(None, "tp"),
            P("tp"),
            P("tp", None),
            P("ctx", "tp"),
        ),
        out_specs=(P("ctx", "tp"), P("ctx", "tp"), P("ctx", "tp"), P("ctx", "tp"), P("tp", "ctx")),
        check_vma=False,
    )
```

time: 418 us -> 209 us (0.50)
  the two profiles are of different devices: /device:TPU:0 before, /device:TPU:27 now
where the time goes in v1:
time: 209 us; the launch traced here: 208 us
  waiting for transfers between devices  70.4 us (34%)
  starting transfers between devices  49.6 us (24%)
  Pallas kernels  40.4 us (19%)
  local copies, waits for them, and re-layouts  20.6 us (10%)
  other arithmetic  12.5 us (6%)
  matrix products  12.4 us (6%)
    ppermute x2, waiting for transfers between devices, next_shard(): lax.ppermute(a, 'ctx', [(i, i + d) for i in range(n) if 0 <= i + d < n])  34.5 us
    ppermute x10, waiting for transfers between devices, along_z(): return lax.ppermute(a, 'ctx', ctx_pairs(lambda z, yl, c: (z + d, yl, c)))  22.3 us
    ppermute x10, starting transfers between devices, along_z(): return lax.ppermute(a, 'ctx', ctx_pairs(lambda z, yl, c: (z + d, yl, c)))  18.9 us
    ppermute x10, waiting for transfers between devices, along_x(): return lax.ppermute(a, 'tp', tp_pairs(lambda yh, x: (yh, x + d)))  13.6 us
    pallas_call x3, Pallas kernels, project(): pl.pallas_call(functools.partial(project_kernel, len(adds), n // 2), grid...  13.6 us
    pallas_call x2, Pallas kernels, grad_product(): pl.pallas_call(functools.partial(grad_kernel, start is not None), grid_sp...  12.7 us
    ppermute x10, starting transfers between devices, along_x(): return lax.ppermute(a, 'tp', tp_pairs(lambda yh, x: (yh, x + d)))  8.51 us
    ppermute x3, starting transfers between devices, across_core(): return lax.ppermute(a, 'ctx', ctx_pairs(lambda z, yl, c: (z, yl, c + 1)))  7.53 us
  transfers between devices with their start and end apart: 29, of which 7 were waited for; matrix products, arithmetic and copies ran while one was open for 19% of the time, Pallas kernels for 19%

profile of v1, /device:TPU:27, one launch (start us, length us, event | category | flops | bytes accessed | tf_op | source)
XLA Modules:
  0.0 208.0 jit_solution(1178147387661269614)
XLA Ops:
  3.5 3.8 %collective-permute-start = (bf16[304,1024]{1,0:T(8,128)(2,1)}, bf16[304,1024]{1,0:T(8,128)(2,1)}, u32[]{:S(2)}, u32[]{:S(2)}) collective-permute-start(bf16[304,1024]{1,0:T(8,128)(2,1)} %pad_maximum_fusion.5), channel_id=1, source_target_pairs={{0,8},{8,16},{16,24},{24,32},{32,40},{40,48},{48,56},{56,64},{64,7... | collective-permute-start | bytes 1867784 | tf_op jit(solution)/shard_map/ppermute | solution.py:52
  10.5 9.3 %collective-permute-done = bf16[304,1024]{1,0:T(8,128)(2,1)} collective-permute-done((bf16[304,1024]{1,0:T(8,128)(2,1)}, bf16[304,1024]{1,0:T(8,128)(2,1)}, u32[]{:S(2)}, u32[]{:S(2)}) %collective-permute-start) | collective-permute-done | bytes 622624 | tf_op jit(solution)/shard_map/ppermute | solution.py:52
  21.7 7.1 %forward.1 = (f32[256,1024]{1,0:T(8,128)S(1)}, f32[256,1024]{1,0:T(8,128)S(1)}, f32[256,1024]{1,0:T(8,128)}, f32[256,1024]{1,0:T(8,128)}, bf16[256,1024]{1,0:T(8,128)(2,1)S(1)}, /*index=5*/bf16[1024,256]{1,0:T(8,128)(2,1)S(1)}) custom-call(bf16[256,1024]{1,0:T(8,128)(2,1)S(1)} %copy-done.3, bf16[256,1024]{1,0:T(8,128)(2,1)S(1)} %copy-done.1, ...), custom_call_target="tpu_custom_call" | custom-call | flops 4000000000 | bytes 8388608 | tf_op jit(solution)/shard_map/forward/pallas_call | solution.py:117
  30.5 3.6 %project.3 = bf16[2,256,1024]{2,1,0:T(8,128)(2,1)S(1)} custom-call(s32[2]{0:T(128)S(1)} %broadcast_add_fusion.cols, bf16[256,1024]{1,0:T(8,128)(2,1)S(1)} %get-tuple-element.14.qg, bf16[1024,8192]{1,0:T(8,128)(2,1)} %w.9), custom_call_target="tpu_custom_call" | custom-call | flops 1073741824 | bytes 4194304 | tf_op jit(solution)/shard_map/project/pallas_call | solution.py:269
  38.7 3.2 %collective-permute-done.17 = bf16[1024,256]{1,0:T(8,128)(2,1)S(1)} collective-permute-done((bf16[1024,256]{1,0:T(8,128)(2,1)S(1)}, bf16[1024,256]{1,0:T(8,128)(2,1)S(1)}, u32[]{:S(2)}, u32[]{:S(2)}) %collective-permute-start.17) | collective-permute-done | bytes 524320 | tf_op jit(solution)/shard_map/ppermute | solution.py:43
  44.6 3.1 %collective-permute-start.18 = (bf16[512,256]{1,0:T(8,128)(2,1)}, bf16[512,256]{1,0:T(8,128)(2,1)}, u32[]{:S(2)}, u32[]{:S(2)}) collective-permute-start(bf16[512,256]{1,0:T(8,128)(2,1)} %slice.227), channel_id=1, source_target_pairs={{0,32},{8,40},{16,48},{24,56},{32,64},{40,72},{48,80},{56,88},{64,... | collective-permute-start | bytes 786440 | tf_op jit(solution)/shard_map/ppermute | solution.py:43
  47.8 6.3 %project.4 = bf16[4,256,1024]{2,1,0:T(8,128)(2,1)S(1)} custom-call(s32[4]{0:T(128)S(1)} %fusion.32.cols, bf16[256,1024]{1,0:T(8,128)(2,1)S(1)} %get-tuple-element.14.qg, bf16[1024,8192]{1,0:T(8,128)(2,1)} %w.9, bf16[4,128,1024]{2,1,0:T(8,128)(2,1)S(1)} %pad_maximum_fusion.4.refs_0_), custom_call_target="tpu_custom_call" | custom-call | flops 2147483648 | bytes 8388608 | tf_op jit(solution)/shard_map/project/pallas_call | solution.py:269
  60.5 5.9 %grad_product.2.refs_0_ = f32[512,1024]{1,0:T(8,128)S(1)} custom-call(s32[4]{0:T(128)S(1)} %get-tuple-element.23.cols, bf16[4,512,512]{2,1,0:T(8,128)(2,1)S(1)} %pad_maximum_fusion.1.blocks, bf16[1024,8192]{1,0:T(8,128)(2,1)} %w.9), custom_call_target="tpu_custom_call" | custom-call | flops 2147483648 | bytes 4194304 | tf_op jit(solution)/shard_map/grad_product/pallas_call | solution.py:221
  70.0 3.3 %collective-permute-start.20 = (bf16[2,256,512]{2,1,0:T(8,128)(2,1)S(1)}, bf16[2,256,512]{2,1,0:T(8,128)(2,1)S(1)}, u32[]{:S(2)}, u32[]{:S(2)}) collective-permute-start(bf16[2,256,512]{2,1,0:T(8,128)(2,1)S(1)} %get-tuple-element.29), channel_id=1, source_target_pairs={{0,32},{8,40},{16,48},{24,56},{32,64},{40,72},{48,80},{56,88},{64,... | collective-permute-start | bytes 1572872 | tf_op jit(solution)/shard_map/ppermute | solution.py:43
  73.3 2.9 %maximum_maximum_fusion = bf16[1024,1024]{1,0:T(8,128)(2,1)} fusion(bf16[512,256]{1,0:T(8,128)(2,1)} %collective-permute-done.19, bf16[512,256]{1,0:T(8,128)(2,1)} %collective-permute-done.18, bf16[1024,256]{1,0:T(8,128)(2,1)S(1)} %collective-permute-done.17, bf16[1024,256]{1,0:T(8,128)(2,1)S(1)} %collective-permute-done.16, ...), kind=kLoop, calls=%fused_computation.2 | loop fusion | flops 10485760 | bytes 4194304 | tf_op jit(solution)/shard_map/concatenate | solution.py:323
  76.2 13.6 %collective-permute-done.13 = bf16[2,256,512]{2,1,0:T(8,128)(2,1)} collective-permute-done((bf16[2,256,512]{2,1,0:T(8,128)(2,1)}, bf16[2,256,512]{2,1,0:T(8,128)(2,1)}, u32[]{:S(2)}, u32[]{:S(2)}) %collective-permute-start.13) | collective-permute-done | bytes 524320 | tf_op jit(solution)/shard_map/ppermute | solution.py:35
  89.8 2.7 %collective-permute-start.22 = (bf16[2,256,512]{2,1,0:T(8,128)(2,1)}, bf16[2,256,512]{2,1,0:T(8,128)(2,1)}, u32[]{:S(2)}, u32[]{:S(2)}) collective-permute-start(bf16[2,256,512]{2,1,0:T(8,128)(2,1)} %get-tuple-element.30), channel_id=1, source_target_pairs={{0,64},{8,72},{16,80},{24,88},{32,96},{40,104},{48,112},{56,120},{... | collective-permute-start | bytes 1572872 | tf_op jit(solution)/shard_map/ppermute | solution.py:43
  93.6 2.6 %collective-permute-start.21 = (bf16[2,256,512]{2,1,0:T(8,128)(2,1)}, bf16[2,256,512]{2,1,0:T(8,128)(2,1)}, u32[]{:S(2)}, u32[]{:S(2)}) collective-permute-start(bf16[2,256,512]{2,1,0:T(8,128)(2,1)} %get-tuple-element.31), channel_id=1, source_target_pairs={{0,96},{8,104},{16,112},{24,120},{32,0},{40,8},{48,16},{56,24},{64... | collective-permute-start | bytes 1572872 | tf_op jit(solution)/shard_map/ppermute | solution.py:43
  96.7 4.3 %collective-permute-start.23 = (bf16[1024,1024]{1,0:T(8,128)(2,1)}, bf16[1024,1024]{1,0:T(8,128)(2,1)}, u32[]{:S(2)}, u32[]{:S(2)}) collective-permute-start(bf16[1024,1024]{1,0:T(8,128)(2,1)} %maximum_maximum_fusion), channel_id=1, source_target_pairs={{0,8},{8,0},{16,24},{24,16},{32,40},{40,32},{48,56},{56,48},{64,72... | collective-permute-start | bytes 6291464 | tf_op jit(solution)/shard_map/ppermute | solution.py:47
  101.8 6.8 %grad_product.3 = f32[512,1024]{1,0:T(8,128)S(1)} custom-call(s32[4]{0:T(128)S(1)} %fusion.45.cols, bf16[4,512,512]{2,1,0:T(8,128)(2,1)S(1)} %pad_maximum_fusion.blocks, bf16[1024,8192]{1,0:T(8,128)(2,1)} %w.9, f32[512,1024]{1,0:T(8,128)} %copy-done), custom_call_target="tpu_custom_call" | custom-call | flops 2147483648 | bytes 4194304 | tf_op jit(solution)/shard_map/grad_product/pallas_call | solution.py:221
  109.7 1.9 slice_bitcast_fusion.11
  111.6 3.1 %collective-permute-done.21 = bf16[2,256,512]{2,1,0:T(8,128)(2,1)} collective-permute-done((bf16[2,256,512]{2,1,0:T(8,128)(2,1)}, bf16[2,256,512]{2,1,0:T(8,128)(2,1)}, u32[]{:S(2)}, u32[]{:S(2)}) %collective-permute-start.21) | collective-permute-done | bytes 524320 | tf_op jit(solution)/shard_map/ppermute | solution.py:43
  114.7 2.5 %collective-permute-start.14 = (bf16[256,1024]{1,0:T(8,128)(2,1)S(1)}, bf16[256,1024]{1,0:T(8,128)(2,1)S(1)}, u32[]{:S(2)}, u32[]{:S(2)}) collective-permute-start(bf16[256,1024]{1,0:T(8,128)(2,1)S(1)} %slice.266), channel_id=1, source_target_pairs={{0,8},{8,0},{16,24},{24,16},{32,40},{40,32},{48,56},{56,48},{64,72... | collective-permute-start | bytes 1572872 | tf_op jit(solution)/shard_map/ppermute | solution.py:47
  117.2 1.9 slice_bitcast_fusion.12
  119.9 3.6 %collective-permute-start.26 = (bf16[2,256,512]{2,1,0:T(8,128)(2,1)S(1)}, bf16[2,256,512]{2,1,0:T(8,128)(2,1)S(1)}, u32[]{:S(2)}, u32[]{:S(2)}) collective-permute-start(bf16[2,256,512]{2,1,0:T(8,128)(2,1)S(1)} %get-tuple-element.35), channel_id=1, source_target_pairs={{0,64},{8,72},{16,80},{24,88},{32,96},{40,104},{48,112},{56,120},{... | collective-permute-start | bytes 1572872 | tf_op jit(solution)/shard_map/ppermute | solution.py:43
  124.9 3.7 %project.5 = bf16[2,256,1024]{2,1,0:T(8,128)(2,1)S(1)} custom-call(s32[2]{0:T(128)S(1)} %broadcast_add_fusion.1.cols, bf16[256,1024]{1,0:T(8,128)(2,1)S(1)} %get-tuple-element.14.qg, bf16[1024,8192]{1,0:T(8,128)(2,1)} %w.9, bf16[2,256,1024]{2,1,0:T(8,128)(2,1)S(1)} %collective-permute-done.3.refs_0_, bf16[2,256,1024]{2,1,0:T(8,128)(2,1)S(1)} %collective-permute-done.4.refs_1_), custom_call_target="tpu_custom_call" | custom-call | flops 1073741824 | bytes 4194304 | tf_op jit(solution)/shard_map/project/pallas_call | solution.py:269
  130.2 5.6 %collective-permute-done.26 = bf16[2,256,512]{2,1,0:T(8,128)(2,1)S(1)} collective-permute-done((bf16[2,256,512]{2,1,0:T(8,128)(2,1)S(1)}, bf16[2,256,512]{2,1,0:T(8,128)(2,1)S(1)}, u32[]{:S(2)}, u32[]{:S(2)}) %collective-permute-start.26) | collective-permute-done | bytes 524320 | tf_op jit(solution)/shard_map/ppermute | solution.py:43
  135.8 10.4 %collective-permute-done.25 = bf16[2,256,512]{2,1,0:T(8,128)(2,1)S(1)} collective-permute-done((bf16[2,256,512]{2,1,0:T(8,128)(2,1)S(1)}, bf16[2,256,512]{2,1,0:T(8,128)(2,1)S(1)}, u32[]{:S(2)}, u32[]{:S(2)}) %collective-permute-start.25) | collective-permute-done | bytes 524320 | tf_op jit(solution)/shard_map/ppermute | solution.py:43
  146.3 3.0 %fusion.7 = f32[1024,512]{1,0:T(8,128)S(1)} fusion(bf16[1024,1024]{1,0:T(8,128)(2,1)} %collective-permute-done.23, bf16[256,512]{1,0:T(8,128)(2,1)S(1)} %copy-done.25, bf16[256,512]{1,0:T(8,128)(2,1)S(1)} %copy-done.27, bf16[256,512]{1,0:T(8,128)(2,1)S(1)} %copy-done.23, bf16[256,512]{1,0:T(8,128)(2,1)S(1)} %copy-done.19), kind=kOutput, calls=%fused_computation.18 | convolution fusion | flops 1077936128 | bytes 5242880 | tf_op jit(solution)/shard_map/dot_general | solution.py:357
  149.4 3.3 %multiply_convert_fusion.1 = bf16[1024,512]{1,0:T(8,128)(2,1)} fusion(f32[1024,512]{1,0:T(8,128)S(1)} %fusion.7, bf16[256,512]{1,0:T(8,128)(2,1)S(1)} %copy-done.24, bf16[256,512]{1,0:T(8,128)(2,1)S(1)} %copy-done.26, bf16[256,512]{1,0:T(8,128)(2,1)S(1)} %copy-done.22, bf16[256,512]{1,0:T(8,128)(2,1)S(1)} %copy-done.18, ...), kind=kOutput, calls=%fused_computation.7 | convolution fusion | flops 1089994752 | bytes 6291456 | tf_op jit(solution)/shard_map/dot_general | solution.py:356
  152.7 5.7 %collective-permute-start.27 = (bf16[1024,512]{1,0:T(8,128)(2,1)}, bf16[1024,512]{1,0:T(8,128)(2,1)}, u32[]{:S(2)}, u32[]{:S(2)}) collective-permute-start(bf16[1024,512]{1,0:T(8,128)(2,1)} %multiply_convert_fusion.1), channel_id=1, source_target_pairs={{0,16},{2,18},{4,20},{6,22},{8,24},{10,26},{12,28},{14,30},{17,1},... | collective-permute-start | bytes 3145736 | tf_op jit(solution)/shard_map/ppermute | solution.py:62
  158.4 2.9 %fusion.22 = f32[1024,512]{1,0:T(8,128)S(1)} fusion(bf16[1024,1024]{1,0:T(8,128)(2,1)} %collective-permute-done.23, bf16[256,512]{1,0:T(8,128)(2,1)S(1)} %get-tuple-element.54, bf16[256,512]{1,0:T(8,128)(2,1)S(1)} %get-tuple-element.52, bf16[256,512]{1,0:T(8,128)(2,1)S(1)} %get-tuple-element.50, bf16[256,512]{1,0:T(8,128)(2,1)S(1)} %copy-done.21), kind=kOutput, calls=%fused_computation.33 | convolution fusion | flops 1077936128 | bytes 5242880 | tf_op jit(solution)/shard_map/dot_general | solution.py:357
  161.3 3.3 %multiply_convert_fusion = bf16[1024,512]{1,0:T(8,128)(2,1)} fusion(f32[1024,512]{1,0:T(8,128)S(1)} %fusion.22, bf16[256,512]{1,0:T(8,128)(2,1)S(1)} %get-tuple-element.53, bf16[256,512]{1,0:T(8,128)(2,1)S(1)} %get-tuple-element.51, bf16[256,512]{1,0:T(8,128)(2,1)S(1)} %get-tuple-element.49, bf16[256,512]{1,0:T(8,128)(2,1)S(1)} %copy-done.20, ...), kind=kOutput, calls=%fused_computation.6 | convolution fusion | flops 1089994752 | bytes 6291456 | tf_op jit(solution)/shard_map/dot_general | solution.py:356
  166.6 3.0 %collective-permute-start.15 = (bf16[192,1024]{1,0:T(8,128)(2,1)}, bf16[192,1024]{1,0:T(8,128)(2,1)}, u32[]{:S(2)}, u32[]{:S(2)}) collective-permute-start(bf16[192,1024]{1,0:T(8,128)(2,1)} %pad_maximum_fusion.11), channel_id=1, source_target_pairs={{8,0},{16,8},{24,16},{32,24},{40,32},{48,40},{56,48},{64,56},{72,6... | collective-permute-start | bytes 1179656 | tf_op jit(solution)/shard_map/ppermute | solution.py:52
  170.7 25.2 %collective-permute-done.15 = bf16[192,1024]{1,0:T(8,128)(2,1)} collective-permute-done((bf16[192,1024]{1,0:T(8,128)(2,1)}, bf16[192,1024]{1,0:T(8,128)(2,1)}, u32[]{:S(2)}, u32[]{:S(2)}) %collective-permute-start.15) | collective-permute-done | bytes 393248 | tf_op jit(solution)/shard_map/ppermute | solution.py:52
  197.7 6.9 %backward.1 = (bf16[256,1024]{1,0:T(8,128)(2,1)}, bf16[256,1024]{1,0:T(8,128)(2,1)}, bf16[256,1024]{1,0:T(8,128)(2,1)}) custom-call(bf16[256,1024]{1,0:T(8,128)(2,1)S(1)} %get-tuple-element.26.gc, f32[256,1024]{1,0:T(8,128)S(1)} %get-tuple-element.25.gq, f32[256,1024]{1,0:T(8,128)S(1)} %copy-done.5, f32[256,1024]{1,0:T(8,128)S(1)} %copy-done.4, ...), custom_call_target="tpu_custom_call" | custom-call | flops 4000000000 | bytes 6291456 | tf_op jit(solution)/shard_map/backward/pallas_call | solution.py:174
  204.6 3.4 %add_convert_fusion = bf16[1024,512]{1,0:T(8,128)(2,1)} fusion(bf16[1024,512]{1,0:T(8,128)(2,1)} %collective-permute-done.28, bf16[1024,512]{1,0:T(8,128)(2,1)} %collective-permute-done.27, bf16[1024,512]{1,0:T(8,128)(2,1)} %multiply_convert_fusion.1, bf16[1024,512]{1,0:T(8,128)(2,1)} %multiply_convert_fusion, pred[]{:T(512)S(6)} %eq.84), kind=kLoop, calls=%fused_computation.5 | loop fusion | flops 3670016 | bytes 5242881 | tf_op jit(solution)/shard_map/convert_element_type | solution.py:402
  (170 shorter events, 38.1 us)
Async XLA Ops:
  1.9 6.4 %collective-permute-start.6 = (bf16[256,512]{1,0:T(8,128)(2,1)S(1)}, bf16[256,512]{1,0:T(8,128)(2,1)S(1)}, u32[]{:S(2)}, u32[]{:S(2)}) collective-permute-start(bf16[256,512]{1,0:T(8,128)(2,1)S(1)} %get-tuple-element.66), channel_id=1, source_target_pairs={{0,8},{8,0},{16,24},{24,16},{32,40},{40,32},{48,56},{56,48},{64,72... | collective-permute-start | bytes 786440 | tf_op jit(solution)/shard_map/ppermute | solution.py:47
  3.5 16.3 %collective-permute-start = (bf16[304,1024]{1,0:T(8,128)(2,1)}, bf16[304,1024]{1,0:T(8,128)(2,1)}, u32[]{:S(2)}, u32[]{:S(2)}) collective-permute-start(bf16[304,1024]{1,0:T(8,128)(2,1)} %pad_maximum_fusion.5), channel_id=1, source_target_pairs={{0,8},{8,16},{16,24},{24,32},{32,40},{40,48},{48,56},{56,64},{64,7... | collective-permute-start | bytes 1867784 | tf_op jit(solution)/shard_map/ppermute | solution.py:52
  8.3 25.9 %collective-permute-start.11 = (bf16[2,256,512]{2,1,0:T(8,128)(2,1)S(1)}, bf16[2,256,512]{2,1,0:T(8,128)(2,1)S(1)}, u32[]{:S(2)}, u32[]{:S(2)}) collective-permute-start(bf16[2,256,512]{2,1,0:T(8,128)(2,1)S(1)} %get-tuple-element.56), channel_id=1, source_target_pairs={{0,3},{1,0},{2,1},{3,2},{4,7},{5,4},{6,5},{7,6},{8,11},{9,8},{10,9... | collective-permute-start | bytes 1572872 | tf_op jit(solution)/shard_map/ppermute | solution.py:35
  8.6 26.9 %collective-permute-start.8 = (bf16[2,256,512]{2,1,0:T(8,128)(2,1)S(1)}, bf16[2,256,512]{2,1,0:T(8,128)(2,1)S(1)}, u32[]{:S(2)}, u32[]{:S(2)}) collective-permute-start(bf16[2,256,512]{2,1,0:T(8,128)(2,1)S(1)} %get-tuple-element.56), channel_id=1, source_target_pairs={{0,4},{1,5},{2,6},{3,7},{4,0},{5,1},{6,2},{7,3},{8,12},{9,13},{10,... | collective-permute-start | bytes 1572872 | tf_op jit(solution)/shard_map/ppermute | solution.py:39
  9.3 28.2 %collective-permute-start.7 = (bf16[2,256,512]{2,1,0:T(8,128)(2,1)S(1)}, bf16[2,256,512]{2,1,0:T(8,128)(2,1)S(1)}, u32[]{:S(2)}, u32[]{:S(2)}) collective-permute-start(bf16[2,256,512]{2,1,0:T(8,128)(2,1)S(1)} %get-tuple-element.56), channel_id=1, source_target_pairs={{0,1},{1,2},{2,3},{3,0},{4,5},{5,6},{6,7},{7,4},{8,9},{9,10},{10,1... | collective-permute-start | bytes 1572872 | tf_op jit(solution)/shard_map/ppermute | solution.py:35
  28.8 13.1 %collective-permute-start.17 = (bf16[1024,256]{1,0:T(8,128)(2,1)S(1)}, bf16[1024,256]{1,0:T(8,128)(2,1)S(1)}, u32[]{:S(2)}, u32[]{:S(2)}) collective-permute-start(bf16[1024,256]{1,0:T(8,128)(2,1)S(1)} %get-tuple-element.22), channel_id=1, source_target_pairs={{0,96},{8,104},{16,112},{24,120},{32,0},{40,8},{48,16},{56,24},{64... | collective-permute-start | bytes 1572872 | tf_op jit(solution)/shard_map/ppermute | solution.py:43
  28.8 15.0 %collective-permute-start.16 = (bf16[1024,256]{1,0:T(8,128)(2,1)S(1)}, bf16[1024,256]{1,0:T(8,128)(2,1)S(1)}, u32[]{:S(2)}, u32[]{:S(2)}) collective-permute-start(bf16[1024,256]{1,0:T(8,128)(2,1)S(1)} %get-tuple-element.22), channel_id=1, source_target_pairs={{0,32},{8,40},{16,48},{24,56},{32,64},{40,72},{48,80},{56,88},{64,... | collective-permute-start | bytes 1572872 | tf_op jit(solution)/shard_map/ppermute | solution.py:43
  34.2 10.4 %collective-permute-start.1 = (bf16[2,128,1024]{2,1,0:T(8,128)(2,1)S(1)}, bf16[2,128,1024]{2,1,0:T(8,128)(2,1)S(1)}, u32[]{:S(2)}, u32[]{:S(2)}) collective-permute-start(bf16[2,128,1024]{2,1,0:T(8,128)(2,1)S(1)} %get-tuple-element.39), channel_id=1, source_target_pairs={{0,1},{1,2},{2,3},{3,0},{4,5},{5,6},{6,7},{7,4},{8,9},{9,10},{10,1... | collective-permute-start | bytes 1572872 | tf_op jit(solution)/shard_map/ppermute | solution.py:35
  35.5 12.2 %collective-permute-start.2 = (bf16[2,128,1024]{2,1,0:T(8,128)(2,1)S(1)}, bf16[2,128,1024]{2,1,0:T(8,128)(2,1)S(1)}, u32[]{:S(2)}, u32[]{:S(2)}) collective-permute-start(bf16[2,128,1024]{2,1,0:T(8,128)(2,1)S(1)} %get-tuple-element.40), channel_id=1, source_target_pairs={{0,3},{1,0},{2,1},{3,2},{4,7},{5,4},{6,5},{7,6},{8,11},{9,8},{10,9... | collective-permute-start | bytes 1572872 | tf_op jit(solution)/shard_map/ppermute | solution.py:35
  37.5 19.4 %collective-permute-start.12 = (bf16[2,256,512]{2,1,0:T(8,128)(2,1)S(1)}, bf16[2,256,512]{2,1,0:T(8,128)(2,1)S(1)}, u32[]{:S(2)}, u32[]{:S(2)}) collective-permute-start(bf16[2,256,512]{2,1,0:T(8,128)(2,1)S(1)} %collective-permute-done.8), channel_id=1, source_target_pairs={{0,3},{1,0},{2,1},{3,2},{4,7},{5,4},{6,5},{7,6},{8,11},{9,8},{10,9... | collective-permute-start | bytes 1572872 | tf_op jit(solution)/shard_map/ppermute | solution.py:35
  41.9 31.4 %copy-start.14 = (bf16[1024,256]{1,0:T(8,128)(2,1)}, bf16[1024,256]{1,0:T(8,128)(2,1)S(1)}, u32[]{:S(2)}) copy-start(bf16[1024,256]{1,0:T(8,128)(2,1)S(1)} %collective-permute-done.17) | copy-start | bytes 1572868
  41.9 17.1 %collective-permute-start.9 = (bf16[2,256,512]{2,1,0:T(8,128)(2,1)S(1)}, bf16[2,256,512]{2,1,0:T(8,128)(2,1)S(1)}, u32[]{:S(2)}, u32[]{:S(2)}) collective-permute-start(bf16[2,256,512]{2,1,0:T(8,128)(2,1)S(1)} %collective-permute-done.8), channel_id=1, source_target_pairs={{0,1},{1,2},{2,3},{3,0},{4,5},{5,6},{6,7},{7,4},{8,9},{9,10},{10,1... | collective-permute-start | bytes 1572872 | tf_op jit(solution)/shard_map/ppermute | solution.py:35
  43.8 29.5 %copy-start.16 = (bf16[1024,256]{1,0:T(8,128)(2,1)}, bf16[1024,256]{1,0:T(8,128)(2,1)S(1)}, u32[]{:S(2)}) copy-start(bf16[1024,256]{1,0:T(8,128)(2,1)S(1)} %collective-permute-done.16) | copy-start | bytes 1572868
  43.8 25.8 %collective-permute-start.19 = (bf16[512,256]{1,0:T(8,128)(2,1)}, bf16[512,256]{1,0:T(8,128)(2,1)}, u32[]{:S(2)}, u32[]{:S(2)}) collective-permute-start(bf16[512,256]{1,0:T(8,128)(2,1)} %slice.228), channel_id=1, source_target_pairs={{0,96},{8,104},{16,112},{24,120},{32,0},{40,8},{48,16},{56,24},{64... | collective-permute-start | bytes 786440 | tf_op jit(solution)/shard_map/ppermute | solution.py:43
  44.6 25.4 %collective-permute-start.18 = (bf16[512,256]{1,0:T(8,128)(2,1)}, bf16[512,256]{1,0:T(8,128)(2,1)}, u32[]{:S(2)}, u32[]{:S(2)}) collective-permute-start(bf16[512,256]{1,0:T(8,128)(2,1)} %slice.227), channel_id=1, source_target_pairs={{0,32},{8,40},{16,48},{24,56},{32,64},{40,72},{48,80},{56,88},{64,... | collective-permute-start | bytes 786440 | tf_op jit(solution)/shard_map/ppermute | solution.py:43
  55.7 64.2 %collective-permute-start.4 = (bf16[2,256,1024]{2,1,0:T(8,128)(2,1)}, bf16[2,256,1024]{2,1,0:T(8,128)(2,1)S(1)}, u32[]{:S(2)}, u32[]{:S(2)}) collective-permute-start(bf16[2,256,1024]{2,1,0:T(8,128)(2,1)} %get-tuple-element.37), channel_id=1, source_target_pairs={{0,3},{1,0},{2,1},{3,2},{4,7},{5,4},{6,5},{7,6},{8,11},{9,8},{10,9... | collective-permute-start | bytes 3145736 | tf_op jit(solution)/shard_map/ppermute | solution.py:35
  57.8 32.0 %collective-permute-start.13 = (bf16[2,256,512]{2,1,0:T(8,128)(2,1)}, bf16[2,256,512]{2,1,0:T(8,128)(2,1)}, u32[]{:S(2)}, u32[]{:S(2)}) collective-permute-start(bf16[2,256,512]{2,1,0:T(8,128)(2,1)} %pad_maximum_fusion.8), channel_id=1, source_target_pairs={{0,3},{1,0},{2,1},{3,2},{4,7},{5,4},{6,5},{7,6},{8,11},{9,8},{10,9... | collective-permute-start | bytes 1572872 | tf_op jit(solution)/shard_map/ppermute | solution.py:35
  59.9 33.7 %collective-permute-start.10 = (bf16[2,256,512]{2,1,0:T(8,128)(2,1)}, bf16[2,256,512]{2,1,0:T(8,128)(2,1)S(1)}, u32[]{:S(2)}, u32[]{:S(2)}) collective-permute-start(bf16[2,256,512]{2,1,0:T(8,128)(2,1)} %pad_maximum_fusion.7), channel_id=1, source_target_pairs={{0,1},{1,2},{2,3},{3,0},{4,5},{5,6},{6,7},{7,4},{8,9},{9,10},{10,1... | collective-permute-start | bytes 1572872 | tf_op jit(solution)/shard_map/ppermute | solution.py:35
  69.6 53.9 %collective-permute-start.3 = (bf16[2,256,1024]{2,1,0:T(8,128)(2,1)}, bf16[2,256,1024]{2,1,0:T(8,128)(2,1)S(1)}, u32[]{:S(2)}, u32[]{:S(2)}) collective-permute-start(bf16[2,256,1024]{2,1,0:T(8,128)(2,1)} %get-tuple-element.38), channel_id=1, source_target_pairs={{0,1},{1,2},{2,3},{3,0},{4,5},{5,6},{6,7},{7,4},{8,9},{9,10},{10,1... | collective-permute-start | bytes 3145736 | tf_op jit(solution)/shard_map/ppermute | solution.py:35
  70.0 26.7 %collective-permute-start.20 = (bf16[2,256,512]{2,1,0:T(8,128)(2,1)S(1)}, bf16[2,256,512]{2,1,0:T(8,128)(2,1)S(1)}, u32[]{:S(2)}, u32[]{:S(2)}) collective-permute-start(bf16[2,256,512]{2,1,0:T(8,128)(2,1)S(1)} %get-tuple-element.29), channel_id=1, source_target_pairs={{0,32},{8,40},{16,48},{24,56},{32,64},{40,72},{48,80},{56,88},{64,... | collective-permute-start | bytes 1572872 | tf_op jit(solution)/shard_map/ppermute | solution.py:43
  89.8 19.4 %collective-permute-start.22 = (bf16[2,256,512]{2,1,0:T(8,128)(2,1)}, bf16[2,256,512]{2,1,0:T(8,128)(2,1)}, u32[]{:S(2)}, u32[]{:S(2)}) collective-permute-start(bf16[2,256,512]{2,1,0:T(8,128)(2,1)} %get-tuple-element.30), channel_id=1, source_target_pairs={{0,64},{8,72},{16,80},{24,88},{32,96},{40,104},{48,112},{56,120},{... | collective-permute-start | bytes 1572872 | tf_op jit(solution)/shard_map/ppermute | solution.py:43
  93.6 21.0 %collective-permute-start.21 = (bf16[2,256,512]{2,1,0:T(8,128)(2,1)}, bf16[2,256,512]{2,1,0:T(8,128)(2,1)}, u32[]{:S(2)}, u32[]{:S(2)}) collective-permute-start(bf16[2,256,512]{2,1,0:T(8,128)(2,1)} %get-tuple-element.31), channel_id=1, source_target_pairs={{0,96},{8,104},{16,112},{24,120},{32,0},{40,8},{48,16},{56,24},{64... | collective-permute-start | bytes 1572872 | tf_op jit(solution)/shard_map/ppermute | solution.py:43
  96.7 49.5 %collective-permute-start.23 = (bf16[1024,1024]{1,0:T(8,128)(2,1)}, bf16[1024,1024]{1,0:T(8,128)(2,1)}, u32[]{:S(2)}, u32[]{:S(2)}) collective-permute-start(bf16[1024,1024]{1,0:T(8,128)(2,1)} %maximum_maximum_fusion), channel_id=1, source_target_pairs={{0,8},{8,0},{16,24},{24,16},{32,40},{40,32},{48,56},{56,48},{64,72... | collective-permute-start | bytes 6291464 | tf_op jit(solution)/shard_map/ppermute | solution.py:47
  109.2 20.9 %collective-permute-start.24 = (bf16[2,256,512]{2,1,0:T(8,128)(2,1)S(1)}, bf16[2,256,512]{2,1,0:T(8,128)(2,1)S(1)}, u32[]{:S(2)}, u32[]{:S(2)}) collective-permute-start(bf16[2,256,512]{2,1,0:T(8,128)(2,1)S(1)} %get-tuple-element.34), channel_id=1, source_target_pairs={{0,32},{8,40},{16,48},{24,56},{32,64},{40,72},{48,80},{56,88},{64,... | collective-permute-start | bytes 1572872 | tf_op jit(solution)/shard_map/ppermute | solution.py:43
  114.7 14.7 %collective-permute-start.14 = (bf16[256,1024]{1,0:T(8,128)(2,1)S(1)}, bf16[256,1024]{1,0:T(8,128)(2,1)S(1)}, u32[]{:S(2)}, u32[]{:S(2)}) collective-permute-start(bf16[256,1024]{1,0:T(8,128)(2,1)S(1)} %slice.266), channel_id=1, source_target_pairs={{0,8},{8,0},{16,24},{24,16},{32,40},{40,32},{48,56},{56,48},{64,72... | collective-permute-start | bytes 1572872 | tf_op jit(solution)/shard_map/ppermute | solution.py:47
  119.9 15.9 %collective-permute-start.26 = (bf16[2,256,512]{2,1,0:T(8,128)(2,1)S(1)}, bf16[2,256,512]{2,1,0:T(8,128)(2,1)S(1)}, u32[]{:S(2)}, u32[]{:S(2)}) collective-permute-start(bf16[2,256,512]{2,1,0:T(8,128)(2,1)S(1)} %get-tuple-element.35), channel_id=1, source_target_pairs={{0,64},{8,72},{16,80},{24,88},{32,96},{40,104},{48,112},{56,120},{... | collective-permute-start | bytes 1572872 | tf_op jit(solution)/shard_map/ppermute | solution.py:43
  123.5 22.7 %collective-permute-start.25 = (bf16[2,256,512]{2,1,0:T(8,128)(2,1)S(1)}, bf16[2,256,512]{2,1,0:T(8,128)(2,1)S(1)}, u32[]{:S(2)}, u32[]{:S(2)}) collective-permute-start(bf16[2,256,512]{2,1,0:T(8,128)(2,1)S(1)} %get-tuple-element.36), channel_id=1, source_target_pairs={{0,96},{8,104},{16,112},{24,120},{32,0},{40,8},{48,16},{56,24},{64... | collective-permute-start | bytes 1572872 | tf_op jit(solution)/shard_map/ppermute | solution.py:43
  129.4 40.3 %collective-permute-start.5 = (bf16[256,1024]{1,0:T(8,128)(2,1)}, bf16[256,1024]{1,0:T(8,128)(2,1)S(1)}, u32[]{:S(2)}, u32[]{:S(2)}) collective-permute-start(bf16[256,1024]{1,0:T(8,128)(2,1)} %slice_bitcast_fusion), channel_id=1, source_target_pairs={{0,4},{1,5},{2,6},{3,7},{4,0},{5,1},{6,2},{7,3},{8,12},{9,13},{10,... | collective-permute-start | bytes 1572872 | tf_op jit(solution)/shard_map/ppermute | solution.py:39
  152.7 51.9 %collective-permute-start.27 = (bf16[1024,512]{1,0:T(8,128)(2,1)}, bf16[1024,512]{1,0:T(8,128)(2,1)}, u32[]{:S(2)}, u32[]{:S(2)}) collective-permute-start(bf16[1024,512]{1,0:T(8,128)(2,1)} %multiply_convert_fusion.1), channel_id=1, source_target_pairs={{0,16},{2,18},{4,20},{6,22},{8,24},{10,26},{12,28},{14,30},{17,1},... | collective-permute-start | bytes 3145736 | tf_op jit(solution)/shard_map/ppermute | solution.py:62
  164.6 40.1 %collective-permute-start.28 = (bf16[1024,512]{1,0:T(8,128)(2,1)}, bf16[1024,512]{1,0:T(8,128)(2,1)}, u32[]{:S(2)}, u32[]{:S(2)}) collective-permute-start(bf16[1024,512]{1,0:T(8,128)(2,1)} %multiply_convert_fusion), channel_id=1, source_target_pairs={{1,17},{3,19},{5,21},{7,23},{9,25},{11,27},{13,29},{15,31},{16,0},... | collective-permute-start | bytes 3145736 | tf_op jit(solution)/shard_map/ppermute | solution.py:62
  166.6 29.3 %collective-permute-start.15 = (bf16[192,1024]{1,0:T(8,128)(2,1)}, bf16[192,1024]{1,0:T(8,128)(2,1)}, u32[]{:S(2)}, u32[]{:S(2)}) collective-permute-start(bf16[192,1024]{1,0:T(8,128)(2,1)} %pad_maximum_fusion.11), channel_id=1, source_target_pairs={{8,0},{16,8},{24,16},{32,24},{40,32},{48,40},{56,48},{64,56},{72,6... | collective-permute-start | bytes 1179656 | tf_op jit(solution)/shard_map/ppermute | solution.py:52
  169.7 28.0 %copy-start.4 = (f32[256,1024]{1,0:T(8,128)S(1)}, f32[256,1024]{1,0:T(8,128)}, u32[]{:S(2)}) copy-start(f32[256,1024]{1,0:T(8,128)} %get-tuple-element.18.kc) | copy-start | bytes 3145732
  (36 other events, 306.7 us)

commit v2 on v1

v2 whole, which is shorter than its diff:
```python
import functools

import jax
import jax.numpy as jnp
from jax import lax
from jax.experimental import pallas as pl
from jax.experimental.pallas import tpu as pltpu
from jax.sharding import PartitionSpec as P

Z, YL, CORE, YH, X = 4, 2, 2, 2, 4
F32, BF16 = jnp.float32, jnp.bfloat16
HALO = 144
HEAD = 16
LANES = 128
VMEM_LIMIT = 16 * 1024 * 1024
VMEM_MOST = 50 * 1024 * 1024


def cost(us):
    return pl.CostEstimate(flops=int(us * 4.6e9), bytes_accessed=2**16, transcendentals=0)


def ctx_pairs(move):
    pairs = []
    for i in range(Z * YL * CORE):
        z, yl, c = move(i // 4, (i // 2) % 2, i % 2)
        pairs.append((i, (z % Z) * 4 + (yl % YL) * 2 + c % CORE))
    return pairs


def tp_pairs(move):
    pairs = []
    for j in range(YH * X):
        yh, x = move(j // 4, j % 4)
        pairs.append((j, (yh % YH) * 4 + x % X))
    return pairs


def along_x(a, d):
    return lax.ppermute(a, "tp", tp_pairs(lambda yh, x: (yh, x + d)))


def across_yh(a):
    return lax.ppermute(a, "tp", tp_pairs(lambda yh, x: (yh + 1, x)))


def along_z(a, d):
    return lax.ppermute(a, "ctx", ctx_pairs(lambda z, yl, c: (z + d, yl, c)))


def across_core(a):
    return lax.ppermute(a, "ctx", ctx_pairs(lambda z, yl, c: (z, yl, c + 1)))


def next_shard(a, d):
    n = Z * YL * CORE
    return lax.ppermute(a, "ctx", [(i, i + d) for i in range(n) if 0 <= i + d < n])


def across_yl(a):
    return lax.ppermute(a, "ctx", ctx_pairs(lambda z, yl, c: (z, yl + 1, c)))


def any_specs(n):
    return [pl.BlockSpec(memory_space=pl.ANY)] * n


def toeplitz_into(table, rows):
    for g in range(8):
        wide = jnp.broadcast_to(rows[g : g + 1, :], (LANES, 2 * LANES))
        table[g * LANES : (g + 1) * LANES, :] = pltpu.roll(
            wide, 0, 1, stride=1, stride_axis=0
        ).astype(BF16)


def pick_groups(res, rows):
    lane_group = (lax.broadcasted_iota(jnp.int32, (rows, res.shape[1]), 1) % LANES) // 16
    out = res[:rows]
    for g in range(1, 8):
        out = jnp.where(lane_group == g, res[g * rows : (g + 1) * rows], out)
    return out


def forward_kernel(
    q, k, v, halo, sf, taps, gain, *refs
):
    qc_o, ca_o, kc_o, vc_o, qg_o, qgt_o, qs, ks, vs, table = refs[-10:]
    n = q.shape[0]
    qs[:HEAD] = halo[:HEAD].astype(F32)
    qs[HEAD:] = q[...].astype(F32)
    ks[:HALO] = halo[HEAD : HEAD + HALO].astype(F32)
    ks[HALO:] = k[...].astype(F32)
    vs[:HALO] = halo[HEAD + HALO :].astype(F32)
    vs[HALO:] = v[...].astype(F32)
    toeplitz_into(table, taps[...])

    def short(scr, member, first, rows):
        acc = sf[member, 0:1, :] * scr[pl.ds(first, rows), :]
        for s in range(1, 7):
            acc = acc + sf[member, s : s + 1, :] * scr[pl.ds(first - s, rows), :]
        return acc

    qc = short(qs, 0, HEAD, n)
    kc = short(ks, 1, HALO - LANES, n + LANES)
    vc = short(vs, 2, HALO - LANES, n + LANES)
    kv = (kc * vc).astype(BF16)
    window = jnp.concatenate([kv[: 2 * LANES], kv[LANES:]], axis=1)
    res = pick_groups(jnp.dot(table[...], window, preferred_element_type=F32), LANES)
    carried = jnp.concatenate([res[:, :LANES], res[:, LANES:]], axis=0)
    carried = carried + gain[...] * kv[LANES:].astype(F32)
    qc_o[...] = qc
    ca_o[...] = carried
    kc_o[...] = kc[LANES:]
    vc_o[...] = vc[LANES:]
    gated = qc * carried
    qg_o[...] = gated.astype(BF16)
    qgt_o[...] = gated.T.astype(BF16)


def forward(q, k, v, halo, sf, taps, gain, after):
    n, ch = q.shape
    col = lambda rows: pl.BlockSpec((rows, LANES), lambda i: (0, i))
    return pl.pallas_call(
        forward_kernel,
        grid=(ch // LANES,),
        in_specs=[
            col(n), col(n), col(n), col(HEAD + 2 * HALO),
            pl.BlockSpec((3, 7, LANES), lambda i: (0, 0, i)),
            pl.BlockSpec((8, 2 * LANES), lambda i: (i, 0)),
            col(1),
        ]
        + [pl.BlockSpec(memory_space=pl.ANY)] * len(after),
        out_specs=[col(n)] * 5 + [pl.BlockSpec((LANES, n), lambda i: (i, 0))],
        out_shape=[jax.ShapeDtypeStruct((n, ch), F32)] * 4
        + [jax.ShapeDtypeStruct((n, ch), BF16), jax.ShapeDtypeStruct((ch, n), BF16)],
        scratch_shapes=[
            pltpu.VMEM((HEAD + n, LANES), F32),
            pltpu.VMEM((HALO + n, LANES), F32),
            pltpu.VMEM((HALO + n, LANES), F32),
            pltpu.VMEM((8 * LANES, 2 * LANES), BF16),
        ],
        compiler_params=pltpu.CompilerParams(vmem_limit_bytes=VMEM_LIMIT),
        cost_estimate=cost(8),
        name="forward",
    )(q, k, v, halo, sf, taps, gain, *after)


def backward_kernel(gc, gq, vc, kc, rim, sf, taps, gain, *refs):
    dq_o, dk_o, dv_o, gs, qs, ks, vs, table = refs[-8:]
    n = gc.shape[0]
    gs[:n] = gc[...]
    gs[n : n + HALO] = rim[:HALO]
    gs[n + HALO :] = jnp.zeros((gs.shape[0] - n - HALO, LANES), BF16)
    toeplitz_into(table, taps[...])
    window = jnp.concatenate([gs[: 2 * LANES], gs[LANES : 3 * LANES]], axis=1)
    res = pick_groups(jnp.dot(table[...], window, preferred_element_type=F32), LANES)
    small = jnp.concatenate([table[g * LANES : g * LANES + HEAD] for g in range(8)], axis=0)
    tail = pick_groups(jnp.dot(small, gs[2 * LANES :], preferred_element_type=F32), HEAD)
    gp = jnp.concatenate([res[:, :LANES], res[:, LANES:]], axis=0) + gain[...] * gs[:n].astype(F32)
    gp_tail = tail + gain[...] * gs[n : n + HEAD].astype(F32)
    qs[:n] = gq[...]
    qs[n:] = rim[HALO + 0 * HEAD : HALO + 1 * HEAD].astype(F32)
    ks[:n] = gp * vc[...]
    ks[n:] = gp_tail * rim[HALO + 1 * HEAD : HALO + 2 * HEAD].astype(F32)
    vs[:n] = gp * kc[...]
    vs[n:] = gp_tail * rim[HALO + 2 * HEAD : HALO + 3 * HEAD].astype(F32)

    def short(scr, member):
        acc = sf[member, 0:1, :] * scr[pl.ds(0, n), :]
        for s in range(1, 7):
            acc = acc + sf[member, s : s + 1, :] * scr[pl.ds(s, n), :]
        return acc.astype(BF16)

    dq_o[...] = short(qs, 0)
    dk_o[...] = short(ks, 1)
    dv_o[...] = short(vs, 2)


def backward(gc, gq, vc, kc, rim, sf, taps, gain, after):
    n, ch = gc.shape
    col = lambda rows: pl.BlockSpec((rows, LANES), lambda i: (0, i))
    return pl.pallas_call(
        backward_kernel,
        grid=(ch // LANES,),
        in_specs=[
            col(n), col(n), col(n), col(n), col(HALO + 3 * HEAD),
            pl.BlockSpec((3, 7, LANES), lambda i: (0, 0, i)),
            pl.BlockSpec((8, 2 * LANES), lambda i: (i, 0)),
            col(1),
        ]
        + any_specs(len(after)),
        out_specs=[col(n)] * 3,
        out_shape=[jax.ShapeDtypeStruct((n, ch), BF16)] * 3,
        scratch_shapes=[
            pltpu.VMEM((4 * LANES, LANES), BF16),
            pltpu.VMEM((n + HEAD, LANES), F32),
            pltpu.VMEM((n + HEAD, LANES), F32),
            pltpu.VMEM((n + HEAD, LANES), F32),
            pltpu.VMEM((8 * LANES, 2 * LANES), BF16),
        ],
        compiler_params=pltpu.CompilerParams(vmem_limit_bytes=VMEM_LIMIT),
        cost_estimate=cost(8),
        name="backward",
    )(gc, gq, vc, kc, rim, sf, taps, gain, *after)


def grad_kernel(n_blocks, last, cols, *refs):
    blocks, w = refs[:n_blocks], refs[n_blocks]
    acc = refs[-1]
    i = pl.program_id(0)
    for k in range(n_blocks):

        @pl.when(i == k)
        def _():
            part = lax.dot_general(
                blocks[k][...], w[...], (((1,), (1,)), ((), ())), preferred_element_type=F32
            )
            if k == 0 and last:
                acc[...] = part + refs[n_blocks + 1][...]
            elif k == 0:
                acc[...] = part
            else:
                acc[...] += part

    if not last:

        @pl.when(i == n_blocks - 1)
        def _():
            refs[-2][...] = acc[...]

        return

    query_conv, carried, value_conv, key_conv = refs[n_blocks + 2 : n_blocks + 6]
    gc_o, gq_o, rim_o = refs[-4:-1]

    @pl.when(i == n_blocks - 1)
    def _():
        grad_carried = (acc[...] * query_conv[...]).astype(BF16)
        gc_o[...] = grad_carried
        gq = acc[...] * carried[...]
        gq_o[...] = gq
        rim_o[:HALO] = grad_carried[:HALO]
        for k, rows in enumerate((gq, value_conv, key_conv)):
            rim_o[HALO + k * HEAD : HALO + (k + 1) * HEAD] = rows[:HEAD].astype(BF16)


def grad_product(cols, blocks, w, rest=(), after=(), us=6.4):
    n = len(blocks)
    rows, width = blocks[0].shape
    ch = w.shape[0]
    whole = lambda r: pl.BlockSpec((r, ch), lambda i, s: (0, 0))
    if rest:
        outs = [
            jax.ShapeDtypeStruct((rows, ch), BF16),
            jax.ShapeDtypeStruct((rows, ch), F32),
            jax.ShapeDtypeStruct((HALO + 3 * HEAD, ch), BF16),
        ]
        rest_specs = [whole(rows)] * 3 + [whole(HEAD)] * 2
    else:
        outs, rest_specs = [jax.ShapeDtypeStruct((rows, ch), F32)], []
    return pl.pallas_call(
        functools.partial(grad_kernel, n, bool(rest)),
        grid_spec=pltpu.PrefetchScalarGridSpec(
            num_scalar_prefetch=1,
            grid=(n,),
            in_specs=[whole(rows)] * n
            + [pl.BlockSpec((ch, width), lambda i, s: (0, s[i]))]
            + rest_specs
            + any_specs(len(after)),
            out_specs=[whole(o.shape[0]) for o in outs],
            scratch_shapes=[pltpu.VMEM((rows, ch), F32)],
        ),
        out_shape=outs,
        compiler_params=pltpu.CompilerParams(vmem_limit_bytes=VMEM_MOST),
        cost_estimate=cost(us),
        name="grad_product",
    )(cols, *blocks, w, *rest, *after)


def project_kernel(n, cols, qg, w, *refs):
    i = pl.program_id(0)
    part = jnp.dot(qg[...], w[...], preferred_element_type=F32)
    for k in range(n):

        @pl.when(i == k)
        def _():
            refs[k - n][...] = part.astype(refs[k - n].dtype)


def project(cols, qg, w, kinds, after=(), us=3.2):
    n = len(kinds)
    rows, ch = qg.shape
    whole = pl.BlockSpec((rows, ch), lambda i, s: (0, 0))
    return pl.pallas_call(
        functools.partial(project_kernel, n),
        grid_spec=pltpu.PrefetchScalarGridSpec(
            num_scalar_prefetch=1,
            grid=(n,),
            in_specs=[whole, pl.BlockSpec((ch, ch), lambda i, s: (0, s[i]))] + any_specs(len(after)),
            out_specs=[whole] * n,
        ),
        out_shape=[jax.ShapeDtypeStruct((rows, ch), kind) for kind in kinds],
        compiler_params=pltpu.CompilerParams(vmem_limit_bytes=VMEM_MOST),
        cost_estimate=cost(us),
        name="project",
    )(cols, qg, w, *after)


def select_kernel(first, width, places, *refs):
    blocks, outs, sems = refs[:8], refs[-5:-1], refs[-1]
    core = places[8]
    for o in range(4):
        for t in range(2):
            for u in range(2):
                start = pl.multiple_of((core if u == 0 else 1 - core) * 512 + first, LANES)
                place = outs[o].at[:, pl.ds((2 * t + u) * width, width)]
                for k in range(8):

                    @pl.when(places[2 * o + t] == k)
                    def _():
                        pltpu.make_async_copy(
                            blocks[k].at[:, pl.ds(start, width)], place, sems.at[4 * o + 2 * t + u]
                        ).start()

    for o in range(4):
        for q in range(4):
            place = outs[o].at[:, pl.ds(q * width, width)]
            pltpu.make_async_copy(blocks[0].at[:, pl.ds(0, width)], place, sems.at[4 * o + q]).wait()


def select(places, blocks, first, width, after=(), us=2.5):
    rows = blocks[0].shape[0]
    return pl.pallas_call(
        functools.partial(select_kernel, first, width),
        in_specs=[pl.BlockSpec(memory_space=pltpu.SMEM)] + any_specs(8 + len(after)),
        out_specs=[pl.BlockSpec(memory_space=pltpu.VMEM)] * 4,
        out_shape=[jax.ShapeDtypeStruct((rows, 4 * width), BF16)] * 4,
        scratch_shapes=[pltpu.SemaphoreType.DMA((16,))],
        compiler_params=pltpu.CompilerParams(vmem_limit_bytes=VMEM_LIMIT),
        cost_estimate=cost(us),
        name="select",
    )(places, *blocks, *after)


def weight_kernel(scale, q0, q1, q2, q3, g0, g1, g2, g3, *refs):
    keep, give = refs[-2:]
    width = g0.shape[1] // 4
    total = jnp.dot(q0[...], g0[...], preferred_element_type=F32)
    total = total + jnp.dot(q1[...], g1[...], preferred_element_type=F32)
    total = total + jnp.dot(q2[...], g2[...], preferred_element_type=F32)
    total = total + jnp.dot(q3[...], g3[...], preferred_element_type=F32)
    total = (total * scale).astype(BF16)
    for t in range(2):
        keep[t] = total[:, 2 * t * width : (2 * t + 1) * width]
        give[t] = total[:, (2 * t + 1) * width : (2 * t + 2) * width]


def weight_sum(left, got, scale, after=()):
    ch, n = left[0].shape
    width = got[0].shape[1] // 4
    tile = 256
    rows = pl.BlockSpec((tile, n), lambda i: (i, 0))
    right = pl.BlockSpec((n, 4 * width), lambda i: (0, 0))
    return pl.pallas_call(
        functools.partial(weight_kernel, scale),
        grid=(ch // tile,),
        in_specs=[rows] * 4 + [right] * 4 + any_specs(len(after)),
        out_specs=[pl.BlockSpec((2, tile, width), lambda i: (0, i, 0))] * 2,
        out_shape=[jax.ShapeDtypeStruct((2, ch, width), BF16)] * 2,
        compiler_params=pltpu.CompilerParams(vmem_limit_bytes=VMEM_LIMIT),
        cost_estimate=cost(0.2),
        name="weight_sum",
    )(*left, *got, *after)


def halo_kernel(q, k, v, out, sems):
    n = q.shape[0]
    copies = [
        pltpu.make_async_copy(q.at[n - HEAD :], out.at[:HEAD], sems.at[0]),
        pltpu.make_async_copy(k.at[n - HALO :], out.at[HEAD : HEAD + HALO], sems.at[1]),
        pltpu.make_async_copy(v.at[n - HALO :], out.at[HEAD + HALO :], sems.at[2]),
    ]
    for copy in copies:
        copy.start()
    for copy in copies:
        copy.wait()


def last_rows(q, k, v):
    return pl.pallas_call(
        halo_kernel,
        in_specs=[pl.BlockSpec(memory_space=pltpu.HBM)] * 3,
        out_specs=pl.BlockSpec(memory_space=pltpu.VMEM),
        out_shape=jax.ShapeDtypeStruct((HEAD + 2 * HALO, q.shape[1]), BF16),
        scratch_shapes=[pltpu.SemaphoreType.DMA((3,))],
        compiler_params=pltpu.CompilerParams(vmem_limit_bytes=VMEM_LIMIT),
        cost_estimate=cost(1),
        name="last_rows",
    )(q, k, v)


def wave_kernel(right, left, got, *refs):
    refs[-2][...] = right[...]
    refs[-1][...] = (left[...] + got[...].astype(F32)).astype(BF16)


def wave(right, left, got, after):
    rows, ch = right.shape
    spec = pl.BlockSpec((rows // 2, ch), lambda i: (i, 0))
    return pl.pallas_call(
        wave_kernel,
        grid=(2,),
        in_specs=[spec] * 3 + any_specs(len(after)),
        out_specs=[spec, spec],
        out_shape=[jax.ShapeDtypeStruct((rows, ch), BF16)] * 2,
        compiler_params=pltpu.CompilerParams(vmem_limit_bytes=VMEM_LIMIT),
        cost_estimate=cost(0.2),
        name="wave",
    )(right, left, got, *after)


def combine_kernel(kept, from_core, *refs):
    refs[-1][...] = (kept[0].astype(F32) + from_core[0].astype(F32)).astype(BF16)


def combine(kept, from_core, after):
    _, rows, width = kept.shape
    tile = 256
    second = pl.BlockSpec((1, tile, width), lambda i: (1, i, 0))
    return pl.pallas_call(
        combine_kernel,
        grid=(rows // tile,),
        in_specs=[second, second] + any_specs(len(after)),
        out_specs=pl.BlockSpec((tile, width), lambda i: (i, 0)),
        out_shape=jax.ShapeDtypeStruct((rows, width), BF16),
        compiler_params=pltpu.CompilerParams(vmem_limit_bytes=VMEM_LIMIT),
        cost_estimate=cost(0.2),
        name="combine",
    )(kept, from_core, *after)


def finish_kernel(kept, from_core, from_yl, *refs):
    total = kept[0].astype(F32) + from_core[0].astype(F32) + from_yl[...].astype(F32)
    refs[-1][...] = total.astype(BF16)


def finish(kept, from_core, from_yl, first, width, shape, us, before=()):
    tile = 256
    both = pl.BlockSpec((1, tile, width), lambda i: (0, i, 0))
    return pl.pallas_call(
        finish_kernel,
        grid=(shape[0] // tile,),
        in_specs=[both, both, pl.BlockSpec((tile, width), lambda i: (i, 0))] + any_specs(len(before)),
        out_specs=pl.BlockSpec((tile, width), lambda i: (i, first // width)),
        out_shape=jax.ShapeDtypeStruct(shape, BF16),
        input_output_aliases={3: 0} if before else {},
        compiler_params=pltpu.CompilerParams(vmem_limit_bytes=VMEM_LIMIT),
        cost_estimate=cost(us),
        name="finish",
    )(kept, from_core, from_yl, *before)


def on_device(query_in, key_in, value_in, short_filter, long_filter, skip_gain, out_weight, grad_output):
    n, ch = query_in.shape
    ctx, tp = lax.axis_index("ctx"), lax.axis_index("tp")
    z, yl, c = ctx // 4, (ctx // 2) % 2, ctx % 2
    yh, x = tp // 4, tp % 4
    gain = skip_gain.reshape(1, ch)
    w = out_weight

    own = grad_output
    r1, l1 = along_x(own, 1), along_x(own, -1)
    other = across_yh(own)
    halo = next_shard(last_rows(query_in, key_in, value_in), 1)
    r2, l2 = along_x(other, 1), along_x(other, -1)
    r3, l3 = along_x(r1, 1), along_x(l2, -1)

    taps = long_filter.astype(F32).T
    none = jnp.zeros((taps.shape[0], 1), F32)
    pad = jnp.zeros((taps.shape[0], taps.shape[1] - 1), F32)
    taps_fwd = jnp.concatenate([none, taps[:, ::-1], pad], axis=1)
    taps_bwd = jnp.concatenate([taps, none, pad], axis=1)
    query_conv, carried, key_conv, value_conv, gated, gated_t = forward(
        query_in, key_in, value_in, halo, short_filter, taps_fwd, gain, [other, r1, l1]
    )

    left = [gated_t, along_z(gated_t, 1), along_z(gated_t, -1), along_z(gated_t, 2)]

    def block_cols(dys, dxs):
        dy, dx = jnp.array(dys), jnp.array(dxs)
        return (((yh + dy) % YH) * X + (x + dx) % X).astype(jnp.int32)

    near_gg = grad_product(block_cols([0, 0, 1, 1], [3, 1, 3, 1]), [r1, l1, r2, l2], w)

    far_up, far_down = project(
        block_cols([1, 0], [2, 2]), gated, w, [BF16, BF16], after=near_gg
    )
    got_r, got_l = along_x(far_up, 1), along_x(far_down, -1)

    plane = (z + jnp.array([0, 1, 3, 2])) % Z
    parity = (yl + jnp.array([0, 1])) % 2
    to_x = (2 * (plane % 2))[:, None] + parity[None]
    dy, dx = (plane // 2 + yh) % 2, (to_x - x) % X
    places = jnp.array([0, 2, 6, 1, 3, 5, 7, 4])[dy[:, None] * 4 + dx].reshape(8)
    places = jnp.concatenate([places, c[None]]).astype(jnp.int32)
    blocks = [own, r1, l1, other, r2, l2, r3, l3]
    splits = [(0, 256), (256, 256)]
    first = select(places, blocks, *splits[0], after=[far_up])

    right1, left1 = project(block_cols([1, 1], [1, 3]), gated, w, [F32, BF16], after=[first[0], *left], us=6)
    right0, left0, stay0, stay1 = project(
        block_cols([0, 0, 0, 1], [1, 3, 0, 0]), gated, w, [BF16, F32, F32, F32], after=[left1, *left], us=8
    )
    grad_carried, grad_query_conv, rim = grad_product(
        block_cols([0, 0, 1, 1], [0, 2, 0, 2]), [own, r3, other, l3], w,
        (near_gg[0], query_conv, carried, value_conv, key_conv), after=[stay1, got_r, got_l], us=0.2,
    )
    rim = next_shard(rim, -1)
    second = select(places, blocks, *splits[1], after=[grad_carried], us=0.2)

    from_r1 = along_x((right1.astype(F32) + got_r.astype(F32)).astype(BF16), 1)
    from_l1 = along_x(left1, -1)
    swap = (stay1 + from_r1.astype(F32) + from_l1.astype(F32)).astype(BF16)
    swapped = across_yh(swap)

    grad_query, grad_key, grad_value = backward(
        grad_carried, grad_query_conv, value_conv, key_conv, rim,
        short_filter, taps_bwd, gain, [from_r1, from_l1],
    )

    scale = float(n * Z * YL * CORE) ** -0.5
    after, done = [second[0], from_r1, from_l1], []
    waves = []
    for (keep, up, down, across), split, us in zip((first, second), splits, (20, 1)):
        got = [keep, along_z(up, 1), along_z(down, -1), along_z(across, 2)]
        kept, given = weight_sum(left, got, scale, after)
        from_core = across_core(given)
        total = combine(kept, from_core, done)
        waves = waves or wave(right0, left0, got_l, [total])
        after = [total, grad_query]
        done = [finish(kept, from_core, across_yl(total), *split, (ch, 512), us, done)]

    from_r0, from_l0 = along_x(waves[0], 1), along_x(waves[1], -1)
    output = stay0 + from_r0.astype(F32) + from_l0.astype(F32) + swapped.astype(F32)
    output = output.astype(BF16)
    return output, grad_query, grad_key, grad_value, done[0]


def solution(mesh):
    return jax.shard_map(
        on_device,
        mesh=mesh,
        in_specs=(
            P("ctx", "tp"),
            P("ctx", "tp"),
            P("ctx", "tp"),
            P(None, None, "tp"),
            P(None, "tp"),
            P("tp"),
            P("tp", None),
            P("ctx", "tp"),
        ),
        out_specs=(P("ctx", "tp"), P("ctx", "tp"), P("ctx", "tp"), P("ctx", "tp"), P("tp", "ctx")),
        check_vma=False,
    )
```

time: 209 us -> 159 us (0.76)
  the two profiles are of different devices: /device:TPU:27 before, /device:TPU:0 now
where the time goes in v2:
time: 159 us; the launch traced here: 156 us
  Pallas kernels  61.3 us (39%)
  starting transfers between devices  45.6 us (29%)
  waiting for transfers between devices  27.7 us (17%)
  local copies, waits for them, and re-layouts  15.5 us (10%)
  other arithmetic  4.33 us (3%)
    ppermute x9, starting transfers between devices, along_z(): return lax.ppermute(a, 'ctx', ctx_pairs(lambda z, yl, c: (z + d, yl, c)))  18.1 us
    ppermute x12, starting transfers between devices, along_x(): return lax.ppermute(a, 'tp', tp_pairs(lambda yh, x: (yh, x + d)))  17.1 us
    pallas_call x3, Pallas kernels, project(): pl.pallas_call(functools.partial(project_kernel, n), grid_spec=pltpu.Pref...  16.5 us
    pallas_call x2, Pallas kernels, grad_product(): pl.pallas_call(functools.partial(grad_kernel, n, bool(rest)), grid_spec=p...  14.7 us
    unnamed x72, local copies, waits for them, and re-layouts  14.6 us
    ppermute x2, waiting for transfers between devices, across_yl(): return lax.ppermute(a, 'ctx', ctx_pairs(lambda z, yl, c: (z, yl + 1, c)))  11.1 us
    ppermute x9, waiting for transfers between devices, along_z(): return lax.ppermute(a, 'ctx', ctx_pairs(lambda z, yl, c: (z + d, yl, c)))  8.33 us
    pallas_call x2, Pallas kernels, weight_sum(): pl.pallas_call(functools.partial(weight_kernel, scale), grid=(ch // tile,...  7.24 us
  transfers between devices with their start and end apart: 29, of which 6 were waited for; matrix products, arithmetic and copies ran while one was open for 3% of the time, Pallas kernels for 36%

profile of v2, /device:TPU:0, one launch (start us, length us, event | category | flops | bytes accessed | tf_op | source)
XLA Modules:
  0.0 155.7 jit_solution(2745405579500498040)
XLA Ops:
  0.7 2.9 %collective-permute-start.3 = (bf16[256,1024]{1,0:T(8,128)(2,1)}, bf16[256,1024]{1,0:T(8,128)(2,1)S(1)}, u32[]{:S(2)}, u32[]{:S(2)}) collective-permute-start(bf16[256,1024]{1,0:T(8,128)(2,1)} %refs_0_.5), channel_id=1, source_target_pairs={{0,3},{1,0},{2,1},{3,2},{4,7},{5,4},{6,5},{7,6},{8,11},{9,8},{10,9... | collective-permute-start | bytes 1572872 | tf_op jit(solution)/shard_map/ppermute | solution.py:40
  3.6 3.2 %collective-permute-start.1 = (bf16[256,1024]{1,0:T(8,128)(2,1)}, bf16[256,1024]{1,0:T(8,128)(2,1)S(1)}, u32[]{:S(2)}, u32[]{:S(2)}) collective-permute-start(bf16[256,1024]{1,0:T(8,128)(2,1)} %refs_0_.5), channel_id=1, source_target_pairs={{0,4},{1,5},{2,6},{3,7},{4,0},{5,1},{6,2},{7,3},{8,12},{9,13},{10,... | collective-permute-start | bytes 1572872 | tf_op jit(solution)/shard_map/ppermute | solution.py:44
  13.8 6.4 %collective-permute-done.1.refs_0_.refs_3_.refs_2_ = bf16[256,1024]{1,0:T(8,128)(2,1)S(1)} collective-permute-done((bf16[256,1024]{1,0:T(8,128)(2,1)}, bf16[256,1024]{1,0:T(8,128)(2,1)S(1)}, u32[]{:S(2)}, u32[]{:S(2)}) %collective-permute-start.1) | collective-permute-done | bytes 524320 | tf_op jit(solution)/shard_map/ppermute | solution.py:44
  20.2 3.2 %collective-permute-start.5 = (bf16[256,1024]{1,0:T(8,128)(2,1)S(1)}, bf16[256,1024]{1,0:T(8,128)(2,1)S(1)}, u32[]{:S(2)}, u32[]{:S(2)}) collective-permute-start(bf16[256,1024]{1,0:T(8,128)(2,1)S(1)} %collective-permute-done.1.refs_0_.refs_3_.refs_2_), channel_id=1, source_target_pairs={{0,3},{1,0},{2,1},{3,2},{4,7},{5,4},{6,5},{7,6},{8,11},{9,8},{10,9... | collective-permute-start | bytes 1572872 | tf_op jit(solution)/shard_map/ppermute | solution.py:40
  26.6 6.6 %forward.1 = (f32[256,1024]{1,0:T(8,128)S(1)}, f32[256,1024]{1,0:T(8,128)S(1)}, f32[256,1024]{1,0:T(8,128)S(1)}, f32[256,1024]{1,0:T(8,128)S(1)}, bf16[256,1024]...) custom-call(bf16[256,1024]{1,0:T(8,128)(2,1)S(1)} %copy-done.14, bf16[256,1024]{1,0:T(8,128)(2,1)S(1)} %copy-done.16, ...), custom_call_target="tpu_custom_call" | custom-call | flops 36800000000 | bytes 65536 | tf_op jit(solution)/shard_map/forward/pallas_call | solution.py:123
  37.2 5.7 %collective-permute-start.10 = (bf16[1024,256]{1,0:T(8,128)(2,1)S(1)}, bf16[1024,256]{1,0:T(8,128)(2,1)S(1)}, u32[]{:S(2)}, u32[]{:S(2)}) collective-permute-start(bf16[1024,256]{1,0:T(8,128)(2,1)S(1)} %get-tuple-element.42.refs_1_.q0), channel_id=1, source_target_pairs={{0,64},{8,72},{16,80},{24,88},{32,96},{40,104},{48,112},{56,120},{... | collective-permute-start | bytes 1572872 | tf_op jit(solution)/shard_map/ppermute | solution.py:48
  44.9 3.0 %collective-permute-start.7 = (bf16[256,1024]{1,0:T(8,128)(2,1)S(1)}, bf16[256,1024]{1,0:T(8,128)(2,1)S(1)}, u32[]{:S(2)}, u32[]{:S(2)}) collective-permute-start(bf16[256,1024]{1,0:T(8,128)(2,1)S(1)} %collective-permute-done.5.refs_3_.refs_5_), channel_id=1, source_target_pairs={{0,3},{1,0},{2,1},{3,2},{4,7},{5,4},{6,5},{7,6},{8,11},{9,8},{10,9... | collective-permute-start | bytes 1572872 | tf_op jit(solution)/shard_map/ppermute | solution.py:40
  47.9 6.2 %grad_product.2.refs_0_.refs_5_ = f32[256,1024]{1,0:T(8,128)S(1)} custom-call(s32[4]{0:T(128)S(1)} %fusion.3.cols, bf16[256,1024]{1,0:T(8,128)(2,1)S(1)} %collective-permute-done.2.refs_1_.refs_0_, bf16[256,1024]{1,0:T(8,128)(2,1)S(1)} %collective-permute-done.3.refs_2_.refs_1_, bf16[256,1024]{1,0:T(8,128)(2,1)S(1)} %collective-permute-done.4.refs_2_.refs_4_, ...), custom_call_target="tpu_custom_call" | custom-call | flops 29440000000 | bytes 65536 | tf_op jit(solution)/shard_map/grad_product/pallas_call | solution.py:261
  54.1 3.7 %project.3 = (bf16[256,1024]{1,0:T(8,128)(2,1)S(1)}, bf16[256,1024]{1,0:T(8,128)(2,1)S(1)}) custom-call(s32[2]{0:T(128)S(1)} %fusion.13.cols, bf16[256,1024]{1,0:T(8,128)(2,1)S(1)} %get-tuple-element.39.qg, bf16[1024,8192]{1,0:T(8,128)(2,1)} %refs_4_.3, f32[256,1024]{1,0:T(8,128)S(1)} %grad_product.2.refs_0_.refs_5_), custom_call_target="tpu_custom_call" | custom-call | flops 14720000000 | bytes 65536 | tf_op jit(solution)/shard_map/project/pallas_call | solution.py:294
  59.9 3.0 %select.66 = (bf16[256,1024]{1,0:T(8,128)(2,1)S(1)}, bf16[256,1024]{1,0:T(8,128)(2,1)}, bf16[256,1024]{1,0:T(8,128)(2,1)}, bf16[256,1024]{1,0:T(8,128)(2,1)S(1)}) custom-call(s32[9]{0:T(128)S(1)} %pad_add_fusion.places, bf16[256,1024]{1,0:T(8,128)(2,1)S(1)} %copy-done, bf16[256,1024]{1,0:T(8,128)(2,1)S(1)} %collective-permute-done.2.refs_1_.refs_0_, ...), custom_call_target="tpu_custom_call" | custom-call | flops 11500000256 | bytes 65536 | tf_op jit(solution)/shard_map/select/pallas_call | solution.py:333
  63.0 1.6 %collective-permute-start.12 = (bf16[256,1024]{1,0:T(8,128)(2,1)}, bf16[256,1024]{1,0:T(8,128)(2,1)S(1)}, u32[]{:S(2)}, u32[]{:S(2)}) collective-permute-start(bf16[256,1024]{1,0:T(8,128)(2,1)} %get-tuple-element.48), channel_id=1, source_target_pairs={{0,32},{8,40},{16,48},{24,56},{32,64},{40,72},{48,80},{56,88},{64,... | collective-permute-start | bytes 1572872 | tf_op jit(solution)/shard_map/ppermute | solution.py:48
  64.5 2.0 %collective-permute-done.9.refs_3_.q2 = bf16[1024,256]{1,0:T(8,128)(2,1)S(1)} collective-permute-done((bf16[1024,256]{1,0:T(8,128)(2,1)S(1)}, bf16[1024,256]{1,0:T(8,128)(2,1)S(1)}, u32[]{:S(2)}, u32[]{:S(2)}) %collective-permute-start.9) | collective-permute-done | bytes 524320 | tf_op jit(solution)/shard_map/ppermute | solution.py:48
  66.5 2.6 %collective-permute-start.13 = (bf16[256,1024]{1,0:T(8,128)(2,1)}, bf16[256,1024]{1,0:T(8,128)(2,1)}, u32[]{:S(2)}, u32[]{:S(2)}) collective-permute-start(bf16[256,1024]{1,0:T(8,128)(2,1)} %get-tuple-element.49), channel_id=1, source_target_pairs={{0,96},{8,104},{16,112},{24,120},{32,0},{40,8},{48,16},{56,24},{64... | collective-permute-start | bytes 1572872 | tf_op jit(solution)/shard_map/ppermute | solution.py:48
  69.2 4.8 %project.4 = (f32[256,1024]{1,0:T(8,128)}, bf16[256,1024]{1,0:T(8,128)(2,1)}) custom-call(s32[2]{0:T(128)S(1)} %fusion.9.cols, bf16[256,1024]{1,0:T(8,128)(2,1)S(1)} %get-tuple-element.39.qg, bf16[1024,8192]{1,0:T(8,128)(2,1)} %refs_4_.3, bf16[256,1024]{1,0:T(8,128)(2,1)S(1)} %get-tuple-element.41.refs_0_.g0, ...), custom_call_target="tpu_custom_call" | custom-call | flops 27599998976 | bytes 65536 | tf_op jit(solution)/shard_map/project/pallas_call | solution.py:294
  74.0 1.4 add_convert_fusion.2
  75.9 2.8 %collective-permute-start.17 = (bf16[256,1024]{1,0:T(8,128)(2,1)}, bf16[256,1024]{1,0:T(8,128)(2,1)S(1)}, u32[]{:S(2)}, u32[]{:S(2)}) collective-permute-start(bf16[256,1024]{1,0:T(8,128)(2,1)} %get-tuple-element.43.refs_0_), channel_id=1, source_target_pairs={{0,3},{1,0},{2,1},{3,2},{4,7},{5,4},{6,5},{7,6},{8,11},{9,8},{10,9... | collective-permute-start | bytes 1572872 | tf_op jit(solution)/shard_map/ppermute | solution.py:40
  78.7 8.0 %project.5 = (bf16[256,1024]{1,0:T(8,128)(2,1)S(1)}, f32[256,1024]{1,0:T(8,128)}, f32[256,1024]{1,0:T(8,128)}, f32[256,1024]{1,0:T(8,128)}) custom-call(s32[4]{0:T(128)S(1)} %fusion.2.cols, bf16[256,1024]{1,0:T(8,128)(2,1)S(1)} %get-tuple-element.39.qg, bf16[1024,8192]{1,0:T(8,128)(2,1)} %refs_4_.3, bf16[256,1024]{1,0:T(8,128)(2,1)} %get-tuple-element.43.refs_0_, ...), custom_call_target="tpu_custom_call" | custom-call | flops 36800000000 | bytes 65536 | tf_op jit(solution)/shard_map/project/pallas_call | solution.py:294
  87.4 8.5 %grad_product.3 = (bf16[256,1024]{1,0:T(8,128)(2,1)S(1)}, f32[256,1024]{1,0:T(8,128)}, bf16[192,1024]{1,0:T(8,128)(2,1)S(1)}) custom-call(s32[4]{0:T(128)S(1)} %get-tuple-element.73.cols, bf16[256,1024]{1,0:T(8,128)(2,1)S(1)} %copy-done, bf16[256,1024]{1,0:T(8,128)(2,1)S(1)} %collective-permute-done.6.refs_6_.refs_1_, ...), custom_call_target="tpu_custom_call" | custom-call | flops 920000000 | bytes 65536 | tf_op jit(solution)/shard_map/grad_product/pallas_call | solution.py:261
  96.0 2.0 %select.67 = (bf16[256,1024]{1,0:T(8,128)(2,1)S(1)}, bf16[256,1024]{1,0:T(8,128)(2,1)S(1)}, bf16[256,1024]{1,0:T(8,128)(2,1)S(1)}, bf16[256,1024]{1,0:T(8,128)(2,1)S(1)}) custom-call(s32[9]{0:T(128)S(1)} %pad_add_fusion.places, bf16[256,1024]{1,0:T(8,128)(2,1)S(1)} %copy-done, bf16[256,1024]{1,0:T(8,128)(2,1)S(1)} %collective-permute-done.2.refs_1_.refs_0_, ...), custom_call_target="tpu_custom_call" | custom-call | flops 920000000 | bytes 65536 | tf_op jit(solution)/shard_map/select/pallas_call | solution.py:333
  98.1 4.2 %weight_sum.2 = (bf16[2,1024,256]{2,1,0:T(8,128)(2,1)S(1)}, bf16[2,1024,256]{2,1,0:T(8,128)(2,1)S(1)}) custom-call(bf16[1024,256]{1,0:T(8,128)(2,1)S(1)} %get-tuple-element.42.refs_1_.q0, bf16[1024,256]{1,0:T(8,128)(2,1)S(1)} %collective-permute-done.8.refs_2_.q1, bf16[1024,256]{1,0:T(8,128)(2,1)S(1)} %collective-permute-done.9.refs_3_.q2, ...), custom_call_target="tpu_custom_call" | custom-call | flops 920000000 | bytes 65536 | tf_op jit(solution)/shard_map/weight_sum/pallas_call | solution.py:364
  103.7 2.9 %collective-permute-start.23 = (bf16[256,1024]{1,0:T(8,128)(2,1)S(1)}, bf16[256,1024]{1,0:T(8,128)(2,1)S(1)}, u32[]{:S(2)}, u32[]{:S(2)}) collective-permute-start(bf16[256,1024]{1,0:T(8,128)(2,1)S(1)} %get-tuple-element.68), channel_id=1, source_target_pairs={{0,32},{8,40},{16,48},{24,56},{32,64},{40,72},{48,80},{56,88},{64,... | collective-permute-start | bytes 1572872 | tf_op jit(solution)/shard_map/ppermute | solution.py:48
  107.3 2.7 %collective-permute-start.25 = (bf16[256,1024]{1,0:T(8,128)(2,1)S(1)}, bf16[256,1024]{1,0:T(8,128)(2,1)S(1)}, u32[]{:S(2)}, u32[]{:S(2)}) collective-permute-start(bf16[256,1024]{1,0:T(8,128)(2,1)S(1)} %get-tuple-element.70), channel_id=1, source_target_pairs={{0,64},{8,72},{16,80},{24,88},{32,96},{40,104},{48,112},{56,120},{... | collective-permute-start | bytes 1572872 | tf_op jit(solution)/shard_map/ppermute | solution.py:48
  110.0 1.5 add_convert_fusion.1
  112.3 1.8 %collective-permute-start.27 = (bf16[1024,256]{1,0:T(8,128)(2,1)S(1)}, bf16[1024,256]{1,0:T(8,128)(2,1)S(1)}, u32[]{:S(2)}, u32[]{:S(2)}) collective-permute-start(bf16[1024,256]{1,0:T(8,128)(2,1)S(1)} %combine.2.refs_0_), channel_id=1, source_target_pairs={{0,16},{8,24},{16,0},{24,8},{32,48},{40,56},{48,32},{56,40},{64,80... | collective-permute-start | bytes 1572872 | tf_op jit(solution)/shard_map/ppermute | solution.py:61
  115.4 6.7 %backward.1 = (bf16[256,1024]{1,0:T(8,128)(2,1)}, bf16[256,1024]{1,0:T(8,128)(2,1)}, bf16[256,1024]{1,0:T(8,128)(2,1)}) custom-call(bf16[256,1024]{1,0:T(8,128)(2,1)S(1)} %get-tuple-element.56.refs_8_.gc, f32[256,1024]{1,0:T(8,128)S(1)} %copy-done.12, f32[256,1024]{1,0:T(8,128)S(1)} %copy-done.4, f32[256,1024]{1,0:T(8,128)S(1)} %copy-done.2, ...), custom_call_target="tpu_custom_call" | custom-call | flops 36800000000 | bytes 65536 | tf_op jit(solution)/shard_map/backward/pallas_call | solution.py:182
  122.4 3.2 %collective-permute-start.20 = (bf16[256,1024]{1,0:T(8,128)(2,1)S(1)}, bf16[256,1024]{1,0:T(8,128)(2,1)S(1)}, u32[]{:S(2)}, u32[]{:S(2)}) collective-permute-start(bf16[256,1024]{1,0:T(8,128)(2,1)S(1)} %get-tuple-element.62), channel_id=1, source_target_pairs={{0,3},{1,0},{2,1},{3,2},{4,7},{5,4},{6,5},{7,6},{8,11},{9,8},{10,9... | collective-permute-start | bytes 1572872 | tf_op jit(solution)/shard_map/ppermute | solution.py:40
  125.7 6.3 %collective-permute-done.25.g3 = bf16[256,1024]{1,0:T(8,128)(2,1)S(1)} collective-permute-done((bf16[256,1024]{1,0:T(8,128)(2,1)S(1)}, bf16[256,1024]{1,0:T(8,128)(2,1)S(1)}, u32[]{:S(2)}, u32[]{:S(2)}) %collective-permute-start.25) | collective-permute-done | bytes 524320 | tf_op jit(solution)/shard_map/ppermute | solution.py:48
  133.0 3.0 %weight_sum.3 = (bf16[2,1024,256]{2,1,0:T(8,128)(2,1)S(1)}, bf16[2,1024,256]{2,1,0:T(8,128)(2,1)S(1)}) custom-call(bf16[1024,256]{1,0:T(8,128)(2,1)S(1)} %get-tuple-element.42.refs_1_.q0, bf16[1024,256]{1,0:T(8,128)(2,1)S(1)} %collective-permute-done.8.refs_2_.q1, bf16[1024,256]{1,0:T(8,128)(2,1)S(1)} %collective-permute-done.9.refs_3_.q2, ...), custom_call_target="tpu_custom_call" | custom-call | flops 920000000 | bytes 65536 | tf_op jit(solution)/shard_map/weight_sum/pallas_call | solution.py:364
  136.1 1.5 finish.2.refs_0_
  140.2 1.9 %collective-permute-start.28 = (bf16[1024,256]{1,0:T(8,128)(2,1)S(1)}, bf16[1024,256]{1,0:T(8,128)(2,1)S(1)}, u32[]{:S(2)}, u32[]{:S(2)}) collective-permute-start(bf16[1024,256]{1,0:T(8,128)(2,1)S(1)} %combine.3), channel_id=1, source_target_pairs={{0,16},{8,24},{16,0},{24,8},{32,48},{40,56},{48,32},{56,40},{64,80... | collective-permute-start | bytes 1572872 | tf_op jit(solution)/shard_map/ppermute | solution.py:61
  143.2 11.1 %collective-permute-done.28.from_yl = bf16[1024,256]{1,0:T(8,128)(2,1)S(1)} collective-permute-done((bf16[1024,256]{1,0:T(8,128)(2,1)S(1)}, bf16[1024,256]{1,0:T(8,128)(2,1)S(1)}, u32[]{:S(2)}, u32[]{:S(2)}) %collective-permute-start.28) | collective-permute-done | bytes 524320 | tf_op jit(solution)/shard_map/ppermute | solution.py:61
  154.3 1.5 finish.3
  (137 shorter events, 28.7 us)
Async XLA Ops:
  0.7 22.7 %collective-permute-start.3 = (bf16[256,1024]{1,0:T(8,128)(2,1)}, bf16[256,1024]{1,0:T(8,128)(2,1)S(1)}, u32[]{:S(2)}, u32[]{:S(2)}) collective-permute-start(bf16[256,1024]{1,0:T(8,128)(2,1)} %refs_0_.5), channel_id=1, source_target_pairs={{0,3},{1,0},{2,1},{3,2},{4,7},{5,4},{6,5},{7,6},{8,11},{9,8},{10,9... | collective-permute-start | bytes 1572872 | tf_op jit(solution)/shard_map/ppermute | solution.py:40
  3.6 19.8 %collective-permute-start.2 = (bf16[256,1024]{1,0:T(8,128)(2,1)}, bf16[256,1024]{1,0:T(8,128)(2,1)S(1)}, u32[]{:S(2)}, u32[]{:S(2)}) collective-permute-start(bf16[256,1024]{1,0:T(8,128)(2,1)} %refs_0_.5), channel_id=1, source_target_pairs={{0,1},{1,2},{2,3},{3,0},{4,5},{5,6},{6,7},{7,4},{8,9},{9,10},{10,1... | collective-permute-start | bytes 1572872 | tf_op jit(solution)/shard_map/ppermute | solution.py:40
  3.6 16.6 %collective-permute-start.1 = (bf16[256,1024]{1,0:T(8,128)(2,1)}, bf16[256,1024]{1,0:T(8,128)(2,1)S(1)}, u32[]{:S(2)}, u32[]{:S(2)}) collective-permute-start(bf16[256,1024]{1,0:T(8,128)(2,1)} %refs_0_.5), channel_id=1, source_target_pairs={{0,4},{1,5},{2,6},{3,7},{4,0},{5,1},{6,2},{7,3},{8,12},{9,13},{10,... | collective-permute-start | bytes 1572872 | tf_op jit(solution)/shard_map/ppermute | solution.py:44
  11.0 12.5 %collective-permute-start = (bf16[304,1024]{1,0:T(8,128)(2,1)}, bf16[304,1024]{1,0:T(8,128)(2,1)S(1)}, u32[]{:S(2)}, u32[]{:S(2)}) collective-permute-start(bf16[304,1024]{1,0:T(8,128)(2,1)} %last_rows.1), channel_id=1, source_target_pairs={{0,8},{8,16},{16,24},{24,32},{32,40},{40,48},{48,56},{56,64},{64,7... | collective-permute-start | bytes 1867784 | tf_op jit(solution)/shard_map/ppermute | solution.py:57
  20.2 23.4 %collective-permute-start.5 = (bf16[256,1024]{1,0:T(8,128)(2,1)S(1)}, bf16[256,1024]{1,0:T(8,128)(2,1)S(1)}, u32[]{:S(2)}, u32[]{:S(2)}) collective-permute-start(bf16[256,1024]{1,0:T(8,128)(2,1)S(1)} %collective-permute-done.1.refs_0_.refs_3_.refs_2_), channel_id=1, source_target_pairs={{0,3},{1,0},{2,1},{3,2},{4,7},{5,4},{6,5},{7,6},{8,11},{9,8},{10,9... | collective-permute-start | bytes 1572872 | tf_op jit(solution)/shard_map/ppermute | solution.py:40
  23.5 21.5 %collective-permute-start.4 = (bf16[256,1024]{1,0:T(8,128)(2,1)S(1)}, bf16[256,1024]{1,0:T(8,128)(2,1)S(1)}, u32[]{:S(2)}, u32[]{:S(2)}) collective-permute-start(bf16[256,1024]{1,0:T(8,128)(2,1)S(1)} %collective-permute-done.1.refs_0_.refs_3_.refs_2_), channel_id=1, source_target_pairs={{0,1},{1,2},{2,3},{3,0},{4,5},{5,6},{6,7},{7,4},{8,9},{9,10},{10,1... | collective-permute-start | bytes 1572872 | tf_op jit(solution)/shard_map/ppermute | solution.py:40
  23.5 34.4 %collective-permute-start.6 = (bf16[256,1024]{1,0:T(8,128)(2,1)S(1)}, bf16[256,1024]{1,0:T(8,128)(2,1)S(1)}, u32[]{:S(2)}, u32[]{:S(2)}) collective-permute-start(bf16[256,1024]{1,0:T(8,128)(2,1)S(1)} %collective-permute-done.2.refs_1_.refs_0_), channel_id=1, source_target_pairs={{0,1},{1,2},{2,3},{3,0},{4,5},{5,6},{6,7},{7,4},{8,9},{9,10},{10,1... | collective-permute-start | bytes 1572872 | tf_op jit(solution)/shard_map/ppermute | solution.py:40
  37.2 25.7 %collective-permute-start.10 = (bf16[1024,256]{1,0:T(8,128)(2,1)S(1)}, bf16[1024,256]{1,0:T(8,128)(2,1)S(1)}, u32[]{:S(2)}, u32[]{:S(2)}) collective-permute-start(bf16[1024,256]{1,0:T(8,128)(2,1)S(1)} %get-tuple-element.42.refs_1_.q0), channel_id=1, source_target_pairs={{0,64},{8,72},{16,80},{24,88},{32,96},{40,104},{48,112},{56,120},{... | collective-permute-start | bytes 1572872 | tf_op jit(solution)/shard_map/ppermute | solution.py:48
  42.9 23.6 %collective-permute-start.9 = (bf16[1024,256]{1,0:T(8,128)(2,1)S(1)}, bf16[1024,256]{1,0:T(8,128)(2,1)S(1)}, u32[]{:S(2)}, u32[]{:S(2)}) collective-permute-start(bf16[1024,256]{1,0:T(8,128)(2,1)S(1)} %get-tuple-element.42.refs_1_.q0), channel_id=1, source_target_pairs={{0,96},{8,104},{16,112},{24,120},{32,0},{40,8},{48,16},{56,24},{64... | collective-permute-start | bytes 1572872 | tf_op jit(solution)/shard_map/ppermute | solution.py:48
  43.6 25.5 %collective-permute-start.8 = (bf16[1024,256]{1,0:T(8,128)(2,1)S(1)}, bf16[1024,256]{1,0:T(8,128)(2,1)S(1)}, u32[]{:S(2)}, u32[]{:S(2)}) collective-permute-start(bf16[1024,256]{1,0:T(8,128)(2,1)S(1)} %get-tuple-element.42.refs_1_.q0), channel_id=1, source_target_pairs={{0,32},{8,40},{16,48},{24,56},{32,64},{40,72},{48,80},{56,88},{64,... | collective-permute-start | bytes 1572872 | tf_op jit(solution)/shard_map/ppermute | solution.py:48
  44.9 14.2 %collective-permute-start.7 = (bf16[256,1024]{1,0:T(8,128)(2,1)S(1)}, bf16[256,1024]{1,0:T(8,128)(2,1)S(1)}, u32[]{:S(2)}, u32[]{:S(2)}) collective-permute-start(bf16[256,1024]{1,0:T(8,128)(2,1)S(1)} %collective-permute-done.5.refs_3_.refs_5_), channel_id=1, source_target_pairs={{0,3},{1,0},{2,1},{3,2},{4,7},{5,4},{6,5},{7,6},{8,11},{9,8},{10,9... | collective-permute-start | bytes 1572872 | tf_op jit(solution)/shard_map/ppermute | solution.py:40
  57.8 18.1 %collective-permute-start.11 = (bf16[256,1024]{1,0:T(8,128)(2,1)S(1)}, bf16[256,1024]{1,0:T(8,128)(2,1)S(1)}, u32[]{:S(2)}, u32[]{:S(2)}) collective-permute-start(bf16[256,1024]{1,0:T(8,128)(2,1)S(1)} %get-tuple-element.47), channel_id=1, source_target_pairs={{0,3},{1,0},{2,1},{3,2},{4,7},{5,4},{6,5},{7,6},{8,11},{9,8},{10,9... | collective-permute-start | bytes 1572872 | tf_op jit(solution)/shard_map/ppermute | solution.py:40
  59.1 14.9 %collective-permute-start.15 = (bf16[256,1024]{1,0:T(8,128)(2,1)S(1)}, bf16[256,1024]{1,0:T(8,128)(2,1)S(1)}, u32[]{:S(2)}, u32[]{:S(2)}) collective-permute-start(bf16[256,1024]{1,0:T(8,128)(2,1)S(1)} %get-tuple-element.40.refs_8_), channel_id=1, source_target_pairs={{0,1},{1,2},{2,3},{3,0},{4,5},{5,6},{6,7},{7,4},{8,9},{9,10},{10,1... | collective-permute-start | bytes 1572872 | tf_op jit(solution)/shard_map/ppermute | solution.py:40
  63.0 35.1 %collective-permute-start.12 = (bf16[256,1024]{1,0:T(8,128)(2,1)}, bf16[256,1024]{1,0:T(8,128)(2,1)S(1)}, u32[]{:S(2)}, u32[]{:S(2)}) collective-permute-start(bf16[256,1024]{1,0:T(8,128)(2,1)} %get-tuple-element.48), channel_id=1, source_target_pairs={{0,32},{8,40},{16,48},{24,56},{32,64},{40,72},{48,80},{56,88},{64,... | collective-permute-start | bytes 1572872 | tf_op jit(solution)/shard_map/ppermute | solution.py:48
  66.5 31.5 %collective-permute-start.13 = (bf16[256,1024]{1,0:T(8,128)(2,1)}, bf16[256,1024]{1,0:T(8,128)(2,1)}, u32[]{:S(2)}, u32[]{:S(2)}) collective-permute-start(bf16[256,1024]{1,0:T(8,128)(2,1)} %get-tuple-element.49), channel_id=1, source_target_pairs={{0,96},{8,104},{16,112},{24,120},{32,0},{40,8},{48,16},{56,24},{64... | collective-permute-start | bytes 1572872 | tf_op jit(solution)/shard_map/ppermute | solution.py:48
  69.2 28.9 %collective-permute-start.14 = (bf16[256,1024]{1,0:T(8,128)(2,1)S(1)}, bf16[256,1024]{1,0:T(8,128)(2,1)}, u32[]{:S(2)}, u32[]{:S(2)}) collective-permute-start(bf16[256,1024]{1,0:T(8,128)(2,1)S(1)} %get-tuple-element.50), channel_id=1, source_target_pairs={{0,64},{8,72},{16,80},{24,88},{32,96},{40,104},{48,112},{56,120},{... | collective-permute-start | bytes 1572872 | tf_op jit(solution)/shard_map/ppermute | solution.py:48
  75.4 22.7 %collective-permute-start.16 = (bf16[256,1024]{1,0:T(8,128)(2,1)S(1)}, bf16[256,1024]{1,0:T(8,128)(2,1)S(1)}, u32[]{:S(2)}, u32[]{:S(2)}) collective-permute-start(bf16[256,1024]{1,0:T(8,128)(2,1)S(1)} %add_convert_fusion.2), channel_id=1, source_target_pairs={{0,1},{1,2},{2,3},{3,0},{4,5},{5,6},{6,7},{7,4},{8,9},{9,10},{10,1... | collective-permute-start | bytes 1572872 | tf_op jit(solution)/shard_map/ppermute | solution.py:40
  75.9 22.2 %collective-permute-start.17 = (bf16[256,1024]{1,0:T(8,128)(2,1)}, bf16[256,1024]{1,0:T(8,128)(2,1)S(1)}, u32[]{:S(2)}, u32[]{:S(2)}) collective-permute-start(bf16[256,1024]{1,0:T(8,128)(2,1)} %get-tuple-element.43.refs_0_), channel_id=1, source_target_pairs={{0,3},{1,0},{2,1},{3,2},{4,7},{5,4},{6,5},{7,6},{8,11},{9,8},{10,9... | collective-permute-start | bytes 1572872 | tf_op jit(solution)/shard_map/ppermute | solution.py:40
  87.4 26.7 %copy-start.2 = (f32[256,1024]{1,0:T(8,128)S(1)}, f32[256,1024]{1,0:T(8,128)}, u32[]{:S(2)}) copy-start(f32[256,1024]{1,0:T(8,128)} %copy-done.1) | copy-start | bytes 3145732
  87.4 26.7 %copy-start.4 = (f32[256,1024]{1,0:T(8,128)S(1)}, f32[256,1024]{1,0:T(8,128)}, u32[]{:S(2)}) copy-start(f32[256,1024]{1,0:T(8,128)} %copy-done.3) | copy-start | bytes 3145732
  87.4 26.7 %copy-start.20 = (f32[3,7,1024]{2,1,0:T(8,128)S(1)}, f32[3,7,1024]{2,1,0:T(8,128)}, u32[]{:S(2)}) copy-start(f32[3,7,1024]{2,1,0:T(8,128)} %sf.3) | copy-start | bytes 258052
  102.3 9.1 %collective-permute-start.18 = (bf16[2,1024,256]{2,1,0:T(8,128)(2,1)S(1)}, bf16[2,1024,256]{2,1,0:T(8,128)(2,1)S(1)}, u32[]{:S(2)}, u32[]{:S(2)}) collective-permute-start(bf16[2,1024,256]{2,1,0:T(8,128)(2,1)S(1)} %get-tuple-element.60), channel_id=1, source_target_pairs={{0,8},{8,0},{16,24},{24,16},{32,40},{40,32},{48,56},{56,48},{64,72... | collective-permute-start | bytes 3145736 | tf_op jit(solution)/shard_map/ppermute | solution.py:52
  102.4 9.9 %collective-permute-start.22 = (bf16[192,1024]{1,0:T(8,128)(2,1)S(1)}, bf16[192,1024]{1,0:T(8,128)(2,1)S(1)}, u32[]{:S(2)}, u32[]{:S(2)}) collective-permute-start(bf16[192,1024]{1,0:T(8,128)(2,1)S(1)} %get-tuple-element.64), channel_id=1, source_target_pairs={{8,0},{16,8},{24,16},{32,24},{40,32},{48,40},{56,48},{64,56},{72,6... | collective-permute-start | bytes 1179656 | tf_op jit(solution)/shard_map/ppermute | solution.py:57
  103.7 18.6 %collective-permute-start.23 = (bf16[256,1024]{1,0:T(8,128)(2,1)S(1)}, bf16[256,1024]{1,0:T(8,128)(2,1)S(1)}, u32[]{:S(2)}, u32[]{:S(2)}) collective-permute-start(bf16[256,1024]{1,0:T(8,128)(2,1)S(1)} %get-tuple-element.68), channel_id=1, source_target_pairs={{0,32},{8,40},{16,48},{24,56},{32,64},{40,72},{48,80},{56,88},{64,... | collective-permute-start | bytes 1572872 | tf_op jit(solution)/shard_map/ppermute | solution.py:48
  106.6 15.9 %collective-permute-start.24 = (bf16[256,1024]{1,0:T(8,128)(2,1)S(1)}, bf16[256,1024]{1,0:T(8,128)(2,1)S(1)}, u32[]{:S(2)}, u32[]{:S(2)}) collective-permute-start(bf16[256,1024]{1,0:T(8,128)(2,1)S(1)} %get-tuple-element.69), channel_id=1, source_target_pairs={{0,96},{8,104},{16,112},{24,120},{32,0},{40,8},{48,16},{56,24},{64... | collective-permute-start | bytes 1572872 | tf_op jit(solution)/shard_map/ppermute | solution.py:48
  107.3 24.7 %collective-permute-start.25 = (bf16[256,1024]{1,0:T(8,128)(2,1)S(1)}, bf16[256,1024]{1,0:T(8,128)(2,1)S(1)}, u32[]{:S(2)}, u32[]{:S(2)}) collective-permute-start(bf16[256,1024]{1,0:T(8,128)(2,1)S(1)} %get-tuple-element.70), channel_id=1, source_target_pairs={{0,64},{8,72},{16,80},{24,88},{32,96},{40,104},{48,112},{56,120},{... | collective-permute-start | bytes 1572872 | tf_op jit(solution)/shard_map/ppermute | solution.py:48
  111.4 30.6 %collective-permute-start.21 = (bf16[256,1024]{1,0:T(8,128)(2,1)S(1)}, bf16[256,1024]{1,0:T(8,128)(2,1)S(1)}, u32[]{:S(2)}, u32[]{:S(2)}) collective-permute-start(bf16[256,1024]{1,0:T(8,128)(2,1)S(1)} %add_convert_fusion.1), channel_id=1, source_target_pairs={{0,4},{1,5},{2,6},{3,7},{4,0},{5,1},{6,2},{7,3},{8,12},{9,13},{10,... | collective-permute-start | bytes 1572872 | tf_op jit(solution)/shard_map/ppermute | solution.py:44
  112.3 23.8 %collective-permute-start.27 = (bf16[1024,256]{1,0:T(8,128)(2,1)S(1)}, bf16[1024,256]{1,0:T(8,128)(2,1)S(1)}, u32[]{:S(2)}, u32[]{:S(2)}) collective-permute-start(bf16[1024,256]{1,0:T(8,128)(2,1)S(1)} %combine.2.refs_0_), channel_id=1, source_target_pairs={{0,16},{8,24},{16,0},{24,8},{32,48},{40,56},{48,32},{56,40},{64,80... | collective-permute-start | bytes 1572872 | tf_op jit(solution)/shard_map/ppermute | solution.py:61
  122.3 19.7 %collective-permute-start.19 = (bf16[256,1024]{1,0:T(8,128)(2,1)S(1)}, bf16[256,1024]{1,0:T(8,128)(2,1)S(1)}, u32[]{:S(2)}, u32[]{:S(2)}) collective-permute-start(bf16[256,1024]{1,0:T(8,128)(2,1)S(1)} %get-tuple-element.61), channel_id=1, source_target_pairs={{0,1},{1,2},{2,3},{3,0},{4,5},{5,6},{6,7},{7,4},{8,9},{9,10},{10,1... | collective-permute-start | bytes 1572872 | tf_op jit(solution)/shard_map/ppermute | solution.py:40
  122.4 19.6 %collective-permute-start.20 = (bf16[256,1024]{1,0:T(8,128)(2,1)S(1)}, bf16[256,1024]{1,0:T(8,128)(2,1)S(1)}, u32[]{:S(2)}, u32[]{:S(2)}) collective-permute-start(bf16[256,1024]{1,0:T(8,128)(2,1)S(1)} %get-tuple-element.62), channel_id=1, source_target_pairs={{0,3},{1,0},{2,1},{3,2},{4,7},{5,4},{6,5},{7,6},{8,11},{9,8},{10,9... | collective-permute-start | bytes 1572872 | tf_op jit(solution)/shard_map/ppermute | solution.py:40
  136.0 2.7 %collective-permute-start.26 = (bf16[2,1024,256]{2,1,0:T(8,128)(2,1)S(1)}, bf16[2,1024,256]{2,1,0:T(8,128)(2,1)S(1)}, u32[]{:S(2)}, u32[]{:S(2)}) collective-permute-start(bf16[2,1024,256]{2,1,0:T(8,128)(2,1)S(1)} %get-tuple-element.72), channel_id=1, source_target_pairs={{0,8},{8,0},{16,24},{24,16},{32,40},{40,32},{48,56},{56,48},{64,72... | collective-permute-start | bytes 3145736 | tf_op jit(solution)/shard_map/ppermute | solution.py:52
  140.2 14.1 %collective-permute-start.28 = (bf16[1024,256]{1,0:T(8,128)(2,1)S(1)}, bf16[1024,256]{1,0:T(8,128)(2,1)S(1)}, u32[]{:S(2)}, u32[]{:S(2)}) collective-permute-start(bf16[1024,256]{1,0:T(8,128)(2,1)S(1)} %combine.3), channel_id=1, source_target_pairs={{0,16},{8,24},{16,0},{24,8},{32,48},{40,56},{48,32},{56,40},{64,80... | collective-permute-start | bytes 1572872 | tf_op jit(solution)/shard_map/ppermute | solution.py:61
  (33 other events, 197.6 us)

commit v3 on v2

--- a/solution.py
+++ b/solution.py
@@ -13,6 +13,7 @@
 HEAD = 16
 LANES = 128
 VMEM_LIMIT = 16 * 1024 * 1024
+VMEM_ALL = 60 * 1024 * 1024
 VMEM_MOST = 50 * 1024 * 1024
 
 
@@ -88,10 +89,10 @@
     n = q.shape[0]
     qs[:HEAD] = halo[:HEAD].astype(F32)
     qs[HEAD:] = q[...].astype(F32)
-    ks[:HALO] = halo[HEAD : HEAD + HALO].astype(F32)
-    ks[HALO:] = k[...].astype(F32)
-    vs[:HALO] = halo[HEAD + HALO :].astype(F32)
-    vs[HALO:] = v[...].astype(F32)
+    ks[:HEAD] = halo[HEAD : 2 * HEAD].astype(F32)
+    ks[HEAD:] = k[...].astype(F32)
+    vs[:HEAD] = halo[2 * HEAD : 3 * HEAD].astype(F32)
+    vs[HEAD:] = v[...].astype(F32)
     toeplitz_into(table, taps[...])
 
     def short(scr, member, first, rows):
@@ -101,17 +102,17 @@
         return acc
 
     qc = short(qs, 0, HEAD, n)
-    kc = short(ks, 1, HALO - LANES, n + LANES)
-    vc = short(vs, 2, HALO - LANES, n + LANES)
-    kv = (kc * vc).astype(BF16)
+    kc = short(ks, 1, HEAD, n)
+    vc = short(vs, 2, HEAD, n)
+    kv = jnp.concatenate([halo[3 * HEAD :], (kc * vc).astype(BF16)], axis=0)
     window = jnp.concatenate([kv[: 2 * LANES], kv[LANES:]], axis=1)
     res = pick_groups(jnp.dot(table[...], window, preferred_element_type=F32), LANES)
     carried = jnp.concatenate([res[:, :LANES], res[:, LANES:]], axis=0)
     carried = carried + gain[...] * kv[LANES:].astype(F32)
     qc_o[...] = qc
     ca_o[...] = carried
-    kc_o[...] = kc[LANES:]
-    vc_o[...] = vc[LANES:]
+    kc_o[...] = kc
+    vc_o[...] = vc
     gated = qc * carried
     qg_o[...] = gated.astype(BF16)
     qgt_o[...] = gated.T.astype(BF16)
@@ -124,7 +125,7 @@
         forward_kernel,
         grid=(ch // LANES,),
         in_specs=[
-            col(n), col(n), col(n), col(HEAD + 2 * HALO),
+            col(n), col(n), col(n), col(3 * HEAD + LANES),
             pl.BlockSpec((3, 7, LANES), lambda i: (0, 0, i)),
             pl.BlockSpec((8, 2 * LANES), lambda i: (i, 0)),
             col(1),
@@ -135,11 +136,11 @@
         + [jax.ShapeDtypeStruct((n, ch), BF16), jax.ShapeDtypeStruct((ch, n), BF16)],
         scratch_shapes=[
             pltpu.VMEM((HEAD + n, LANES), F32),
-            pltpu.VMEM((HALO + n, LANES), F32),
-            pltpu.VMEM((HALO + n, LANES), F32),
+            pltpu.VMEM((HEAD + n, LANES), F32),
+            pltpu.VMEM((HEAD + n, LANES), F32),
             pltpu.VMEM((8 * LANES, 2 * LANES), BF16),
         ],
-        compiler_params=pltpu.CompilerParams(vmem_limit_bytes=VMEM_LIMIT),
+        compiler_params=pltpu.CompilerParams(vmem_limit_bytes=VMEM_ALL),
         cost_estimate=cost(8),
         name="forward",
     )(q, k, v, halo, sf, taps, gain, *after)
@@ -373,30 +374,40 @@
     )(*left, *got, *after)
 
 
-def halo_kernel(q, k, v, out, sems):
-    n = q.shape[0]
-    copies = [
-        pltpu.make_async_copy(q.at[n - HEAD :], out.at[:HEAD], sems.at[0]),
-        pltpu.make_async_copy(k.at[n - HALO :], out.at[HEAD : HEAD + HALO], sems.at[1]),
-        pltpu.make_async_copy(v.at[n - HALO :], out.at[HEAD + HALO :], sems.at[2]),
-    ]
-    for copy in copies:
-        copy.start()
-    for copy in copies:
-        copy.wait()
-
-
-def last_rows(q, k, v):
-    return pl.pallas_call(
-        halo_kernel,
-        in_specs=[pl.BlockSpec(memory_space=pltpu.HBM)] * 3,
-        out_specs=pl.BlockSpec(memory_space=pltpu.VMEM),
-        out_shape=jax.ShapeDtypeStruct((HEAD + 2 * HALO, q.shape[1]), BF16),
-        scratch_shapes=[pltpu.SemaphoreType.DMA((3,))],
-        compiler_params=pltpu.CompilerParams(vmem_limit_bytes=VMEM_LIMIT),
+def last_rows_kernel(q, k_before, k, v_before, v, sf, out, ks, vs):
+    for scratch, before, tail in ((ks, k_before, k), (vs, v_before, v)):
+        scratch[:HEAD] = before[...].astype(F32)
+        scratch[HEAD:] = tail[...].astype(F32)
+    rows = k.shape[0]
+    kc = sf[1, 0:1, :] * ks[HEAD:]
+    vc = sf[2, 0:1, :] * vs[HEAD:]
+    for s in range(1, 7):
+        kc = kc + sf[1, s : s + 1, :] * ks[pl.ds(HEAD - s, rows), :]
+        vc = vc + sf[2, s : s + 1, :] * vs[pl.ds(HEAD - s, rows), :]
+    out[:HEAD] = q[...]
+    out[HEAD : 2 * HEAD] = k[rows - HEAD :]
+    out[2 * HEAD : 3 * HEAD] = v[rows - HEAD :]
+    out[3 * HEAD :] = (kc * vc).astype(BF16)
+
+
+def last_rows(q, k, v, sf):
+    n, ch = q.shape
+    width = 512
+    part = lambda rows, i: pl.BlockSpec((rows, width), lambda j: (i, j))
+    tail = part(LANES, n // LANES - 1)
+    before = part(HEAD, (n - LANES) // HEAD - 1)
+    return pl.pallas_call(
+        last_rows_kernel,
+        grid=(ch // width,),
+        in_specs=[part(HEAD, n // HEAD - 1), before, tail, before, tail]
+        + [pl.BlockSpec((3, 7, width), lambda j: (0, 0, j))],
+        out_specs=part(3 * HEAD + LANES, 0),
+        out_shape=jax.ShapeDtypeStruct((3 * HEAD + LANES, ch), BF16),
+        scratch_shapes=[pltpu.VMEM((HEAD + LANES, width), F32)] * 2,
+        compiler_params=pltpu.CompilerParams(vmem_limit_bytes=VMEM_ALL),
         cost_estimate=cost(1),
         name="last_rows",
-    )(q, k, v)
+    )(q, k, k, v, v, sf)
 
 
 def wave_kernel(right, left, got, *refs):
@@ -414,7 +425,7 @@
         out_specs=[spec, spec],
         out_shape=[jax.ShapeDtypeStruct((rows, ch), BF16)] * 2,
         compiler_params=pltpu.CompilerParams(vmem_limit_bytes=VMEM_LIMIT),
-        cost_estimate=cost(0.2),
+        cost_estimate=cost(8),
         name="wave",
     )(right, left, got, *after)
 
@@ -423,7 +434,7 @@
     refs[-1][...] = (kept[0].astype(F32) + from_core[0].astype(F32)).astype(BF16)
 
 
-def combine(kept, from_core, after):
+def combine(kept, from_core, after, us):
     _, rows, width = kept.shape
     tile = 256
     second = pl.BlockSpec((1, tile, width), lambda i: (1, i, 0))
@@ -434,26 +445,34 @@
         out_specs=pl.BlockSpec((tile, width), lambda i: (i, 0)),
         out_shape=jax.ShapeDtypeStruct((rows, width), BF16),
         compiler_params=pltpu.CompilerParams(vmem_limit_bytes=VMEM_LIMIT),
-        cost_estimate=cost(0.2),
+        cost_estimate=cost(us),
         name="combine",
     )(kept, from_core, *after)
 
 
 def finish_kernel(kept, from_core, from_yl, *refs):
+    before, out = refs[:-1], refs[-1]
+    width = from_yl.shape[1]
     total = kept[0].astype(F32) + from_core[0].astype(F32) + from_yl[...].astype(F32)
-    refs[-1][...] = total.astype(BF16)
-
-
-def finish(kept, from_core, from_yl, first, width, shape, us, before=()):
+    if before:
+        out[:, :-width] = before[0][...]
+        out[:, -width:] = total.astype(BF16)
+    else:
+        out[...] = total.astype(BF16)
+
+
+def finish(kept, from_core, from_yl, us, before=()):
     tile = 256
+    rows, width = from_yl.shape
     both = pl.BlockSpec((1, tile, width), lambda i: (0, i, 0))
+    plain = lambda a: pl.BlockSpec((tile, a.shape[1]), lambda i: (i, 0))
+    total = width + sum(a.shape[1] for a in before)
     return pl.pallas_call(
         finish_kernel,
-        grid=(shape[0] // tile,),
-        in_specs=[both, both, pl.BlockSpec((tile, width), lambda i: (i, 0))] + any_specs(len(before)),
-        out_specs=pl.BlockSpec((tile, width), lambda i: (i, first // width)),
-        out_shape=jax.ShapeDtypeStruct(shape, BF16),
-        input_output_aliases={3: 0} if before else {},
+        grid=(rows // tile,),
+        in_specs=[both, both, plain(from_yl)] + [plain(a) for a in before],
+        out_specs=pl.BlockSpec((tile, total), lambda i: (i, 0)),
+        out_shape=jax.ShapeDtypeStruct((rows, total), BF16),
         compiler_params=pltpu.CompilerParams(vmem_limit_bytes=VMEM_LIMIT),
         cost_estimate=cost(us),
         name="finish",
@@ -471,10 +490,7 @@
     own = grad_output
     r1, l1 = along_x(own, 1), along_x(own, -1)
     other = across_yh(own)
-    halo = next_shard(last_rows(query_in, key_in, value_in), 1)
-    r2, l2 = along_x(other, 1), along_x(other, -1)
-    r3, l3 = along_x(r1, 1), along_x(l2, -1)
-
+    halo = next_shard(last_rows(query_in, key_in, value_in, short_filter), 1)
     taps = long_filter.astype(F32).T
     none = jnp.zeros((taps.shape[0], 1), F32)
     pad = jnp.zeros((taps.shape[0], taps.shape[1] - 1), F32)
@@ -484,6 +500,10 @@
         query_in, key_in, value_in, halo, short_filter, taps_fwd, gain, [other, r1, l1]
     )
 
+    r2, l2 = along_x(other, 1), along_x(other, -1)
+    after_r2, _ = lax.optimization_barrier((r1, r2))
+    r3, l3 = along_x(after_r2, 1), along_x(l2, -1)
+
     left = [gated_t, along_z(gated_t, 1), along_z(gated_t, -1), along_z(gated_t, 2)]
 
     def block_cols(dys, dxs):
@@ -504,46 +524,52 @@
     places = jnp.array([0, 2, 6, 1, 3, 5, 7, 4])[dy[:, None] * 4 + dx].reshape(8)
     places = jnp.concatenate([places, c[None]]).astype(jnp.int32)
     blocks = [own, r1, l1, other, r2, l2, r3, l3]
-    splits = [(0, 256), (256, 256)]
+    splits = [(0, 384), (384, 128)]
     first = select(places, blocks, *splits[0], after=[far_up])
 
     right1, left1 = project(block_cols([1, 1], [1, 3]), gated, w, [F32, BF16], after=[first[0], *left], us=6)
     right0, left0, stay0, stay1 = project(
-        block_cols([0, 0, 0, 1], [1, 3, 0, 0]), gated, w, [BF16, F32, F32, F32], after=[left1, *left], us=8
+        block_cols([0, 0, 0, 1], [1, 3, 0, 0]), gated, w, [BF16, F32, F32, F32], after=[left1, got_r, got_l, *left], us=8
     )
+    second = select(places, blocks, *splits[1], after=[stay1], us=0.2)
     grad_carried, grad_query_conv, rim = grad_product(
         block_cols([0, 0, 1, 1], [0, 2, 0, 2]), [own, r3, other, l3], w,
-        (near_gg[0], query_conv, carried, value_conv, key_conv), after=[stay1, got_r, got_l], us=0.2,
+        (near_gg[0], query_conv, carried, value_conv, key_conv), after=[second[0]], us=0.2,
     )
-    rim = next_shard(rim, -1)
-    second = select(places, blocks, *splits[1], after=[grad_carried], us=0.2)
 
     from_r1 = along_x((right1.astype(F32) + got_r.astype(F32)).astype(BF16), 1)
     from_l1 = along_x(left1, -1)
     swap = (stay1 + from_r1.astype(F32) + from_l1.astype(F32)).astype(BF16)
     swapped = across_yh(swap)
 
+    scale = float(n * Z * YL * CORE) ** -0.5
+
+    *second, _ = lax.optimization_barrier((*second, swap))
+    rim, _ = lax.optimization_barrier((rim, swap))
+    rim = next_shard(rim, -1)
+
+    def over_z(keep, up, down, across):
+        return [keep, along_z(up, 1), along_z(down, -1), along_z(across, 2)]
+
+    kept_a, given_a = weight_sum(left, over_z(*first), scale, [grad_carried, swap])
+    core_a = across_core(given_a)
+    waves = wave(right0, left0, got_l, [kept_a])
+    sent_a = combine(kept_a, core_a, [waves[0]], 0.2)
     grad_query, grad_key, grad_value = backward(
         grad_carried, grad_query_conv, value_conv, key_conv, rim,
-        short_filter, taps_bwd, gain, [from_r1, from_l1],
+        short_filter, taps_bwd, gain, [swapped, sent_a],
     )
-
-    scale = float(n * Z * YL * CORE) ** -0.5
-    after, done = [second[0], from_r1, from_l1], []
-    waves = []
-    for (keep, up, down, across), split, us in zip((first, second), splits, (20, 1)):
-        got = [keep, along_z(up, 1), along_z(down, -1), along_z(across, 2)]
-        kept, given = weight_sum(left, got, scale, after)
-        from_core = across_core(given)
-        total = combine(kept, from_core, done)
-        waves = waves or wave(right0, left0, got_l, [total])
-        after = [total, grad_query]
-        done = [finish(kept, from_core, across_yl(total), *split, (ch, 512), us, done)]
-
+    kept_b, given_b = weight_sum(left, over_z(*second), scale, [grad_query])
+    done_a = finish(kept_a, core_a, across_yl(sent_a), 20)
+    core_b = across_core(given_b)
+    sent_b = combine(kept_b, core_b, [done_a], 0.2)
+    weight_grad = finish(kept_b, core_b, across_yl(sent_b), 1, [done_a])
+
+    *waves, _ = lax.optimization_barrier((*waves, grad_query))
     from_r0, from_l0 = along_x(waves[0], 1), along_x(waves[1], -1)
     output = stay0 + from_r0.astype(F32) + from_l0.astype(F32) + swapped.astype(F32)
     output = output.astype(BF16)
-    return output, grad_query, grad_key, grad_value, done[0]
+    return output, grad_query, grad_key, grad_value, weight_grad
 
 
 def solution(mesh):

time: 159 us -> 144 us (0.906); the launches traced: 156 us -> 143 us
  local copies, waits for them, and re-layouts: 15.5 us -> 7.4 us
  waiting for transfers between devices: 27.7 us -> 20.4 us
  Pallas kernels: 61.3 us -> 63.2 us
    ppermute x9, waiting for transfers between devices: 8.33 us -> 0.02 us  [along_z(): return lax.ppermute(a, 'ctx', ctx_pairs(lambda z, yl, c: (z + d, yl, c)))]
    unnamed x72 -> x80, local copies, waits for them, and re-layouts: 14.6 us -> 6.51 us
    ppermute x9, starting transfers between devices: 18.1 us -> 14.9 us  [along_z(): return lax.ppermute(a, 'ctx', ctx_pairs(lambda z, yl, c: (z + d, yl, c)))]
    ppermute x2, waiting for transfers between devices: 11.1 us -> 8.26 us  [across_yl(): return lax.ppermute(a, 'ctx', ctx_pairs(lambda z, yl, c: (z, yl + 1, c)))]
    ppermute x2, starting transfers between devices: 3.87 us -> 6.47 us  [across_yh(): return lax.ppermute(a, 'tp', tp_pairs(lambda yh, x: (yh + 1, x)))]
    ppermute x2, starting transfers between devices: 3.72 us -> 1.51 us  [across_yl(): return lax.ppermute(a, 'ctx', ctx_pairs(lambda z, yl, c: (z, yl + 1, c)))]
    ppermute x12, waiting for transfers between devices: 0.73 us -> 2.52 us  [along_x(): return lax.ppermute(a, 'tp', tp_pairs(lambda yh, x: (yh, x + d)))]
    ppermute x2, waiting for transfers between devices: 1.13 us -> 2.88 us  [across_core(): return lax.ppermute(a, 'ctx', ctx_pairs(lambda z, yl, c: (z, yl, c + 1)))]
  transfers between devices with their start and end apart: 29 -> 29, of which waited for: 6 -> 5; matrix products, arithmetic and copies ran while one was open for 3% -> 5% of each run, Pallas kernels for 36% -> 43%
where the time goes in v3:
time: 144 us; the launch traced here: 143 us
  Pallas kernels  63.2 us (44%)
  starting transfers between devices  45.1 us (31%)
  waiting for transfers between devices  20.4 us (14%)
  local copies, waits for them, and re-layouts  7.4 us (5%)
  other arithmetic  5.64 us (4%)
    ppermute x12, starting transfers between devices, along_x(): return lax.ppermute(a, 'tp', tp_pairs(lambda yh, x: (yh, x + d)))  18 us
    pallas_call x3, Pallas kernels, project(): pl.pallas_call(functools.partial(project_kernel, n), grid_spec=pltpu.Pref...  16.9 us
    ppermute x9, starting transfers between devices, along_z(): return lax.ppermute(a, 'ctx', ctx_pairs(lambda z, yl, c: (z + d, yl, c)))  14.9 us
    pallas_call x2, Pallas kernels, grad_product(): pl.pallas_call(functools.partial(grad_kernel, n, bool(rest)), grid_spec=p...  14.4 us
    ppermute x2, waiting for transfers between devices, across_yl(): return lax.ppermute(a, 'ctx', ctx_pairs(lambda z, yl, c: (z, yl + 1, c)))  8.26 us
    pallas_call x1, Pallas kernels, forward(): pl.pallas_call(forward_kernel, grid=(ch // LANES,), in_specs=[col(n), col...  7.92 us
    pallas_call x1, Pallas kernels, backward(): pl.pallas_call(backward_kernel, grid=(ch // LANES,), in_specs=[col(n), co...  6.7 us
    ppermute x2, waiting for transfers between devices, across_yh(): return lax.ppermute(a, 'tp', tp_pairs(lambda yh, x: (yh + 1, x)))  6.67 us
  transfers between devices with their start and end apart: 29, of which 5 were waited for; matrix products, arithmetic and copies ran while one was open for 5% of the time, Pallas kernels for 43%

profile of v3, /device:TPU:0, one launch (start us, length us, event | category | flops | bytes accessed | tf_op | source)
XLA Modules:
  0.0 143.0 jit_solution(7518791767315327749)
XLA Ops:
  0.7 2.9 %collective-permute-start.3 = (bf16[256,1024]{1,0:T(8,128)(2,1)}, bf16[256,1024]{1,0:T(8,128)(2,1)S(1)}, u32[]{:S(2)}, u32[]{:S(2)}) collective-permute-start(bf16[256,1024]{1,0:T(8,128)(2,1)} %refs_0_.5), channel_id=1, source_target_pairs={{0,3},{1,0},{2,1},{3,2},{4,7},{5,4},{6,5},{7,6},{8,11},{9,8},{10,9... | collective-permute-start | bytes 1572872 | tf_op jit(solution)/shard_map/ppermute | solution.py:41
  3.7 3.2 %collective-permute-start.1 = (bf16[256,1024]{1,0:T(8,128)(2,1)}, bf16[256,1024]{1,0:T(8,128)(2,1)S(1)}, u32[]{:S(2)}, u32[]{:S(2)}) collective-permute-start(bf16[256,1024]{1,0:T(8,128)(2,1)} %refs_0_.5), channel_id=1, source_target_pairs={{0,4},{1,5},{2,6},{3,7},{4,0},{5,1},{6,2},{7,3},{8,12},{9,13},{10,... | collective-permute-start | bytes 1572872 | tf_op jit(solution)/shard_map/ppermute | solution.py:45
  6.9 3.1 %last_rows.1 = bf16[176,1024]{1,0:T(8,128)(2,1)} custom-call(bf16[256,1024]{1,0:T(8,128)(2,1)} %q.3, bf16[256,1024]{1,0:T(8,128)(2,1)} %k.3, bf16[256,1024]{1,0:T(8,128)(2,1)} %k.3, bf16[256,1024]{1,0:T(8,128)(2,1)} %v.3, bf16[256,1024]{1,0:T(8,128)(2,1)} %v.3, f32[3,7,1024]{2,1,0:T(8,128)} %sf.5), custom_call_target="tpu_custom_call" | custom-call | flops 4600000000 | bytes 65536 | tf_op jit(solution)/shard_map/last_rows/pallas_call | solution.py:399
  13.6 6.7 %collective-permute-done.1.refs_0_.refs_3_.refs_2_ = bf16[256,1024]{1,0:T(8,128)(2,1)S(1)} collective-permute-done((bf16[256,1024]{1,0:T(8,128)(2,1)}, bf16[256,1024]{1,0:T(8,128)(2,1)S(1)}, u32[]{:S(2)}, u32[]{:S(2)}) %collective-permute-start.1) | collective-permute-done | bytes 524320 | tf_op jit(solution)/shard_map/ppermute | solution.py:45
  20.2 3.2 %collective-permute-start.5 = (bf16[256,1024]{1,0:T(8,128)(2,1)S(1)}, bf16[256,1024]{1,0:T(8,128)(2,1)S(1)}, u32[]{:S(2)}, u32[]{:S(2)}) collective-permute-start(bf16[256,1024]{1,0:T(8,128)(2,1)S(1)} %collective-permute-done.1.refs_0_.refs_3_.refs_2_), channel_id=1, source_target_pairs={{0,3},{1,0},{2,1},{3,2},{4,7},{5,4},{6,5},{7,6},{8,11},{9,8},{10,9... | collective-permute-start | bytes 1572872 | tf_op jit(solution)/shard_map/ppermute | solution.py:41
  24.6 7.9 %forward.1 = (f32[256,1024]{1,0:T(8,128)}, f32[256,1024]{1,0:T(8,128)}, f32[256,1024]{1,0:T(8,128)}, f32[256,1024]{1,0:T(8,128)}, bf16[256,1024]{1,0:T(8,128)(2,1)}, /*index=5*/bf16[1024,256]{1,0:T(8,128)(2,1)}) custom-call(bf16[256,1024]{1,0:T(8,128)(2,1)} %q.3, bf16[256,1024]{1,0:T(8,128)(2,1)} %k.3, bf16[256,1024]{1,0:T(8,128)(2,1)} %v.3, ...), custom_call_target="tpu_custom_call" | custom-call | flops 36800000000 | bytes 65536 | tf_op jit(solution)/shard_map/forward/pallas_call | solution.py:124
  32.5 4.0 %collective-permute-start.10 = (bf16[1024,256]{1,0:T(8,128)(2,1)}, bf16[1024,256]{1,0:T(8,128)(2,1)S(1)}, u32[]{:S(2)}, u32[]{:S(2)}) collective-permute-start(bf16[1024,256]{1,0:T(8,128)(2,1)} %get-tuple-element.51.refs_1_.refs_3_.q0), channel_id=1, source_target_pairs={{0,64},{8,72},{16,80},{24,88},{32,96},{40,104},{48,112},{56,120},{... | collective-permute-start | bytes 1572872 | tf_op jit(solution)/shard_map/ppermute | solution.py:49
  38.5 3.3 %collective-permute-start.7 = (bf16[256,1024]{1,0:T(8,128)(2,1)S(1)}, bf16[256,1024]{1,0:T(8,128)(2,1)S(1)}, u32[]{:S(2)}, u32[]{:S(2)}) collective-permute-start(bf16[256,1024]{1,0:T(8,128)(2,1)S(1)} %collective-permute-done.5.refs_3_.refs_5_), channel_id=1, source_target_pairs={{0,3},{1,0},{2,1},{3,2},{4,7},{5,4},{6,5},{7,6},{8,11},{9,8},{10,9... | collective-permute-start | bytes 1572872 | tf_op jit(solution)/shard_map/ppermute | solution.py:41
  43.9 6.2 %grad_product.2.refs_0_.refs_5_ = f32[256,1024]{1,0:T(8,128)S(1)} custom-call(s32[4]{0:T(128)S(1)} %fusion.3.cols, bf16[256,1024]{1,0:T(8,128)(2,1)S(1)} %copy-done.18, bf16[256,1024]{1,0:T(8,128)(2,1)S(1)} %copy-done.15, bf16[256,1024]{1,0:T(8,128)(2,1)S(1)} %collective-permute-done.4.refs_2_.refs_4_, ...), custom_call_target="tpu_custom_call" | custom-call | flops 29440000000 | bytes 65536 | tf_op jit(solution)/shard_map/grad_product/pallas_call | solution.py:262
  50.2 4.1 %project.3 = (bf16[256,1024]{1,0:T(8,128)(2,1)S(1)}, bf16[256,1024]{1,0:T(8,128)(2,1)S(1)}) custom-call(s32[2]{0:T(128)S(1)} %fusion.13.cols, bf16[256,1024]{1,0:T(8,128)(2,1)S(1)} %copy-done.23, bf16[1024,8192]{1,0:T(8,128)(2,1)} %refs_4_.3, f32[256,1024]{1,0:T(8,128)S(1)} %grad_product.2.refs_0_.refs_5_), custom_call_target="tpu_custom_call" | custom-call | flops 14720000000 | bytes 65536 | tf_op jit(solution)/shard_map/project/pallas_call | solution.py:295
  54.3 2.0 %collective-permute-start.12 = (bf16[256,1024]{1,0:T(8,128)(2,1)S(1)}, bf16[256,1024]{1,0:T(8,128)(2,1)S(1)}, u32[]{:S(2)}, u32[]{:S(2)}) collective-permute-start(bf16[256,1024]{1,0:T(8,128)(2,1)S(1)} %get-tuple-element.53), channel_id=1, source_target_pairs={{0,3},{1,0},{2,1},{3,2},{4,7},{5,4},{6,5},{7,6},{8,11},{9,8},{10,9... | collective-permute-start | bytes 1572872 | tf_op jit(solution)/shard_map/ppermute | solution.py:41
  56.4 3.5 %select.66 = (bf16[256,1536]{1,0:T(8,128)(2,1)S(1)}, bf16[256,1536]{1,0:T(8,128)(2,1)}, bf16[256,1536]{1,0:T(8,128)(2,1)}, bf16[256,1536]{1,0:T(8,128)(2,1)S(1)}) custom-call(s32[9]{0:T(128)S(1)} %pad_add_fusion.places, bf16[256,1024]{1,0:T(8,128)(2,1)S(1)} %copy-done.7, bf16[256,1024]{1,0:T(8,128)(2,1)S(1)} %copy-done.19, bf16[256,1024]{1,0:T(8,128)(2,1)S(1)} %copy-done.16, ...), custom_call_target="tpu_custom_call" | custom-call | flops 11500000256 | bytes 65536 | tf_op jit(solution)/shard_map/select/pallas_call | solution.py:334
  61.0 2.2 %collective-permute-start.14 = (bf16[256,1536]{1,0:T(8,128)(2,1)}, bf16[256,1536]{1,0:T(8,128)(2,1)S(1)}, u32[]{:S(2)}, u32[]{:S(2)}) collective-permute-start(bf16[256,1536]{1,0:T(8,128)(2,1)} %get-tuple-element.58), channel_id=1, source_target_pairs={{0,96},{8,104},{16,112},{24,120},{32,0},{40,8},{48,16},{56,24},{64... | collective-permute-start | bytes 2359304 | tf_op jit(solution)/shard_map/ppermute | solution.py:49
  63.5 4.8 %project.4 = (f32[256,1024]{1,0:T(8,128)}, bf16[256,1024]{1,0:T(8,128)(2,1)}) custom-call(s32[2]{0:T(128)S(1)} %fusion.9.cols, bf16[256,1024]{1,0:T(8,128)(2,1)S(1)} %copy-done.24, bf16[1024,8192]{1,0:T(8,128)(2,1)} %refs_4_.3, bf16[256,1536]{1,0:T(8,128)(2,1)S(1)} %get-tuple-element.50.refs_0_.g0, bf16[1024,256]{1,0:T(8,128)(2,1)S(1)} %copy-done.2, ...), custom_call_target="tpu_custom_call" | custom-call | flops 27599998976 | bytes 65536 | tf_op jit(solution)/shard_map/project/pallas_call | solution.py:295
  68.3 2.2 %add_convert_fusion.2 = bf16[256,1024]{1,0:T(8,128)(2,1)} fusion(f32[256,1024]{1,0:T(8,128)} %get-tuple-element.67, bf16[256,1024]{1,0:T(8,128)(2,1)S(1)} %collective-permute-done.11.refs_1_), kind=kLoop, calls=%fused_computation.3 | loop fusion | flops 786432 | bytes 2097152 | tf_op jit(solution)/shard_map/convert_element_type | solution.py:540
  70.5 3.2 %collective-permute-start.17 = (bf16[256,1024]{1,0:T(8,128)(2,1)}, bf16[256,1024]{1,0:T(8,128)(2,1)}, u32[]{:S(2)}, u32[]{:S(2)}) collective-permute-start(bf16[256,1024]{1,0:T(8,128)(2,1)} %get-tuple-element.52.refs_0_), channel_id=1, source_target_pairs={{0,3},{1,0},{2,1},{3,2},{4,7},{5,4},{6,5},{7,6},{8,11},{9,8},{10,9... | collective-permute-start | bytes 1572872 | tf_op jit(solution)/shard_map/ppermute | solution.py:41
  73.7 8.0 %project.5 = (bf16[256,1024]{1,0:T(8,128)(2,1)S(1)}, f32[256,1024]{1,0:T(8,128)}, f32[256,1024]{1,0:T(8,128)}, f32[256,1024]{1,0:T(8,128)}) custom-call(s32[4]{0:T(128)S(1)} %fusion.2.cols, bf16[256,1024]{1,0:T(8,128)(2,1)S(1)} %copy-done.24, bf16[1024,8192]{1,0:T(8,128)(2,1)} %refs_4_.3, bf16[256,1024]{1,0:T(8,128)(2,1)} %get-tuple-element.52.refs_0_, ...), custom_call_target="tpu_custom_call" | custom-call | flops 36800000000 | bytes 65536 | tf_op jit(solution)/shard_map/project/pallas_call | solution.py:295
  83.1 2.0 %select.67 = (bf16[256,512]{1,0:T(8,128)(2,1)S(1)}, bf16[256,512]{1,0:T(8,128)(2,1)S(1)}, bf16[256,512]{1,0:T(8,128)(2,1)S(1)}, bf16[256,512]{1,0:T(8,128)(2,1)S(1)}) custom-call(s32[9]{0:T(128)S(1)} %pad_add_fusion.places, bf16[256,1024]{1,0:T(8,128)(2,1)S(1)} %copy-done.7, bf16[256,1024]{1,0:T(8,128)(2,1)S(1)} %copy-done.19, ...), custom_call_target="tpu_custom_call" | custom-call | flops 920000000 | bytes 65536 | tf_op jit(solution)/shard_map/select/pallas_call | solution.py:334
  85.2 8.2 %grad_product.3 = (bf16[256,1024]{1,0:T(8,128)(2,1)S(1)}, f32[256,1024]{1,0:T(8,128)}, bf16[192,1024]{1,0:T(8,128)(2,1)S(1)}) custom-call(s32[4]{0:T(128)S(1)} %get-tuple-element.89.cols, bf16[256,1024]{1,0:T(8,128)(2,1)S(1)} %copy-done.7, bf16[256,1024]{1,0:T(8,128)(2,1)S(1)} %collective-permute-done.6.refs_6_.refs_1_, bf16[256,1024]{1,0:T(8,128)(2,1)S(1)} %copy-done.9, ...), custom_call_target="tpu_custom_call" | custom-call | flops 920000000 | bytes 65536 | tf_op jit(solution)/shard_map/grad_product/pallas_call | solution.py:262
  94.8 3.3 %collective-permute-start.19 = (bf16[256,1024]{1,0:T(8,128)(2,1)S(1)}, bf16[256,1024]{1,0:T(8,128)(2,1)S(1)}, u32[]{:S(2)}, u32[]{:S(2)}) collective-permute-start(bf16[256,1024]{1,0:T(8,128)(2,1)S(1)} %add_convert_fusion.1.refs_1_), channel_id=1, source_target_pairs={{0,4},{1,5},{2,6},{3,7},{4,0},{5,1},{6,2},{7,3},{8,12},{9,13},{10,... | collective-permute-start | bytes 1572872 | tf_op jit(solution)/shard_map/ppermute | solution.py:45
  99.4 1.9 %collective-permute-start.24 = (bf16[256,512]{1,0:T(8,128)(2,1)S(1)}, bf16[256,512]{1,0:T(8,128)(2,1)S(1)}, u32[]{:S(2)}, u32[]{:S(2)}) collective-permute-start(bf16[256,512]{1,0:T(8,128)(2,1)S(1)} %get-tuple-element.85), channel_id=1, source_target_pairs={{0,96},{8,104},{16,112},{24,120},{32,0},{40,8},{48,16},{56,24},{64... | collective-permute-start | bytes 786440 | tf_op jit(solution)/shard_map/ppermute | solution.py:49
  101.3 1.5 %collective-permute-start.18 = (bf16[192,1024]{1,0:T(8,128)(2,1)S(1)}, bf16[192,1024]{1,0:T(8,128)(2,1)S(1)}, u32[]{:S(2)}, u32[]{:S(2)}) collective-permute-start(bf16[192,1024]{1,0:T(8,128)(2,1)S(1)} %get-tuple-element.73), channel_id=1, source_target_pairs={{8,0},{16,8},{24,16},{32,24},{40,32},{48,40},{56,48},{64,56},{72,6... | collective-permute-start | bytes 1179656 | tf_op jit(solution)/shard_map/ppermute | solution.py:58
  102.9 4.2 %weight_sum.2 = (bf16[2,1024,384]{2,1,0:T(8,128)(2,1)S(1)}, bf16[2,1024,384]{2,1,0:T(8,128)(2,1)S(1)}) custom-call(bf16[1024,256]{1,0:T(8,128)(2,1)S(1)} %copy-done.2, bf16[1024,256]{1,0:T(8,128)(2,1)S(1)} %collective-permute-done.8.refs_2_.refs_4_.q1, bf16[1024,256]{1,0:T(8,128)(2,1)S(1)} %copy-done.6, bf16[1024,256]{1,0:T(8,128)(2,1)S(1)} %copy-done.4, ...), custom_call_target="tpu_custom_call" | custom-call | flops 920000000 | bytes 65536 | tf_op jit(solution)/shard_map/weight_sum/pallas_call | solution.py:365
  108.5 2.9 %collective-permute-done.20.from_core = bf16[2,1024,384]{2,1,0:T(8,128)(2,1)S(1)} collective-permute-done((bf16[2,1024,384]{2,1,0:T(8,128)(2,1)S(1)}, bf16[2,1024,384]{2,1,0:T(8,128)(2,1)S(1)}, u32[]{:S(2)}, u32[]{:S(2)}) %collective-permute-start.20) | collective-permute-done | bytes 1572896 | tf_op jit(solution)/shard_map/ppermute | solution.py:53
  111.4 2.1 %collective-permute-start.25 = (bf16[256,512]{1,0:T(8,128)(2,1)S(1)}, bf16[256,512]{1,0:T(8,128)(2,1)S(1)}, u32[]{:S(2)}, u32[]{:S(2)}) collective-permute-start(bf16[256,512]{1,0:T(8,128)(2,1)S(1)} %get-tuple-element.86), channel_id=1, source_target_pairs={{0,64},{8,72},{16,80},{24,88},{32,96},{40,104},{48,112},{56,120},{... | collective-permute-start | bytes 786440 | tf_op jit(solution)/shard_map/ppermute | solution.py:49
  115.3 6.7 %backward.1 = (bf16[256,1024]{1,0:T(8,128)(2,1)}, bf16[256,1024]{1,0:T(8,128)(2,1)}, bf16[256,1024]{1,0:T(8,128)(2,1)}) custom-call(bf16[256,1024]{1,0:T(8,128)(2,1)S(1)} %get-tuple-element.66.refs_0_.gc, f32[256,1024]{1,0:T(8,128)S(1)} %copy-done.20, f32[256,1024]{1,0:T(8,128)S(1)} %copy-done.11, f32[256,1024]{1,0:T(8,128)S(1)} %copy-done.10, ...), custom_call_target="tpu_custom_call" | custom-call | flops 36800000000 | bytes 65536 | tf_op jit(solution)/shard_map/backward/pallas_call | solution.py:183
  122.0 3.2 %collective-permute-start.22 = (bf16[256,1024]{1,0:T(8,128)(2,1)S(1)}, bf16[256,1024]{1,0:T(8,128)(2,1)S(1)}, u32[]{:S(2)}, u32[]{:S(2)}) collective-permute-start(bf16[256,1024]{1,0:T(8,128)(2,1)S(1)} %get-tuple-element.77), channel_id=1, source_target_pairs={{0,3},{1,0},{2,1},{3,2},{4,7},{5,4},{6,5},{7,6},{8,11},{9,8},{10,9... | collective-permute-start | bytes 1572872 | tf_op jit(solution)/shard_map/ppermute | solution.py:41
  126.3 1.9 %weight_sum.3 = (bf16[2,1024,128]{2,1,0:T(8,128)(2,1)S(1)}, bf16[2,1024,128]{2,1,0:T(8,128)(2,1)S(1)}) custom-call(bf16[1024,256]{1,0:T(8,128)(2,1)S(1)} %copy-done.2, bf16[1024,256]{1,0:T(8,128)(2,1)S(1)} %collective-permute-done.8.refs_2_.refs_4_.q1, bf16[1024,256]{1,0:T(8,128)(2,1)S(1)} %copy-done.6, bf16[1024,256]{1,0:T(8,128)(2,1)S(1)} %copy-done.4, ...), custom_call_target="tpu_custom_call" | custom-call | flops 920000000 | bytes 65536 | tf_op jit(solution)/shard_map/weight_sum/pallas_call | solution.py:365
  128.3 5.1 %collective-permute-done.27.from_yl = bf16[1024,384]{1,0:T(8,128)(2,1)S(1)} collective-permute-done((bf16[1024,384]{1,0:T(8,128)(2,1)S(1)}, bf16[1024,384]{1,0:T(8,128)(2,1)S(1)}, u32[]{:S(2)}, u32[]{:S(2)}) %collective-permute-start.27) | collective-permute-done | bytes 786464 | tf_op jit(solution)/shard_map/ppermute | solution.py:62
  134.7 2.5 %collective-permute-done.21 = bf16[256,1024]{1,0:T(8,128)(2,1)S(1)} collective-permute-done((bf16[256,1024]{1,0:T(8,128)(2,1)S(1)}, bf16[256,1024]{1,0:T(8,128)(2,1)S(1)}, u32[]{:S(2)}, u32[]{:S(2)}) %collective-permute-start.21) | collective-permute-done | bytes 524320 | tf_op jit(solution)/shard_map/ppermute | solution.py:41
  138.3 3.2 %collective-permute-done.28.from_yl = bf16[1024,128]{1,0:T(8,128)(2,1)S(1)} collective-permute-done((bf16[1024,128]{1,0:T(8,128)(2,1)S(1)}, bf16[1024,128]{1,0:T(8,128)(2,1)S(1)}, u32[]{:S(2)}, u32[]{:S(2)}) %collective-permute-start.28) | collective-permute-done | bytes 262176 | tf_op jit(solution)/shard_map/ppermute | solution.py:62
  141.4 1.6 %finish.3 = bf16[1024,512]{1,0:T(8,128)(2,1)} custom-call(bf16[2,1024,128]{2,1,0:T(8,128)(2,1)S(1)} %get-tuple-element.87.kept, bf16[2,1024,128]{2,1,0:T(8,128)(2,1)S(1)} %collective-permute-done.26.from_core, bf16[1024,128]{1,0:T(8,128)(2,1)S(1)} %collective-permute-done.28.from_yl, bf16[1024,384]{1,0:T(8,128)(2,1)S(1)} %finish.2.refs_0_), custom_call_target="tpu_custom_call" | custom-call | flops 4600000000 | bytes 65536 | tf_op jit(solution)/shard_map/finish/pallas_call | solution.py:470
  (145 shorter events, 20.9 us)
Async XLA Ops:
  0.7 11.0 %copy-start.36 = (s32[4]{0:T(128)S(1)}, s32[4]{0:T(128)}, u32[]{:S(2)}) copy-start(s32[4]{0:T(128)} %constant.199.clone) | copy-start | bytes 52
  0.7 11.0 %copy-start.35 = (s32[4]{0:T(128)S(1)}, s32[4]{0:T(128)}, u32[]{:S(2)}) copy-start(s32[4]{0:T(128)} %constant.190.clone) | copy-start | bytes 52
  0.7 11.1 %copy-start.34 = (s32[2]{0:T(128)S(1)}, s32[2]{0:T(128)}, u32[]{:S(2)}) copy-start(s32[2]{0:T(128)} %constant.191.clone) | copy-start | bytes 28
  0.7 22.7 %collective-permute-start.3 = (bf16[256,1024]{1,0:T(8,128)(2,1)}, bf16[256,1024]{1,0:T(8,128)(2,1)S(1)}, u32[]{:S(2)}, u32[]{:S(2)}) collective-permute-start(bf16[256,1024]{1,0:T(8,128)(2,1)} %refs_0_.5), channel_id=1, source_target_pairs={{0,3},{1,0},{2,1},{3,2},{4,7},{5,4},{6,5},{7,6},{8,11},{9,8},{10,9... | collective-permute-start | bytes 1572872 | tf_op jit(solution)/shard_map/ppermute | solution.py:41
  3.7 19.9 %collective-permute-start.2 = (bf16[256,1024]{1,0:T(8,128)(2,1)}, bf16[256,1024]{1,0:T(8,128)(2,1)S(1)}, u32[]{:S(2)}, u32[]{:S(2)}) collective-permute-start(bf16[256,1024]{1,0:T(8,128)(2,1)} %refs_0_.5), channel_id=1, source_target_pairs={{0,1},{1,2},{2,3},{3,0},{4,5},{5,6},{6,7},{7,4},{8,9},{9,10},{10,1... | collective-permute-start | bytes 1572872 | tf_op jit(solution)/shard_map/ppermute | solution.py:41
  3.7 16.6 %collective-permute-start.1 = (bf16[256,1024]{1,0:T(8,128)(2,1)}, bf16[256,1024]{1,0:T(8,128)(2,1)S(1)}, u32[]{:S(2)}, u32[]{:S(2)}) collective-permute-start(bf16[256,1024]{1,0:T(8,128)(2,1)} %refs_0_.5), channel_id=1, source_target_pairs={{0,4},{1,5},{2,6},{3,7},{4,0},{5,1},{6,2},{7,3},{8,12},{9,13},{10,... | collective-permute-start | bytes 1572872 | tf_op jit(solution)/shard_map/ppermute | solution.py:45
  10.0 13.5 %collective-permute-start = (bf16[176,1024]{1,0:T(8,128)(2,1)}, bf16[176,1024]{1,0:T(8,128)(2,1)S(1)}, u32[]{:S(2)}, u32[]{:S(2)}) collective-permute-start(bf16[176,1024]{1,0:T(8,128)(2,1)} %last_rows.1), channel_id=1, source_target_pairs={{0,8},{8,16},{16,24},{24,32},{32,40},{40,48},{48,56},{56,64},{64,7... | collective-permute-start | bytes 1081352 | tf_op jit(solution)/shard_map/ppermute | solution.py:58
  20.2 18.3 %collective-permute-start.5 = (bf16[256,1024]{1,0:T(8,128)(2,1)S(1)}, bf16[256,1024]{1,0:T(8,128)(2,1)S(1)}, u32[]{:S(2)}, u32[]{:S(2)}) collective-permute-start(bf16[256,1024]{1,0:T(8,128)(2,1)S(1)} %collective-permute-done.1.refs_0_.refs_3_.refs_2_), channel_id=1, source_target_pairs={{0,3},{1,0},{2,1},{3,2},{4,7},{5,4},{6,5},{7,6},{8,11},{9,8},{10,9... | collective-permute-start | bytes 1572872 | tf_op jit(solution)/shard_map/ppermute | solution.py:41
  23.5 15.0 %collective-permute-start.4 = (bf16[256,1024]{1,0:T(8,128)(2,1)S(1)}, bf16[256,1024]{1,0:T(8,128)(2,1)S(1)}, u32[]{:S(2)}, u32[]{:S(2)}) collective-permute-start(bf16[256,1024]{1,0:T(8,128)(2,1)S(1)} %collective-permute-done.1.refs_0_.refs_3_.refs_2_), channel_id=1, source_target_pairs={{0,1},{1,2},{2,3},{3,0},{4,5},{5,6},{6,7},{7,4},{8,9},{9,10},{10,1... | collective-permute-start | bytes 1572872 | tf_op jit(solution)/shard_map/ppermute | solution.py:41
  32.5 27.4 %collective-permute-start.10 = (bf16[1024,256]{1,0:T(8,128)(2,1)}, bf16[1024,256]{1,0:T(8,128)(2,1)S(1)}, u32[]{:S(2)}, u32[]{:S(2)}) collective-permute-start(bf16[1024,256]{1,0:T(8,128)(2,1)} %get-tuple-element.51.refs_1_.refs_3_.q0), channel_id=1, source_target_pairs={{0,64},{8,72},{16,80},{24,88},{32,96},{40,104},{48,112},{56,120},{... | collective-permute-start | bytes 1572872 | tf_op jit(solution)/shard_map/ppermute | solution.py:49
  36.4 24.6 %collective-permute-start.9 = (bf16[1024,256]{1,0:T(8,128)(2,1)}, bf16[1024,256]{1,0:T(8,128)(2,1)S(1)}, u32[]{:S(2)}, u32[]{:S(2)}) collective-permute-start(bf16[1024,256]{1,0:T(8,128)(2,1)} %get-tuple-element.51.refs_1_.refs_3_.q0), channel_id=1, source_target_pairs={{0,96},{8,104},{16,112},{24,120},{32,0},{40,8},{48,16},{56,24},{64... | collective-permute-start | bytes 1572872 | tf_op jit(solution)/shard_map/ppermute | solution.py:49
  37.2 26.1 %collective-permute-start.8 = (bf16[1024,256]{1,0:T(8,128)(2,1)}, bf16[1024,256]{1,0:T(8,128)(2,1)S(1)}, u32[]{:S(2)}, u32[]{:S(2)}) collective-permute-start(bf16[1024,256]{1,0:T(8,128)(2,1)} %get-tuple-element.51.refs_1_.refs_3_.q0), channel_id=1, source_target_pairs={{0,32},{8,40},{16,48},{24,56},{32,64},{40,72},{48,80},{56,88},{64,... | collective-permute-start | bytes 1572872 | tf_op jit(solution)/shard_map/ppermute | solution.py:49
  38.5 17.8 %collective-permute-start.6 = (bf16[256,1024]{1,0:T(8,128)(2,1)}, bf16[256,1024]{1,0:T(8,128)(2,1)S(1)}, u32[]{:S(2)}, u32[]{:S(2)}) collective-permute-start(bf16[256,1024]{1,0:T(8,128)(2,1)} %copy-done.17), channel_id=1, source_target_pairs={{0,1},{1,2},{2,3},{3,0},{4,5},{5,6},{6,7},{7,4},{8,9},{9,10},{10,1... | collective-permute-start | bytes 1572872 | tf_op jit(solution)/shard_map/ppermute | solution.py:41
  38.5 15.8 %collective-permute-start.7 = (bf16[256,1024]{1,0:T(8,128)(2,1)S(1)}, bf16[256,1024]{1,0:T(8,128)(2,1)S(1)}, u32[]{:S(2)}, u32[]{:S(2)}) collective-permute-start(bf16[256,1024]{1,0:T(8,128)(2,1)S(1)} %collective-permute-done.5.refs_3_.refs_5_), channel_id=1, source_target_pairs={{0,3},{1,0},{2,1},{3,2},{4,7},{5,4},{6,5},{7,6},{8,11},{9,8},{10,9... | collective-permute-start | bytes 1572872 | tf_op jit(solution)/shard_map/ppermute | solution.py:41
  54.3 16.2 %collective-permute-start.12 = (bf16[256,1024]{1,0:T(8,128)(2,1)S(1)}, bf16[256,1024]{1,0:T(8,128)(2,1)S(1)}, u32[]{:S(2)}, u32[]{:S(2)}) collective-permute-start(bf16[256,1024]{1,0:T(8,128)(2,1)S(1)} %get-tuple-element.53), channel_id=1, source_target_pairs={{0,3},{1,0},{2,1},{3,2},{4,7},{5,4},{6,5},{7,6},{8,11},{9,8},{10,9... | collective-permute-start | bytes 1572872 | tf_op jit(solution)/shard_map/ppermute | solution.py:41
  56.3 12.0 %collective-permute-start.11 = (bf16[256,1024]{1,0:T(8,128)(2,1)S(1)}, bf16[256,1024]{1,0:T(8,128)(2,1)S(1)}, u32[]{:S(2)}, u32[]{:S(2)}) collective-permute-start(bf16[256,1024]{1,0:T(8,128)(2,1)S(1)} %get-tuple-element.49.refs_8_), channel_id=1, source_target_pairs={{0,1},{1,2},{2,3},{3,0},{4,5},{5,6},{6,7},{7,4},{8,9},{9,10},{10,1... | collective-permute-start | bytes 1572872 | tf_op jit(solution)/shard_map/ppermute | solution.py:41
  59.9 39.5 %collective-permute-start.13 = (bf16[256,1536]{1,0:T(8,128)(2,1)}, bf16[256,1536]{1,0:T(8,128)(2,1)S(1)}, u32[]{:S(2)}, u32[]{:S(2)}) collective-permute-start(bf16[256,1536]{1,0:T(8,128)(2,1)} %get-tuple-element.57), channel_id=1, source_target_pairs={{0,32},{8,40},{16,48},{24,56},{32,64},{40,72},{48,80},{56,88},{64,... | collective-permute-start | bytes 2359304 | tf_op jit(solution)/shard_map/ppermute | solution.py:49
  61.0 40.3 %collective-permute-start.14 = (bf16[256,1536]{1,0:T(8,128)(2,1)}, bf16[256,1536]{1,0:T(8,128)(2,1)S(1)}, u32[]{:S(2)}, u32[]{:S(2)}) collective-permute-start(bf16[256,1536]{1,0:T(8,128)(2,1)} %get-tuple-element.58), channel_id=1, source_target_pairs={{0,96},{8,104},{16,112},{24,120},{32,0},{40,8},{48,16},{56,24},{64... | collective-permute-start | bytes 2359304 | tf_op jit(solution)/shard_map/ppermute | solution.py:49
  63.3 39.6 %collective-permute-start.15 = (bf16[256,1536]{1,0:T(8,128)(2,1)S(1)}, bf16[256,1536]{1,0:T(8,128)(2,1)S(1)}, u32[]{:S(2)}, u32[]{:S(2)}) collective-permute-start(bf16[256,1536]{1,0:T(8,128)(2,1)S(1)} %get-tuple-element.59), channel_id=1, source_target_pairs={{0,64},{8,72},{16,80},{24,88},{32,96},{40,104},{48,112},{56,120},{... | collective-permute-start | bytes 2359304 | tf_op jit(solution)/shard_map/ppermute | solution.py:49
  70.5 22.9 %collective-permute-start.16 = (bf16[256,1024]{1,0:T(8,128)(2,1)}, bf16[256,1024]{1,0:T(8,128)(2,1)S(1)}, u32[]{:S(2)}, u32[]{:S(2)}) collective-permute-start(bf16[256,1024]{1,0:T(8,128)(2,1)} %add_convert_fusion.2), channel_id=1, source_target_pairs={{0,1},{1,2},{2,3},{3,0},{4,5},{5,6},{6,7},{7,4},{8,9},{9,10},{10,1... | collective-permute-start | bytes 1572872 | tf_op jit(solution)/shard_map/ppermute | solution.py:41
  70.5 22.9 %collective-permute-start.17 = (bf16[256,1024]{1,0:T(8,128)(2,1)}, bf16[256,1024]{1,0:T(8,128)(2,1)}, u32[]{:S(2)}, u32[]{:S(2)}) collective-permute-start(bf16[256,1024]{1,0:T(8,128)(2,1)} %get-tuple-element.52.refs_0_), channel_id=1, source_target_pairs={{0,3},{1,0},{2,1},{3,2},{4,7},{5,4},{6,5},{7,6},{8,11},{9,8},{10,9... | collective-permute-start | bytes 1572872 | tf_op jit(solution)/shard_map/ppermute | solution.py:41
  94.8 19.7 %collective-permute-start.19 = (bf16[256,1024]{1,0:T(8,128)(2,1)S(1)}, bf16[256,1024]{1,0:T(8,128)(2,1)S(1)}, u32[]{:S(2)}, u32[]{:S(2)}) collective-permute-start(bf16[256,1024]{1,0:T(8,128)(2,1)S(1)} %add_convert_fusion.1.refs_1_), channel_id=1, source_target_pairs={{0,4},{1,5},{2,6},{3,7},{4,0},{5,1},{6,2},{7,3},{8,12},{9,13},{10,... | collective-permute-start | bytes 1572872 | tf_op jit(solution)/shard_map/ppermute | solution.py:45
  98.1 24.0 %collective-permute-start.23 = (bf16[256,512]{1,0:T(8,128)(2,1)S(1)}, bf16[256,512]{1,0:T(8,128)(2,1)S(1)}, u32[]{:S(2)}, u32[]{:S(2)}) collective-permute-start(bf16[256,512]{1,0:T(8,128)(2,1)S(1)} %get-tuple-element.84), channel_id=1, source_target_pairs={{0,32},{8,40},{16,48},{24,56},{32,64},{40,72},{48,80},{56,88},{64,... | collective-permute-start | bytes 786440 | tf_op jit(solution)/shard_map/ppermute | solution.py:49
  99.4 25.9 %collective-permute-start.24 = (bf16[256,512]{1,0:T(8,128)(2,1)S(1)}, bf16[256,512]{1,0:T(8,128)(2,1)S(1)}, u32[]{:S(2)}, u32[]{:S(2)}) collective-permute-start(bf16[256,512]{1,0:T(8,128)(2,1)S(1)} %get-tuple-element.85), channel_id=1, source_target_pairs={{0,96},{8,104},{16,112},{24,120},{32,0},{40,8},{48,16},{56,24},{64... | collective-permute-start | bytes 786440 | tf_op jit(solution)/shard_map/ppermute | solution.py:49
  101.3 12.5 %collective-permute-start.18 = (bf16[192,1024]{1,0:T(8,128)(2,1)S(1)}, bf16[192,1024]{1,0:T(8,128)(2,1)S(1)}, u32[]{:S(2)}, u32[]{:S(2)}) collective-permute-start(bf16[192,1024]{1,0:T(8,128)(2,1)S(1)} %get-tuple-element.73), channel_id=1, source_target_pairs={{8,0},{16,8},{24,16},{32,24},{40,32},{48,40},{56,48},{64,56},{72,6... | collective-permute-start | bytes 1179656 | tf_op jit(solution)/shard_map/ppermute | solution.py:58
  107.1 4.2 %collective-permute-start.20 = (bf16[2,1024,384]{2,1,0:T(8,128)(2,1)S(1)}, bf16[2,1024,384]{2,1,0:T(8,128)(2,1)S(1)}, u32[]{:S(2)}, u32[]{:S(2)}) collective-permute-start(bf16[2,1024,384]{2,1,0:T(8,128)(2,1)S(1)} %get-tuple-element.74), channel_id=1, source_target_pairs={{0,8},{8,0},{16,24},{24,16},{32,40},{40,32},{48,56},{56,48},{64,72... | collective-permute-start | bytes 4718600 | tf_op jit(solution)/shard_map/ppermute | solution.py:53
  111.4 13.9 %collective-permute-start.25 = (bf16[256,512]{1,0:T(8,128)(2,1)S(1)}, bf16[256,512]{1,0:T(8,128)(2,1)S(1)}, u32[]{:S(2)}, u32[]{:S(2)}) collective-permute-start(bf16[256,512]{1,0:T(8,128)(2,1)S(1)} %get-tuple-element.86), channel_id=1, source_target_pairs={{0,64},{8,72},{16,80},{24,88},{32,96},{40,104},{48,112},{56,120},{... | collective-permute-start | bytes 786440 | tf_op jit(solution)/shard_map/ppermute | solution.py:49
  113.8 19.6 %collective-permute-start.27 = (bf16[1024,384]{1,0:T(8,128)(2,1)S(1)}, bf16[1024,384]{1,0:T(8,128)(2,1)S(1)}, u32[]{:S(2)}, u32[]{:S(2)}) collective-permute-start(bf16[1024,384]{1,0:T(8,128)(2,1)S(1)} %combine.2.refs_1_), channel_id=1, source_target_pairs={{0,16},{8,24},{16,0},{24,8},{32,48},{40,56},{48,32},{56,40},{64,80... | collective-permute-start | bytes 2359304 | tf_op jit(solution)/shard_map/ppermute | solution.py:62
  122.0 15.1 %collective-permute-start.21 = (bf16[256,1024]{1,0:T(8,128)(2,1)S(1)}, bf16[256,1024]{1,0:T(8,128)(2,1)S(1)}, u32[]{:S(2)}, u32[]{:S(2)}) collective-permute-start(bf16[256,1024]{1,0:T(8,128)(2,1)S(1)} %get-tuple-element.76.refs_0_), channel_id=1, source_target_pairs={{0,1},{1,2},{2,3},{3,0},{4,5},{5,6},{6,7},{7,4},{8,9},{9,10},{10,1... | collective-permute-start | bytes 1572872 | tf_op jit(solution)/shard_map/ppermute | solution.py:41
  122.0 15.1 %collective-permute-start.22 = (bf16[256,1024]{1,0:T(8,128)(2,1)S(1)}, bf16[256,1024]{1,0:T(8,128)(2,1)S(1)}, u32[]{:S(2)}, u32[]{:S(2)}) collective-permute-start(bf16[256,1024]{1,0:T(8,128)(2,1)S(1)} %get-tuple-element.77), channel_id=1, source_target_pairs={{0,3},{1,0},{2,1},{3,2},{4,7},{5,4},{6,5},{7,6},{8,11},{9,8},{10,9... | collective-permute-start | bytes 1572872 | tf_op jit(solution)/shard_map/ppermute | solution.py:41
  128.2 5.5 %collective-permute-start.26 = (bf16[2,1024,128]{2,1,0:T(8,128)(2,1)S(1)}, bf16[2,1024,128]{2,1,0:T(8,128)(2,1)S(1)}, u32[]{:S(2)}, u32[]{:S(2)}) collective-permute-start(bf16[2,1024,128]{2,1,0:T(8,128)(2,1)S(1)} %get-tuple-element.88), channel_id=1, source_target_pairs={{0,8},{8,0},{16,24},{24,16},{32,40},{40,32},{48,56},{56,48},{64,72... | collective-permute-start | bytes 1572872 | tf_op jit(solution)/shard_map/ppermute | solution.py:53
  133.9 7.5 %collective-permute-start.28 = (bf16[1024,128]{1,0:T(8,128)(2,1)S(1)}, bf16[1024,128]{1,0:T(8,128)(2,1)S(1)}, u32[]{:S(2)}, u32[]{:S(2)}) collective-permute-start(bf16[1024,128]{1,0:T(8,128)(2,1)S(1)} %combine.3), channel_id=1, source_target_pairs={{0,16},{8,24},{16,0},{24,8},{32,48},{40,56},{48,32},{56,40},{64,80... | collective-permute-start | bytes 786440 | tf_op jit(solution)/shard_map/ppermute | solution.py:62
  (37 other events, 197.3 us)

commit v4 on v3

--- a/solution.py
+++ b/solution.py
@@ -12,6 +12,7 @@
 HALO = 144
 HEAD = 16
 LANES = 128
+PARTS = 4
 VMEM_LIMIT = 16 * 1024 * 1024
 VMEM_ALL = 60 * 1024 * 1024
 VMEM_MOST = 50 * 1024 * 1024
@@ -82,10 +83,35 @@
     return out
 
 
-def forward_kernel(
-    q, k, v, halo, sf, taps, gain, *refs
-):
-    qc_o, ca_o, kc_o, vc_o, qg_o, qgt_o, qs, ks, vs, table = refs[-10:]
+def table_kernel(taps, out):
+    toeplitz_into(out, taps[...])
+
+
+def toeplitz_table(taps):
+    groups, window = taps.shape
+    return pl.pallas_call(
+        table_kernel,
+        grid=(groups // 8,),
+        in_specs=[pl.BlockSpec((8, window), lambda i: (i, 0))],
+        out_specs=pl.BlockSpec((8 * LANES, window), lambda i: (i, 0)),
+        out_shape=jax.ShapeDtypeStruct((groups * LANES, window), BF16),
+        compiler_params=pltpu.CompilerParams(vmem_limit_bytes=VMEM_LIMIT),
+        cost_estimate=cost(6),
+        name="toeplitz_table",
+    )(taps)
+
+
+def forward_kernel(q, k, v, halo, sf, table, gain, *refs):
+    outs, scratch = refs[-9:-3], refs[-3:]
+    for part in range(PARTS):
+        lanes, rows = pl.ds(part * LANES, LANES), pl.ds(part * 8 * LANES, 8 * LANES)
+        forward_part(
+            *[a.at[:, lanes] for a in (q, k, v, halo)], sf.at[:, :, lanes], table.at[rows], gain.at[:, lanes],
+            *[a.at[:, lanes] for a in outs[:5]], outs[5].at[lanes], *scratch,
+        )
+
+
+def forward_part(q, k, v, halo, sf, table, gain, qc_o, ca_o, kc_o, vc_o, qg_o, qgt_o, qs, ks, vs):
     n = q.shape[0]
     qs[:HEAD] = halo[:HEAD].astype(F32)
     qs[HEAD:] = q[...].astype(F32)
@@ -93,7 +119,6 @@
     ks[HEAD:] = k[...].astype(F32)
     vs[:HEAD] = halo[2 * HEAD : 3 * HEAD].astype(F32)
     vs[HEAD:] = v[...].astype(F32)
-    toeplitz_into(table, taps[...])
 
     def short(scr, member, first, rows):
         acc = sf[member, 0:1, :] * scr[pl.ds(first, rows), :]
@@ -118,36 +143,44 @@
     qgt_o[...] = gated.T.astype(BF16)
 
 
-def forward(q, k, v, halo, sf, taps, gain, after):
+def forward(q, k, v, halo, sf, table, gain, after):
     n, ch = q.shape
-    col = lambda rows: pl.BlockSpec((rows, LANES), lambda i: (0, i))
+    col = lambda rows: pl.BlockSpec((rows, PARTS * LANES), lambda i: (0, i))
     return pl.pallas_call(
         forward_kernel,
-        grid=(ch // LANES,),
+        grid=(ch // LANES // PARTS,),
         in_specs=[
             col(n), col(n), col(n), col(3 * HEAD + LANES),
-            pl.BlockSpec((3, 7, LANES), lambda i: (0, 0, i)),
-            pl.BlockSpec((8, 2 * LANES), lambda i: (i, 0)),
+            pl.BlockSpec((3, 7, PARTS * LANES), lambda i: (0, 0, i)),
+            pl.BlockSpec((PARTS * 8 * LANES, 2 * LANES), lambda i: (i, 0)),
             col(1),
         ]
         + [pl.BlockSpec(memory_space=pl.ANY)] * len(after),
-        out_specs=[col(n)] * 5 + [pl.BlockSpec((LANES, n), lambda i: (i, 0))],
+        out_specs=[col(n)] * 5 + [pl.BlockSpec((PARTS * LANES, n), lambda i: (i, 0))],
         out_shape=[jax.ShapeDtypeStruct((n, ch), F32)] * 4
         + [jax.ShapeDtypeStruct((n, ch), BF16), jax.ShapeDtypeStruct((ch, n), BF16)],
         scratch_shapes=[
             pltpu.VMEM((HEAD + n, LANES), F32),
             pltpu.VMEM((HEAD + n, LANES), F32),
             pltpu.VMEM((HEAD + n, LANES), F32),
-            pltpu.VMEM((8 * LANES, 2 * LANES), BF16),
         ],
         compiler_params=pltpu.CompilerParams(vmem_limit_bytes=VMEM_ALL),
         cost_estimate=cost(8),
         name="forward",
-    )(q, k, v, halo, sf, taps, gain, *after)
+    )(q, k, v, halo, sf, table, gain, *after)
 
 
 def backward_kernel(gc, gq, vc, kc, rim, sf, taps, gain, *refs):
-    dq_o, dk_o, dv_o, gs, qs, ks, vs, table = refs[-8:]
+    outs, scratch = refs[-8:-5], refs[-5:]
+    for part in range(PARTS):
+        lanes, rows = pl.ds(part * LANES, LANES), pl.ds(part * 8, 8)
+        backward_part(
+            *[a.at[:, lanes] for a in (gc, gq, vc, kc, rim)], sf.at[:, :, lanes], taps.at[rows],
+            gain.at[:, lanes], *[a.at[:, lanes] for a in outs], *scratch,
+        )
+
+
+def backward_part(gc, gq, vc, kc, rim, sf, taps, gain, dq_o, dk_o, dv_o, gs, qs, ks, vs, table):
     n = gc.shape[0]
     gs[:n] = gc[...]
     gs[n : n + HALO] = rim[:HALO]
@@ -179,14 +212,14 @@
 
 def backward(gc, gq, vc, kc, rim, sf, taps, gain, after):
     n, ch = gc.shape
-    col = lambda rows: pl.BlockSpec((rows, LANES), lambda i: (0, i))
+    col = lambda rows: pl.BlockSpec((rows, PARTS * LANES), lambda i: (0, i))
     return pl.pallas_call(
         backward_kernel,
-        grid=(ch // LANES,),
+        grid=(ch // LANES // PARTS,),
         in_specs=[
             col(n), col(n), col(n), col(n), col(HALO + 3 * HEAD),
-            pl.BlockSpec((3, 7, LANES), lambda i: (0, 0, i)),
-            pl.BlockSpec((8, 2 * LANES), lambda i: (i, 0)),
+            pl.BlockSpec((3, 7, PARTS * LANES), lambda i: (0, 0, i)),
+            pl.BlockSpec((PARTS * 8, 2 * LANES), lambda i: (i, 0)),
             col(1),
         ]
         + any_specs(len(after)),
@@ -412,7 +445,7 @@
 
 def wave_kernel(right, left, got, *refs):
     refs[-2][...] = right[...]
-    refs[-1][...] = (left[...] + got[...].astype(F32)).astype(BF16)
+    refs[-1][...] = (left[...].astype(F32) + got[...].astype(F32)).astype(BF16)
 
 
 def wave(right, left, got, after):
@@ -497,7 +530,7 @@
     taps_fwd = jnp.concatenate([none, taps[:, ::-1], pad], axis=1)
     taps_bwd = jnp.concatenate([taps, none, pad], axis=1)
     query_conv, carried, key_conv, value_conv, gated, gated_t = forward(
-        query_in, key_in, value_in, halo, short_filter, taps_fwd, gain, [other, r1, l1]
+        query_in, key_in, value_in, halo, short_filter, toeplitz_table(taps_fwd), gain, [other, r1, l1]
     )
 
     r2, l2 = along_x(other, 1), along_x(other, -1)
@@ -515,7 +548,6 @@
     far_up, far_down = project(
         block_cols([1, 0], [2, 2]), gated, w, [BF16, BF16], after=near_gg
     )
-    got_r, got_l = along_x(far_up, 1), along_x(far_down, -1)
 
     plane = (z + jnp.array([0, 1, 3, 2])) % Z
     parity = (yl + jnp.array([0, 1])) % 2
@@ -526,10 +558,12 @@
     blocks = [own, r1, l1, other, r2, l2, r3, l3]
     splits = [(0, 384), (384, 128)]
     first = select(places, blocks, *splits[0], after=[far_up])
+    far_up, far_down, _ = lax.optimization_barrier((far_up, far_down, first[0]))
+    got_r, got_l = along_x(far_up, 1), along_x(far_down, -1)
 
     right1, left1 = project(block_cols([1, 1], [1, 3]), gated, w, [F32, BF16], after=[first[0], *left], us=6)
     right0, left0, stay0, stay1 = project(
-        block_cols([0, 0, 0, 1], [1, 3, 0, 0]), gated, w, [BF16, F32, F32, F32], after=[left1, got_r, got_l, *left], us=8
+        block_cols([0, 0, 0, 1], [1, 3, 0, 0]), gated, w, [BF16, BF16, BF16, BF16], after=[left1, got_r, got_l, *left], us=8
     )
     second = select(places, blocks, *splits[1], after=[stay1], us=0.2)
     grad_carried, grad_query_conv, rim = grad_product(
@@ -539,7 +573,7 @@
 
     from_r1 = along_x((right1.astype(F32) + got_r.astype(F32)).astype(BF16), 1)
     from_l1 = along_x(left1, -1)
-    swap = (stay1 + from_r1.astype(F32) + from_l1.astype(F32)).astype(BF16)
+    swap = (stay1.astype(F32) + from_r1.astype(F32) + from_l1.astype(F32)).astype(BF16)
     swapped = across_yh(swap)
 
     scale = float(n * Z * YL * CORE) ** -0.5
@@ -559,6 +593,8 @@
         grad_carried, grad_query_conv, value_conv, key_conv, rim,
         short_filter, taps_bwd, gain, [swapped, sent_a],
     )
+    beyond, _ = lax.optimization_barrier((second[3], sent_a))
+    second = [*second[:3], beyond]
     kept_b, given_b = weight_sum(left, over_z(*second), scale, [grad_query])
     done_a = finish(kept_a, core_a, across_yl(sent_a), 20)
     core_b = across_core(given_b)
@@ -567,7 +603,7 @@
 
     *waves, _ = lax.optimization_barrier((*waves, grad_query))
     from_r0, from_l0 = along_x(waves[0], 1), along_x(waves[1], -1)
-    output = stay0 + from_r0.astype(F32) + from_l0.astype(F32) + swapped.astype(F32)
+    output = stay0.astype(F32) + from_r0.astype(F32) + from_l0.astype(F32) + swapped.astype(F32)
     output = output.astype(BF16)
     return output, grad_query, grad_key, grad_value, weight_grad
 

time: 144 us -> 138 us (0.958)
  Pallas kernels: 63.2 us -> 60 us
  waiting for transfers between devices: 20.4 us -> 18.5 us
    ppermute x2, waiting for transfers between devices: 6.67 us -> 3.6 us  [across_yh(): return lax.ppermute(a, 'tp', tp_pairs(lambda yh, x: (yh + 1, x)))]
    ppermute x2, waiting for transfers between devices: 8.26 us -> 10.6 us  [across_yl(): return lax.ppermute(a, 'ctx', ctx_pairs(lambda z, yl, c: (z, yl + 1, c)))]
    pallas_call x3, Pallas kernels: 16.9 us -> 14.8 us  [project(): pl.pallas_call(functools.partial(project_kernel, n), grid_spec=pltpu.Pref...]
    pallas_call x2 -> x3, Pallas kernels: 14.6 us -> 13.6 us  [the longest x1 6.33 us: forward(): pl.pallas_call(forward_kernel, grid=(ch // LANES // PARTS,), in_specs=[co...]
    unnamed x80 -> x84, local copies, waits for them, and re-layouts: 6.51 us -> 6.35 us
where the time goes in v4:
time: 138 us; the launch traced here: 137 us
  Pallas kernels  60 us (43%)
  starting transfers between devices  44.8 us (32%)
  waiting for transfers between devices  18.5 us (13%)
  local copies, waits for them, and re-layouts  7.23 us (5%)
  other arithmetic  5.31 us (4%)
  between operations  1.39 us (1%)
    ppermute x12, starting transfers between devices, along_x(): return lax.ppermute(a, 'tp', tp_pairs(lambda yh, x: (yh, x + d)))  18.2 us
    ppermute x9, starting transfers between devices, along_z(): return lax.ppermute(a, 'ctx', ctx_pairs(lambda z, yl, c: (z + d, yl, c)))  15.5 us
    pallas_call x3, Pallas kernels, project(): pl.pallas_call(functools.partial(project_kernel, n), grid_spec=pltpu.Pref...  14.8 us
    pallas_call x2, Pallas kernels, grad_product(): pl.pallas_call(functools.partial(grad_kernel, n, bool(rest)), grid_spec=p...  14.5 us
    ppermute x2, waiting for transfers between devices, across_yl(): return lax.ppermute(a, 'ctx', ctx_pairs(lambda z, yl, c: (z, yl + 1, c)))  10.6 us
    unnamed x84, local copies, waits for them, and re-layouts  6.35 us
    pallas_call x1, Pallas kernels, forward(): pl.pallas_call(forward_kernel, grid=(ch // LANES // PARTS,), in_specs=[co...  6.33 us
    pallas_call x2, Pallas kernels, weight_sum(): pl.pallas_call(functools.partial(weight_kernel, scale), grid=(ch // tile,...  6.1 us
  transfers between devices with their start and end apart: 29, of which 5 were waited for; matrix products, arithmetic and copies ran while one was open for 5% of the time, Pallas kernels for 43%

profile of v4, /device:TPU:0, one launch (start us, length us, event | category | flops | bytes accessed | tf_op | source)
XLA Modules:
  0.0 137.2 jit_solution(9967792721823045444)
XLA Ops:
  0.7 2.9 %collective-permute-start.3 = (bf16[256,1024]{1,0:T(8,128)(2,1)}, bf16[256,1024]{1,0:T(8,128)(2,1)S(1)}, u32[]{:S(2)}, u32[]{:S(2)}) collective-permute-start(bf16[256,1024]{1,0:T(8,128)(2,1)} %refs_0_.5), channel_id=1, source_target_pairs={{0,3},{1,0},{2,1},{3,2},{4,7},{5,4},{6,5},{7,6},{8,11},{9,8},{10,9... | collective-permute-start | bytes 1572872 | tf_op jit(solution)/shard_map/ppermute | solution.py:42
  3.6 3.2 %collective-permute-start.1 = (bf16[256,1024]{1,0:T(8,128)(2,1)}, bf16[256,1024]{1,0:T(8,128)(2,1)S(1)}, u32[]{:S(2)}, u32[]{:S(2)}) collective-permute-start(bf16[256,1024]{1,0:T(8,128)(2,1)} %refs_0_.5), channel_id=1, source_target_pairs={{0,4},{1,5},{2,6},{3,7},{4,0},{5,1},{6,2},{7,3},{8,12},{9,13},{10,... | collective-permute-start | bytes 1572872 | tf_op jit(solution)/shard_map/ppermute | solution.py:46
  6.8 3.1 %last_rows.1 = bf16[176,1024]{1,0:T(8,128)(2,1)} custom-call(bf16[256,1024]{1,0:T(8,128)(2,1)} %q.3, bf16[256,1024]{1,0:T(8,128)(2,1)} %k.3, bf16[256,1024]{1,0:T(8,128)(2,1)} %k.3, bf16[256,1024]{1,0:T(8,128)(2,1)} %v.3, bf16[256,1024]{1,0:T(8,128)(2,1)} %v.3, f32[3,7,1024]{2,1,0:T(8,128)} %sf.5), custom_call_target="tpu_custom_call" | custom-call | flops 4600000000 | bytes 65536 | tf_op jit(solution)/shard_map/last_rows/pallas_call | solution.py:432
  11.7 1.7 %toeplitz_table.1.table = bf16[8192,256]{1,0:T(8,128)(2,1)S(1)} custom-call(f32[64,256]{1,0:T(8,128)S(1)} %get-tuple-element.100.taps), custom_call_target="tpu_custom_call" | custom-call | flops 27599998976 | bytes 65536 | tf_op jit(solution)/shard_map/toeplitz_table/pallas_call | solution.py:92
  13.5 2.0 %copy-done.26 = bf16[8192,256]{1,0:T(8,128)(2,1)} copy-done((bf16[8192,256]{1,0:T(8,128)(2,1)}, bf16[8192,256]{1,0:T(8,128)(2,1)S(1)}, u32[]{:S(2)}) %copy-start.26) | copy-done | bytes 4194328
  16.5 3.6 %collective-permute-done.1.refs_0_.refs_3_.refs_2_ = bf16[256,1024]{1,0:T(8,128)(2,1)S(1)} collective-permute-done((bf16[256,1024]{1,0:T(8,128)(2,1)}, bf16[256,1024]{1,0:T(8,128)(2,1)S(1)}, u32[]{:S(2)}, u32[]{:S(2)}) %collective-permute-start.1) | collective-permute-done | bytes 524320 | tf_op jit(solution)/shard_map/ppermute | solution.py:46
  20.1 3.2 %collective-permute-start.5 = (bf16[256,1024]{1,0:T(8,128)(2,1)S(1)}, bf16[256,1024]{1,0:T(8,128)(2,1)S(1)}, u32[]{:S(2)}, u32[]{:S(2)}) collective-permute-start(bf16[256,1024]{1,0:T(8,128)(2,1)S(1)} %collective-permute-done.1.refs_0_.refs_3_.refs_2_), channel_id=1, source_target_pairs={{0,3},{1,0},{2,1},{3,2},{4,7},{5,4},{6,5},{7,6},{8,11},{9,8},{10,9... | collective-permute-start | bytes 1572872 | tf_op jit(solution)/shard_map/ppermute | solution.py:42
  24.5 6.3 %forward.1 = (f32[256,1024]{1,0:T(8,128)}, f32[256,1024]{1,0:T(8,128)}, f32[256,1024]{1,0:T(8,128)}, f32[256,1024]{1,0:T(8,128)}, bf16[256,1024]{1,0:T(8,128)(2,1)}, /*index=5*/bf16[1024,256]{1,0:T(8,128)(2,1)}) custom-call(bf16[256,1024]{1,0:T(8,128)(2,1)} %q.3, bf16[256,1024]{1,0:T(8,128)(2,1)} %k.3, bf16[256,1024]{1,0:T(8,128)(2,1)} %v.3, ...), custom_call_target="tpu_custom_call" | custom-call | flops 36800000000 | bytes 65536 | tf_op jit(solution)/shard_map/forward/pallas_call | solution.py:149
  30.8 4.0 %collective-permute-start.10 = (bf16[1024,256]{1,0:T(8,128)(2,1)}, bf16[1024,256]{1,0:T(8,128)(2,1)S(1)}, u32[]{:S(2)}, u32[]{:S(2)}) collective-permute-start(bf16[1024,256]{1,0:T(8,128)(2,1)} %get-tuple-element.54.refs_1_.refs_3_.q0), channel_id=1, source_target_pairs={{0,64},{8,72},{16,80},{24,88},{32,96},{40,104},{48,112},{56,120},{... | collective-permute-start | bytes 1572872 | tf_op jit(solution)/shard_map/ppermute | solution.py:50
  36.8 3.3 %collective-permute-start.7 = (bf16[256,1024]{1,0:T(8,128)(2,1)S(1)}, bf16[256,1024]{1,0:T(8,128)(2,1)S(1)}, u32[]{:S(2)}, u32[]{:S(2)}) collective-permute-start(bf16[256,1024]{1,0:T(8,128)(2,1)S(1)} %collective-permute-done.5.refs_3_.refs_5_), channel_id=1, source_target_pairs={{0,3},{1,0},{2,1},{3,2},{4,7},{5,4},{6,5},{7,6},{8,11},{9,8},{10,9... | collective-permute-start | bytes 1572872 | tf_op jit(solution)/shard_map/ppermute | solution.py:42
  42.2 6.2 %grad_product.2.refs_0_.refs_5_ = f32[256,1024]{1,0:T(8,128)S(1)} custom-call(s32[4]{0:T(128)S(1)} %fusion.3.cols, bf16[256,1024]{1,0:T(8,128)(2,1)S(1)} %copy-done.18, bf16[256,1024]{1,0:T(8,128)(2,1)S(1)} %copy-done.15, bf16[256,1024]{1,0:T(8,128)(2,1)S(1)} %collective-permute-done.4.refs_2_.refs_4_, ...), custom_call_target="tpu_custom_call" | custom-call | flops 29440000000 | bytes 65536 | tf_op jit(solution)/shard_map/grad_product/pallas_call | solution.py:295
  48.4 4.0 %project.3 = (bf16[256,1024]{1,0:T(8,128)(2,1)S(1)}, bf16[256,1024]{1,0:T(8,128)(2,1)S(1)}) custom-call(s32[2]{0:T(128)S(1)} %fusion.13.cols, bf16[256,1024]{1,0:T(8,128)(2,1)S(1)} %copy-done.27, bf16[1024,8192]{1,0:T(8,128)(2,1)} %refs_4_.3, f32[256,1024]{1,0:T(8,128)S(1)} %grad_product.2.refs_0_.refs_5_), custom_call_target="tpu_custom_call" | custom-call | flops 14720000000 | bytes 65536 | tf_op jit(solution)/shard_map/project/pallas_call | solution.py:328
  52.5 3.3 %select.66 = (bf16[256,1536]{1,0:T(8,128)(2,1)S(1)}, bf16[256,1536]{1,0:T(8,128)(2,1)}, bf16[256,1536]{1,0:T(8,128)(2,1)S(1)}, bf16[256,1536]{1,0:T(8,128)(2,1)S(1)}) custom-call(s32[9]{0:T(128)S(1)} %pad_add_fusion.places, bf16[256,1024]{1,0:T(8,128)(2,1)S(1)} %copy-done.8, bf16[256,1024]{1,0:T(8,128)(2,1)S(1)} %copy-done.19, ...), custom_call_target="tpu_custom_call" | custom-call | flops 11500000256 | bytes 65536 | tf_op jit(solution)/shard_map/select/pallas_call | solution.py:367
  55.8 3.2 %collective-permute-start.12 = (bf16[256,1024]{1,0:T(8,128)(2,1)S(1)}, bf16[256,1024]{1,0:T(8,128)(2,1)S(1)}, u32[]{:S(2)}, u32[]{:S(2)}) collective-permute-start(bf16[256,1024]{1,0:T(8,128)(2,1)S(1)} %get-tuple-element.58), channel_id=1, source_target_pairs={{0,3},{1,0},{2,1},{3,2},{4,7},{5,4},{6,5},{7,6},{8,11},{9,8},{10,9... | collective-permute-start | bytes 1572872 | tf_op jit(solution)/shard_map/ppermute | solution.py:42
  60.1 2.2 %collective-permute-start.14 = (bf16[256,1536]{1,0:T(8,128)(2,1)S(1)}, bf16[256,1536]{1,0:T(8,128)(2,1)S(1)}, u32[]{:S(2)}, u32[]{:S(2)}) collective-permute-start(bf16[256,1536]{1,0:T(8,128)(2,1)S(1)} %get-tuple-element.63), channel_id=1, source_target_pairs={{0,96},{8,104},{16,112},{24,120},{32,0},{40,8},{48,16},{56,24},{64... | collective-permute-start | bytes 2359304 | tf_op jit(solution)/shard_map/ppermute | solution.py:50
  62.4 1.8 %collective-permute-start.15 = (bf16[256,1536]{1,0:T(8,128)(2,1)S(1)}, bf16[256,1536]{1,0:T(8,128)(2,1)S(1)}, u32[]{:S(2)}, u32[]{:S(2)}) collective-permute-start(bf16[256,1536]{1,0:T(8,128)(2,1)S(1)} %get-tuple-element.64), channel_id=1, source_target_pairs={{0,64},{8,72},{16,80},{24,88},{32,96},{40,104},{48,112},{56,120},{... | collective-permute-start | bytes 2359304 | tf_op jit(solution)/shard_map/ppermute | solution.py:50
  64.1 4.7 %project.4 = (f32[256,1024]{1,0:T(8,128)}, bf16[256,1024]{1,0:T(8,128)(2,1)S(1)}) custom-call(s32[2]{0:T(128)S(1)} %fusion.9.cols, bf16[256,1024]{1,0:T(8,128)(2,1)S(1)} %copy-done.27, bf16[1024,8192]{1,0:T(8,128)(2,1)} %refs_4_.3, bf16[256,1536]{1,0:T(8,128)(2,1)S(1)} %get-tuple-element.53.refs_0_.g0, bf16[1024,256]{1,0:T(8,128)(2,1)S(1)} %copy-done, ...), custom_call_target="tpu_custom_call" | custom-call | flops 27599998976 | bytes 65536 | tf_op jit(solution)/shard_map/project/pallas_call | solution.py:328
  69.0 2.2 %add_convert_fusion.2 = bf16[256,1024]{1,0:T(8,128)(2,1)} fusion(f32[256,1024]{1,0:T(8,128)} %get-tuple-element.72, bf16[256,1024]{1,0:T(8,128)(2,1)S(1)} %collective-permute-done.11.refs_1_), kind=kLoop, calls=%fused_computation.3 | loop fusion | flops 786432 | bytes 2097152 | tf_op jit(solution)/shard_map/convert_element_type | solution.py:574
  71.2 2.0 %collective-permute-start.16 = (bf16[256,1024]{1,0:T(8,128)(2,1)}, bf16[256,1024]{1,0:T(8,128)(2,1)}, u32[]{:S(2)}, u32[]{:S(2)}) collective-permute-start(bf16[256,1024]{1,0:T(8,128)(2,1)} %add_convert_fusion.2), channel_id=1, source_target_pairs={{0,1},{1,2},{2,3},{3,0},{4,5},{5,6},{6,7},{7,4},{8,9},{9,10},{10,1... | collective-permute-start | bytes 1572872 | tf_op jit(solution)/shard_map/ppermute | solution.py:42
  73.2 6.2 %project.5 = (bf16[256,1024]{1,0:T(8,128)(2,1)S(1)}, bf16[256,1024]{1,0:T(8,128)(2,1)S(1)}, bf16[256,1024]{1,0:T(8,128)(2,1)S(1)}, bf16[256,1024]{1,0:T(8,128)(2,1)S(1)}) custom-call(s32[4]{0:T(128)S(1)} %fusion.2.cols, bf16[256,1024]{1,0:T(8,128)(2,1)S(1)} %copy-done.28, bf16[1024,8192]{1,0:T(8,128)(2,1)} %refs_4_.3, ...), custom_call_target="tpu_custom_call" | custom-call | flops 36800000000 | bytes 65536 | tf_op jit(solution)/shard_map/project/pallas_call | solution.py:328
  79.4 2.0 %select.67 = (bf16[256,512]{1,0:T(8,128)(2,1)S(1)}, bf16[256,512]{1,0:T(8,128)(2,1)S(1)}, bf16[256,512]{1,0:T(8,128)(2,1)S(1)}, bf16[256,512]{1,0:T(8,128)(2,1)S(1)}) custom-call(s32[9]{0:T(128)S(1)} %pad_add_fusion.places, bf16[256,1024]{1,0:T(8,128)(2,1)S(1)} %copy-done.8, bf16[256,1024]{1,0:T(8,128)(2,1)S(1)} %copy-done.19, ...), custom_call_target="tpu_custom_call" | custom-call | flops 920000000 | bytes 65536 | tf_op jit(solution)/shard_map/select/pallas_call | solution.py:367
  81.5 8.3 %grad_product.3 = (bf16[256,1024]{1,0:T(8,128)(2,1)S(1)}, f32[256,1024]{1,0:T(8,128)}, bf16[192,1024]{1,0:T(8,128)(2,1)S(1)}) custom-call(s32[4]{0:T(128)S(1)} %get-tuple-element.95.cols, bf16[256,1024]{1,0:T(8,128)(2,1)S(1)} %copy-done.8, bf16[256,1024]{1,0:T(8,128)(2,1)S(1)} %collective-permute-done.6.refs_6_.refs_1_, bf16[256,1024]{1,0:T(8,128)(2,1)S(1)} %copy-done.10, ...), custom_call_target="tpu_custom_call" | custom-call | flops 920000000 | bytes 65536 | tf_op jit(solution)/shard_map/grad_product/pallas_call | solution.py:295
  89.8 1.6 %add_convert_fusion.1.refs_1_ = bf16[256,1024]{1,0:T(8,128)(2,1)S(1)} fusion(bf16[256,1024]{1,0:T(8,128)(2,1)} %collective-permute-done.17, bf16[256,1024]{1,0:T(8,128)(2,1)} %collective-permute-done.16, bf16[256,1024]{1,0:T(8,128)(2,1)S(1)} %get-tuple-element.69.refs_8_), kind=kLoop, calls=%fused_computation.2 | loop fusion | flops 1572864 | bytes 2097152 | tf_op jit(solution)/shard_map/convert_element_type | solution.py:576
  91.5 2.5 %collective-permute-start.19 = (bf16[256,1024]{1,0:T(8,128)(2,1)S(1)}, bf16[256,1024]{1,0:T(8,128)(2,1)S(1)}, u32[]{:S(2)}, u32[]{:S(2)}) collective-permute-start(bf16[256,1024]{1,0:T(8,128)(2,1)S(1)} %add_convert_fusion.1.refs_1_), channel_id=1, source_target_pairs={{0,4},{1,5},{2,6},{3,7},{4,0},{5,1},{6,2},{7,3},{8,12},{9,13},{10,... | collective-permute-start | bytes 1572872 | tf_op jit(solution)/shard_map/ppermute | solution.py:46
  95.0 2.2 %collective-permute-start.24 = (bf16[256,512]{1,0:T(8,128)(2,1)S(1)}, bf16[256,512]{1,0:T(8,128)(2,1)S(1)}, u32[]{:S(2)}, u32[]{:S(2)}) collective-permute-start(bf16[256,512]{1,0:T(8,128)(2,1)S(1)} %get-tuple-element.90), channel_id=1, source_target_pairs={{0,96},{8,104},{16,112},{24,120},{32,0},{40,8},{48,16},{56,24},{64... | collective-permute-start | bytes 786440 | tf_op jit(solution)/shard_map/ppermute | solution.py:50
  98.6 4.2 %weight_sum.2 = (bf16[2,1024,384]{2,1,0:T(8,128)(2,1)S(1)}, bf16[2,1024,384]{2,1,0:T(8,128)(2,1)S(1)}) custom-call(bf16[1024,256]{1,0:T(8,128)(2,1)S(1)} %copy-done.1, bf16[1024,256]{1,0:T(8,128)(2,1)S(1)} %copy-done.7, bf16[1024,256]{1,0:T(8,128)(2,1)S(1)} %copy-done.5, bf16[1024,256]{1,0:T(8,128)(2,1)S(1)} %copy-done.3, ...), custom_call_target="tpu_custom_call" | custom-call | flops 920000000 | bytes 65536 | tf_op jit(solution)/shard_map/weight_sum/pallas_call | solution.py:398
  104.2 2.8 %collective-permute-done.20.from_core = bf16[2,1024,384]{2,1,0:T(8,128)(2,1)S(1)} collective-permute-done((bf16[2,1024,384]{2,1,0:T(8,128)(2,1)S(1)}, bf16[2,1024,384]{2,1,0:T(8,128)(2,1)S(1)}, u32[]{:S(2)}, u32[]{:S(2)}) %collective-permute-start.20) | collective-permute-done | bytes 1572896 | tf_op jit(solution)/shard_map/ppermute | solution.py:54
  109.4 5.6 %backward.1 = (bf16[256,1024]{1,0:T(8,128)(2,1)}, bf16[256,1024]{1,0:T(8,128)(2,1)}, bf16[256,1024]{1,0:T(8,128)(2,1)}) custom-call(bf16[256,1024]{1,0:T(8,128)(2,1)S(1)} %get-tuple-element.71.refs_0_.gc, f32[256,1024]{1,0:T(8,128)S(1)} %copy-done.21, f32[256,1024]{1,0:T(8,128)S(1)} %copy-done.12, f32[256,1024]{1,0:T(8,128)S(1)} %copy-done.11, ...), custom_call_target="tpu_custom_call" | custom-call | flops 36800000000 | bytes 65536 | tf_op jit(solution)/shard_map/backward/pallas_call | solution.py:216
  115.7 2.5 %collective-permute-start.22 = (bf16[256,1024]{1,0:T(8,128)(2,1)S(1)}, bf16[256,1024]{1,0:T(8,128)(2,1)S(1)}, u32[]{:S(2)}, u32[]{:S(2)}) collective-permute-start(bf16[256,1024]{1,0:T(8,128)(2,1)S(1)} %get-tuple-element.82), channel_id=1, source_target_pairs={{0,3},{1,0},{2,1},{3,2},{4,7},{5,4},{6,5},{7,6},{8,11},{9,8},{10,9... | collective-permute-start | bytes 1572872 | tf_op jit(solution)/shard_map/ppermute | solution.py:42
  119.3 1.9 %weight_sum.3 = (bf16[2,1024,128]{2,1,0:T(8,128)(2,1)S(1)}, bf16[2,1024,128]{2,1,0:T(8,128)(2,1)S(1)}) custom-call(bf16[1024,256]{1,0:T(8,128)(2,1)S(1)} %copy-done.1, bf16[1024,256]{1,0:T(8,128)(2,1)S(1)} %copy-done.7, bf16[1024,256]{1,0:T(8,128)(2,1)S(1)} %copy-done.5, bf16[1024,256]{1,0:T(8,128)(2,1)S(1)} %copy-done.3, ...), custom_call_target="tpu_custom_call" | custom-call | flops 920000000 | bytes 65536 | tf_op jit(solution)/shard_map/weight_sum/pallas_call | solution.py:398
  121.3 6.0 %collective-permute-done.27.from_yl = bf16[1024,384]{1,0:T(8,128)(2,1)S(1)} collective-permute-done((bf16[1024,384]{1,0:T(8,128)(2,1)S(1)}, bf16[1024,384]{1,0:T(8,128)(2,1)S(1)}, u32[]{:S(2)}, u32[]{:S(2)}) %collective-permute-start.27) | collective-permute-done | bytes 786464 | tf_op jit(solution)/shard_map/ppermute | solution.py:63
  131.1 4.6 %collective-permute-done.28.from_yl = bf16[1024,128]{1,0:T(8,128)(2,1)S(1)} collective-permute-done((bf16[1024,128]{1,0:T(8,128)(2,1)S(1)}, bf16[1024,128]{1,0:T(8,128)(2,1)S(1)}, u32[]{:S(2)}, u32[]{:S(2)}) %collective-permute-start.28) | collective-permute-done | bytes 262176 | tf_op jit(solution)/shard_map/ppermute | solution.py:63
  (150 shorter events, 22.4 us)
Async XLA Ops:
  0.6 10.7 %copy-start.35 = (s32[4]{0:T(128)S(1)}, s32[4]{0:T(128)}, u32[]{:S(2)}) copy-start(s32[4]{0:T(128)} %constant.193.clone) | copy-start | bytes 52
  0.6 10.7 %copy-start.32 = (bf16[128,64]{0,1:T(8,128)(2,1)S(1)}, bf16[128,64]{0,1:T(8,128)(2,1)}, u32[]{:S(2)}) copy-start(bf16[128,64]{0,1:T(8,128)(2,1)} %param.25) | copy-start | bytes 49156
  0.7 22.7 %collective-permute-start.3 = (bf16[256,1024]{1,0:T(8,128)(2,1)}, bf16[256,1024]{1,0:T(8,128)(2,1)S(1)}, u32[]{:S(2)}, u32[]{:S(2)}) collective-permute-start(bf16[256,1024]{1,0:T(8,128)(2,1)} %refs_0_.5), channel_id=1, source_target_pairs={{0,3},{1,0},{2,1},{3,2},{4,7},{5,4},{6,5},{7,6},{8,11},{9,8},{10,9... | collective-permute-start | bytes 1572872 | tf_op jit(solution)/shard_map/ppermute | solution.py:42
  3.6 19.9 %collective-permute-start.2 = (bf16[256,1024]{1,0:T(8,128)(2,1)}, bf16[256,1024]{1,0:T(8,128)(2,1)S(1)}, u32[]{:S(2)}, u32[]{:S(2)}) collective-permute-start(bf16[256,1024]{1,0:T(8,128)(2,1)} %refs_0_.5), channel_id=1, source_target_pairs={{0,1},{1,2},{2,3},{3,0},{4,5},{5,6},{6,7},{7,4},{8,9},{9,10},{10,1... | collective-permute-start | bytes 1572872 | tf_op jit(solution)/shard_map/ppermute | solution.py:42
  3.6 16.6 %collective-permute-start.1 = (bf16[256,1024]{1,0:T(8,128)(2,1)}, bf16[256,1024]{1,0:T(8,128)(2,1)S(1)}, u32[]{:S(2)}, u32[]{:S(2)}) collective-permute-start(bf16[256,1024]{1,0:T(8,128)(2,1)} %refs_0_.5), channel_id=1, source_target_pairs={{0,4},{1,5},{2,6},{3,7},{4,0},{5,1},{6,2},{7,3},{8,12},{9,13},{10,... | collective-permute-start | bytes 1572872 | tf_op jit(solution)/shard_map/ppermute | solution.py:46
  9.9 13.5 %collective-permute-start = (bf16[176,1024]{1,0:T(8,128)(2,1)}, bf16[176,1024]{1,0:T(8,128)(2,1)S(1)}, u32[]{:S(2)}, u32[]{:S(2)}) collective-permute-start(bf16[176,1024]{1,0:T(8,128)(2,1)} %last_rows.1), channel_id=1, source_target_pairs={{0,8},{8,16},{16,24},{24,32},{32,40},{40,48},{48,56},{56,64},{64,7... | collective-permute-start | bytes 1081352 | tf_op jit(solution)/shard_map/ppermute | solution.py:59
  20.1 16.7 %collective-permute-start.5 = (bf16[256,1024]{1,0:T(8,128)(2,1)S(1)}, bf16[256,1024]{1,0:T(8,128)(2,1)S(1)}, u32[]{:S(2)}, u32[]{:S(2)}) collective-permute-start(bf16[256,1024]{1,0:T(8,128)(2,1)S(1)} %collective-permute-done.1.refs_0_.refs_3_.refs_2_), channel_id=1, source_target_pairs={{0,3},{1,0},{2,1},{3,2},{4,7},{5,4},{6,5},{7,6},{8,11},{9,8},{10,9... | collective-permute-start | bytes 1572872 | tf_op jit(solution)/shard_map/ppermute | solution.py:42
  23.4 13.4 %collective-permute-start.4 = (bf16[256,1024]{1,0:T(8,128)(2,1)S(1)}, bf16[256,1024]{1,0:T(8,128)(2,1)S(1)}, u32[]{:S(2)}, u32[]{:S(2)}) collective-permute-start(bf16[256,1024]{1,0:T(8,128)(2,1)S(1)} %collective-permute-done.1.refs_0_.refs_3_.refs_2_), channel_id=1, source_target_pairs={{0,1},{1,2},{2,3},{3,0},{4,5},{5,6},{6,7},{7,4},{8,9},{9,10},{10,1... | collective-permute-start | bytes 1572872 | tf_op jit(solution)/shard_map/ppermute | solution.py:42
  30.8 28.3 %collective-permute-start.10 = (bf16[1024,256]{1,0:T(8,128)(2,1)}, bf16[1024,256]{1,0:T(8,128)(2,1)S(1)}, u32[]{:S(2)}, u32[]{:S(2)}) collective-permute-start(bf16[1024,256]{1,0:T(8,128)(2,1)} %get-tuple-element.54.refs_1_.refs_3_.q0), channel_id=1, source_target_pairs={{0,64},{8,72},{16,80},{24,88},{32,96},{40,104},{48,112},{56,120},{... | collective-permute-start | bytes 1572872 | tf_op jit(solution)/shard_map/ppermute | solution.py:50
  34.8 25.4 %collective-permute-start.9 = (bf16[1024,256]{1,0:T(8,128)(2,1)}, bf16[1024,256]{1,0:T(8,128)(2,1)S(1)}, u32[]{:S(2)}, u32[]{:S(2)}) collective-permute-start(bf16[1024,256]{1,0:T(8,128)(2,1)} %get-tuple-element.54.refs_1_.refs_3_.q0), channel_id=1, source_target_pairs={{0,96},{8,104},{16,112},{24,120},{32,0},{40,8},{48,16},{56,24},{64... | collective-permute-start | bytes 1572872 | tf_op jit(solution)/shard_map/ppermute | solution.py:50
  35.5 26.9 %collective-permute-start.8 = (bf16[1024,256]{1,0:T(8,128)(2,1)}, bf16[1024,256]{1,0:T(8,128)(2,1)S(1)}, u32[]{:S(2)}, u32[]{:S(2)}) collective-permute-start(bf16[1024,256]{1,0:T(8,128)(2,1)} %get-tuple-element.54.refs_1_.refs_3_.q0), channel_id=1, source_target_pairs={{0,32},{8,40},{16,48},{24,56},{32,64},{40,72},{48,80},{56,88},{64,... | collective-permute-start | bytes 1572872 | tf_op jit(solution)/shard_map/ppermute | solution.py:50
  36.8 15.6 %collective-permute-start.6 = (bf16[256,1024]{1,0:T(8,128)(2,1)}, bf16[256,1024]{1,0:T(8,128)(2,1)S(1)}, u32[]{:S(2)}, u32[]{:S(2)}) collective-permute-start(bf16[256,1024]{1,0:T(8,128)(2,1)} %copy-done.17), channel_id=1, source_target_pairs={{0,1},{1,2},{2,3},{3,0},{4,5},{5,6},{6,7},{7,4},{8,9},{9,10},{10,1... | collective-permute-start | bytes 1572872 | tf_op jit(solution)/shard_map/ppermute | solution.py:42
  36.8 15.6 %collective-permute-start.7 = (bf16[256,1024]{1,0:T(8,128)(2,1)S(1)}, bf16[256,1024]{1,0:T(8,128)(2,1)S(1)}, u32[]{:S(2)}, u32[]{:S(2)}) collective-permute-start(bf16[256,1024]{1,0:T(8,128)(2,1)S(1)} %collective-permute-done.5.refs_3_.refs_5_), channel_id=1, source_target_pairs={{0,3},{1,0},{2,1},{3,2},{4,7},{5,4},{6,5},{7,6},{8,11},{9,8},{10,9... | collective-permute-start | bytes 1572872 | tf_op jit(solution)/shard_map/ppermute | solution.py:42
  52.5 11.7 %copy-start = (bf16[1024,256]{1,0:T(8,128)(2,1)S(1)}, bf16[1024,256]{1,0:T(8,128)(2,1)}, u32[]{:S(2)}) copy-start(bf16[1024,256]{1,0:T(8,128)(2,1)} %get-tuple-element.54.refs_1_.refs_3_.q0) | copy-start | bytes 1572868
  55.8 13.1 %collective-permute-start.11 = (bf16[256,1024]{1,0:T(8,128)(2,1)S(1)}, bf16[256,1024]{1,0:T(8,128)(2,1)S(1)}, u32[]{:S(2)}, u32[]{:S(2)}) collective-permute-start(bf16[256,1024]{1,0:T(8,128)(2,1)S(1)} %get-tuple-element.57.refs_8_), channel_id=1, source_target_pairs={{0,1},{1,2},{2,3},{3,0},{4,5},{5,6},{6,7},{7,4},{8,9},{9,10},{10,1... | collective-permute-start | bytes 1572872 | tf_op jit(solution)/shard_map/ppermute | solution.py:42
  55.8 15.3 %collective-permute-start.12 = (bf16[256,1024]{1,0:T(8,128)(2,1)S(1)}, bf16[256,1024]{1,0:T(8,128)(2,1)S(1)}, u32[]{:S(2)}, u32[]{:S(2)}) collective-permute-start(bf16[256,1024]{1,0:T(8,128)(2,1)S(1)} %get-tuple-element.58), channel_id=1, source_target_pairs={{0,3},{1,0},{2,1},{3,2},{4,7},{5,4},{6,5},{7,6},{8,11},{9,8},{10,9... | collective-permute-start | bytes 1572872 | tf_op jit(solution)/shard_map/ppermute | solution.py:42
  59.1 35.9 %collective-permute-start.13 = (bf16[256,1536]{1,0:T(8,128)(2,1)}, bf16[256,1536]{1,0:T(8,128)(2,1)S(1)}, u32[]{:S(2)}, u32[]{:S(2)}) collective-permute-start(bf16[256,1536]{1,0:T(8,128)(2,1)} %get-tuple-element.62), channel_id=1, source_target_pairs={{0,32},{8,40},{16,48},{24,56},{32,64},{40,72},{48,80},{56,88},{64,... | collective-permute-start | bytes 2359304 | tf_op jit(solution)/shard_map/ppermute | solution.py:50
  60.1 37.1 %collective-permute-start.14 = (bf16[256,1536]{1,0:T(8,128)(2,1)S(1)}, bf16[256,1536]{1,0:T(8,128)(2,1)S(1)}, u32[]{:S(2)}, u32[]{:S(2)}) collective-permute-start(bf16[256,1536]{1,0:T(8,128)(2,1)S(1)} %get-tuple-element.63), channel_id=1, source_target_pairs={{0,96},{8,104},{16,112},{24,120},{32,0},{40,8},{48,16},{56,24},{64... | collective-permute-start | bytes 2359304 | tf_op jit(solution)/shard_map/ppermute | solution.py:50
  62.4 36.1 %collective-permute-start.15 = (bf16[256,1536]{1,0:T(8,128)(2,1)S(1)}, bf16[256,1536]{1,0:T(8,128)(2,1)S(1)}, u32[]{:S(2)}, u32[]{:S(2)}) collective-permute-start(bf16[256,1536]{1,0:T(8,128)(2,1)S(1)} %get-tuple-element.64), channel_id=1, source_target_pairs={{0,64},{8,72},{16,80},{24,88},{32,96},{40,104},{48,112},{56,120},{... | collective-permute-start | bytes 2359304 | tf_op jit(solution)/shard_map/ppermute | solution.py:50
  68.8 21.0 %collective-permute-start.17 = (bf16[256,1024]{1,0:T(8,128)(2,1)S(1)}, bf16[256,1024]{1,0:T(8,128)(2,1)}, u32[]{:S(2)}, u32[]{:S(2)}) collective-permute-start(bf16[256,1024]{1,0:T(8,128)(2,1)S(1)} %get-tuple-element.55.refs_0_), channel_id=1, source_target_pairs={{0,3},{1,0},{2,1},{3,2},{4,7},{5,4},{6,5},{7,6},{8,11},{9,8},{10,9... | collective-permute-start | bytes 1572872 | tf_op jit(solution)/shard_map/ppermute | solution.py:42
  71.2 18.7 %collective-permute-start.16 = (bf16[256,1024]{1,0:T(8,128)(2,1)}, bf16[256,1024]{1,0:T(8,128)(2,1)}, u32[]{:S(2)}, u32[]{:S(2)}) collective-permute-start(bf16[256,1024]{1,0:T(8,128)(2,1)} %add_convert_fusion.2), channel_id=1, source_target_pairs={{0,1},{1,2},{2,3},{3,0},{4,5},{5,6},{6,7},{7,4},{8,9},{9,10},{10,1... | collective-permute-start | bytes 1572872 | tf_op jit(solution)/shard_map/ppermute | solution.py:42
  91.5 17.9 %collective-permute-start.19 = (bf16[256,1024]{1,0:T(8,128)(2,1)S(1)}, bf16[256,1024]{1,0:T(8,128)(2,1)S(1)}, u32[]{:S(2)}, u32[]{:S(2)}) collective-permute-start(bf16[256,1024]{1,0:T(8,128)(2,1)S(1)} %add_convert_fusion.1.refs_1_), channel_id=1, source_target_pairs={{0,4},{1,5},{2,6},{3,7},{4,0},{5,1},{6,2},{7,3},{8,12},{9,13},{10,... | collective-permute-start | bytes 1572872 | tf_op jit(solution)/shard_map/ppermute | solution.py:46
  94.0 21.8 %collective-permute-start.23 = (bf16[256,512]{1,0:T(8,128)(2,1)S(1)}, bf16[256,512]{1,0:T(8,128)(2,1)S(1)}, u32[]{:S(2)}, u32[]{:S(2)}) collective-permute-start(bf16[256,512]{1,0:T(8,128)(2,1)S(1)} %get-tuple-element.89), channel_id=1, source_target_pairs={{0,32},{8,40},{16,48},{24,56},{32,64},{40,72},{48,80},{56,88},{64,... | collective-permute-start | bytes 786440 | tf_op jit(solution)/shard_map/ppermute | solution.py:50
  95.0 23.3 %collective-permute-start.24 = (bf16[256,512]{1,0:T(8,128)(2,1)S(1)}, bf16[256,512]{1,0:T(8,128)(2,1)S(1)}, u32[]{:S(2)}, u32[]{:S(2)}) collective-permute-start(bf16[256,512]{1,0:T(8,128)(2,1)S(1)} %get-tuple-element.90), channel_id=1, source_target_pairs={{0,96},{8,104},{16,112},{24,120},{32,0},{40,8},{48,16},{56,24},{64... | collective-permute-start | bytes 786440 | tf_op jit(solution)/shard_map/ppermute | solution.py:50
  97.2 10.9 %collective-permute-start.18 = (bf16[192,1024]{1,0:T(8,128)(2,1)S(1)}, bf16[192,1024]{1,0:T(8,128)(2,1)S(1)}, u32[]{:S(2)}, u32[]{:S(2)}) collective-permute-start(bf16[192,1024]{1,0:T(8,128)(2,1)S(1)} %get-tuple-element.78), channel_id=1, source_target_pairs={{8,0},{16,8},{24,16},{32,24},{40,32},{48,40},{56,48},{64,56},{72,6... | collective-permute-start | bytes 1179656 | tf_op jit(solution)/shard_map/ppermute | solution.py:59
  102.8 4.2 %collective-permute-start.20 = (bf16[2,1024,384]{2,1,0:T(8,128)(2,1)S(1)}, bf16[2,1024,384]{2,1,0:T(8,128)(2,1)S(1)}, u32[]{:S(2)}, u32[]{:S(2)}) collective-permute-start(bf16[2,1024,384]{2,1,0:T(8,128)(2,1)S(1)} %get-tuple-element.79), channel_id=1, source_target_pairs={{0,8},{8,0},{16,24},{24,16},{32,40},{40,32},{48,56},{56,48},{64,72... | collective-permute-start | bytes 4718600 | tf_op jit(solution)/shard_map/ppermute | solution.py:54
  107.4 19.9 %collective-permute-start.27 = (bf16[1024,384]{1,0:T(8,128)(2,1)S(1)}, bf16[1024,384]{1,0:T(8,128)(2,1)S(1)}, u32[]{:S(2)}, u32[]{:S(2)}) collective-permute-start(bf16[1024,384]{1,0:T(8,128)(2,1)S(1)} %combine.2.refs_1_), channel_id=1, source_target_pairs={{0,16},{8,24},{16,0},{24,8},{32,48},{40,56},{48,32},{56,40},{64,80... | collective-permute-start | bytes 2359304 | tf_op jit(solution)/shard_map/ppermute | solution.py:63
  108.2 10.1 %collective-permute-start.25 = (bf16[256,512]{1,0:T(8,128)(2,1)S(1)}, bf16[256,512]{1,0:T(8,128)(2,1)S(1)}, u32[]{:S(2)}, u32[]{:S(2)}) collective-permute-start(bf16[256,512]{1,0:T(8,128)(2,1)S(1)} %get-tuple-element.92), channel_id=1, source_target_pairs={{0,64},{8,72},{16,80},{24,88},{32,96},{40,104},{48,112},{56,120},{... | collective-permute-start | bytes 786440 | tf_op jit(solution)/shard_map/ppermute | solution.py:50
  115.0 14.9 %collective-permute-start.21 = (bf16[256,1024]{1,0:T(8,128)(2,1)S(1)}, bf16[256,1024]{1,0:T(8,128)(2,1)S(1)}, u32[]{:S(2)}, u32[]{:S(2)}) collective-permute-start(bf16[256,1024]{1,0:T(8,128)(2,1)S(1)} %get-tuple-element.81.refs_0_), channel_id=1, source_target_pairs={{0,1},{1,2},{2,3},{3,0},{4,5},{5,6},{6,7},{7,4},{8,9},{9,10},{10,1... | collective-permute-start | bytes 1572872 | tf_op jit(solution)/shard_map/ppermute | solution.py:42
  115.7 14.2 %collective-permute-start.22 = (bf16[256,1024]{1,0:T(8,128)(2,1)S(1)}, bf16[256,1024]{1,0:T(8,128)(2,1)S(1)}, u32[]{:S(2)}, u32[]{:S(2)}) collective-permute-start(bf16[256,1024]{1,0:T(8,128)(2,1)S(1)} %get-tuple-element.82), channel_id=1, source_target_pairs={{0,3},{1,0},{2,1},{3,2},{4,7},{5,4},{6,5},{7,6},{8,11},{9,8},{10,9... | collective-permute-start | bytes 1572872 | tf_op jit(solution)/shard_map/ppermute | solution.py:42
  121.2 6.5 %collective-permute-start.26 = (bf16[2,1024,128]{2,1,0:T(8,128)(2,1)S(1)}, bf16[2,1024,128]{2,1,0:T(8,128)(2,1)S(1)}, u32[]{:S(2)}, u32[]{:S(2)}) collective-permute-start(bf16[2,1024,128]{2,1,0:T(8,128)(2,1)S(1)} %get-tuple-element.94), channel_id=1, source_target_pairs={{0,8},{8,0},{16,24},{24,16},{32,40},{40,32},{48,56},{56,48},{64,72... | collective-permute-start | bytes 1572872 | tf_op jit(solution)/shard_map/ppermute | solution.py:54
  127.8 7.9 %collective-permute-start.28 = (bf16[1024,128]{1,0:T(8,128)(2,1)S(1)}, bf16[1024,128]{1,0:T(8,128)(2,1)S(1)}, u32[]{:S(2)}, u32[]{:S(2)}) collective-permute-start(bf16[1024,128]{1,0:T(8,128)(2,1)S(1)} %combine.3), channel_id=1, source_target_pairs={{0,16},{8,24},{16,0},{24,8},{32,48},{40,56},{48,32},{56,40},{64,80... | collective-permute-start | bytes 786440 | tf_op jit(solution)/shard_map/ppermute | solution.py:63
  (39 other events, 161.0 us)

commit v5 on v4

--- a/solution.py
+++ b/solution.py
@@ -15,7 +15,7 @@
 PARTS = 4
 VMEM_LIMIT = 16 * 1024 * 1024
 VMEM_ALL = 60 * 1024 * 1024
-VMEM_MOST = 50 * 1024 * 1024
+VMEM_MOST = 48 * 1024 * 1024
 
 
 def cost(us):

time: 138 us -> 136 us (0.986)
  waiting for transfers between devices: 18.5 us -> 21.2 us
  Pallas kernels: 60 us -> 58 us
  other arithmetic: 5.31 us -> 3.82 us
    ppermute x9, waiting for transfers between devices: 0.02 us -> 2.56 us  [along_z(): return lax.ppermute(a, 'ctx', ctx_pairs(lambda z, yl, c: (z + d, yl, c)))]
    unnamed x84 -> x66, local copies, waits for them, and re-layouts: 6.35 us -> 6.27 us
  transfers between devices with their start and end apart: 29 -> 29, of which waited for: 5 -> 7; matrix products, arithmetic and copies ran while one was open for 5% -> 3% of each run, Pallas kernels for 43% -> 41%
where the time goes in v5:
time: 136 us
  Pallas kernels  58 us (43%)
  starting transfers between devices  44.6 us (33%)
  waiting for transfers between devices  21.2 us (16%)
  local copies, waits for them, and re-layouts  7.15 us (5%)
  other arithmetic  3.82 us (3%)
    ppermute x12, starting transfers between devices, along_x(): return lax.ppermute(a, 'tp', tp_pairs(lambda yh, x: (yh, x + d)))  18 us
    ppermute x9, starting transfers between devices, along_z(): return lax.ppermute(a, 'ctx', ctx_pairs(lambda z, yl, c: (z + d, yl, c)))  16.1 us
    pallas_call x3, Pallas kernels, project(): pl.pallas_call(functools.partial(project_kernel, n), grid_spec=pltpu.Pref...  13.6 us
    pallas_call x2, Pallas kernels, grad_product(): pl.pallas_call(functools.partial(grad_kernel, n, bool(rest)), grid_spec=p...  13.1 us
    ppermute x2, waiting for transfers between devices, across_yl(): return lax.ppermute(a, 'ctx', ctx_pairs(lambda z, yl, c: (z, yl + 1, c)))  9.93 us
    pallas_call x1, Pallas kernels, forward(): pl.pallas_call(forward_kernel, grid=(ch // LANES // PARTS,), in_specs=[co...  6.35 us
    unnamed x66, local copies, waits for them, and re-layouts  6.27 us
    pallas_call x2, Pallas kernels, weight_sum(): pl.pallas_call(functools.partial(weight_kernel, scale), grid=(ch // tile,...  6.1 us
  transfers between devices with their start and end apart: 29, of which 7 were waited for; matrix products, arithmetic and copies ran while one was open for 3% of the time, Pallas kernels for 41%

profile of v5, /device:TPU:0, one launch (start us, length us, event | category | flops | bytes accessed | tf_op | source)
XLA Modules:
  0.0 136.0 jit_solution(17558258425542784394)
XLA Ops:
  0.7 2.9 %collective-permute-start.3 = (bf16[256,1024]{1,0:T(8,128)(2,1)}, bf16[256,1024]{1,0:T(8,128)(2,1)S(1)}, u32[]{:S(2)}, u32[]{:S(2)}) collective-permute-start(bf16[256,1024]{1,0:T(8,128)(2,1)} %refs_0_.5), channel_id=1, source_target_pairs={{0,3},{1,0},{2,1},{3,2},{4,7},{5,4},{6,5},{7,6},{8,11},{9,8},{10,9... | collective-permute-start | bytes 1572872 | tf_op jit(solution)/shard_map/ppermute | solution.py:42
  3.6 3.2 %collective-permute-start.1 = (bf16[256,1024]{1,0:T(8,128)(2,1)}, bf16[256,1024]{1,0:T(8,128)(2,1)S(1)}, u32[]{:S(2)}, u32[]{:S(2)}) collective-permute-start(bf16[256,1024]{1,0:T(8,128)(2,1)} %refs_0_.5), channel_id=1, source_target_pairs={{0,4},{1,5},{2,6},{3,7},{4,0},{5,1},{6,2},{7,3},{8,12},{9,13},{10,... | collective-permute-start | bytes 1572872 | tf_op jit(solution)/shard_map/ppermute | solution.py:46
  6.8 3.1 %last_rows.1 = bf16[176,1024]{1,0:T(8,128)(2,1)} custom-call(bf16[256,1024]{1,0:T(8,128)(2,1)} %q.3, bf16[256,1024]{1,0:T(8,128)(2,1)} %k.3, bf16[256,1024]{1,0:T(8,128)(2,1)} %k.3, bf16[256,1024]{1,0:T(8,128)(2,1)} %v.3, bf16[256,1024]{1,0:T(8,128)(2,1)} %v.3, f32[3,7,1024]{2,1,0:T(8,128)} %sf.5), custom_call_target="tpu_custom_call" | custom-call | flops 4600000000 | bytes 65536 | tf_op jit(solution)/shard_map/last_rows/pallas_call | solution.py:432
  11.7 1.7 %toeplitz_table.1.table = bf16[8192,256]{1,0:T(8,128)(2,1)S(1)} custom-call(f32[64,256]{1,0:T(8,128)S(1)} %get-tuple-element.100.taps), custom_call_target="tpu_custom_call" | custom-call | flops 27599998976 | bytes 65536 | tf_op jit(solution)/shard_map/toeplitz_table/pallas_call | solution.py:92
  13.5 2.0 %copy-done.17 = bf16[8192,256]{1,0:T(8,128)(2,1)} copy-done((bf16[8192,256]{1,0:T(8,128)(2,1)}, bf16[8192,256]{1,0:T(8,128)(2,1)S(1)}, u32[]{:S(2)}) %copy-start.17) | copy-done | bytes 4194328
  16.5 3.6 %collective-permute-done.1.refs_0_.refs_3_.refs_2_ = bf16[256,1024]{1,0:T(8,128)(2,1)S(1)} collective-permute-done((bf16[256,1024]{1,0:T(8,128)(2,1)}, bf16[256,1024]{1,0:T(8,128)(2,1)S(1)}, u32[]{:S(2)}, u32[]{:S(2)}) %collective-permute-start.1) | collective-permute-done | bytes 524320 | tf_op jit(solution)/shard_map/ppermute | solution.py:46
  20.1 3.2 %collective-permute-start.5 = (bf16[256,1024]{1,0:T(8,128)(2,1)S(1)}, bf16[256,1024]{1,0:T(8,128)(2,1)S(1)}, u32[]{:S(2)}, u32[]{:S(2)}) collective-permute-start(bf16[256,1024]{1,0:T(8,128)(2,1)S(1)} %collective-permute-done.1.refs_0_.refs_3_.refs_2_), channel_id=1, source_target_pairs={{0,3},{1,0},{2,1},{3,2},{4,7},{5,4},{6,5},{7,6},{8,11},{9,8},{10,9... | collective-permute-start | bytes 1572872 | tf_op jit(solution)/shard_map/ppermute | solution.py:42
  24.5 6.4 %forward.1 = (f32[256,1024]{1,0:T(8,128)}, f32[256,1024]{1,0:T(8,128)}, f32[256,1024]{1,0:T(8,128)}, f32[256,1024]{1,0:T(8,128)}, bf16[256,1024]{1,0:T(8,128)(2,1)}, /*index=5*/bf16[1024,256]{1,0:T(8,128)(2,1)}) custom-call(bf16[256,1024]{1,0:T(8,128)(2,1)} %q.3, bf16[256,1024]{1,0:T(8,128)(2,1)} %k.3, bf16[256,1024]{1,0:T(8,128)(2,1)} %v.3, ...), custom_call_target="tpu_custom_call" | custom-call | flops 36800000000 | bytes 65536 | tf_op jit(solution)/shard_map/forward/pallas_call | solution.py:149
  30.8 4.0 %collective-permute-start.10 = (bf16[1024,256]{1,0:T(8,128)(2,1)}, bf16[1024,256]{1,0:T(8,128)(2,1)S(1)}, u32[]{:S(2)}, u32[]{:S(2)}) collective-permute-start(bf16[1024,256]{1,0:T(8,128)(2,1)} %get-tuple-element.54.refs_1_.refs_3_.q0), channel_id=1, source_target_pairs={{0,64},{8,72},{16,80},{24,88},{32,96},{40,104},{48,112},{56,120},{... | collective-permute-start | bytes 1572872 | tf_op jit(solution)/shard_map/ppermute | solution.py:50
  36.8 3.3 %collective-permute-start.7 = (bf16[256,1024]{1,0:T(8,128)(2,1)S(1)}, bf16[256,1024]{1,0:T(8,128)(2,1)S(1)}, u32[]{:S(2)}, u32[]{:S(2)}) collective-permute-start(bf16[256,1024]{1,0:T(8,128)(2,1)S(1)} %collective-permute-done.5.refs_3_.refs_5_), channel_id=1, source_target_pairs={{0,3},{1,0},{2,1},{3,2},{4,7},{5,4},{6,5},{7,6},{8,11},{9,8},{10,9... | collective-permute-start | bytes 1572872 | tf_op jit(solution)/shard_map/ppermute | solution.py:42
  42.2 6.2 %grad_product.2.refs_0_.refs_5_ = f32[256,1024]{1,0:T(8,128)S(1)} custom-call(s32[4]{0:T(128)S(1)} %fusion.3.cols, bf16[256,1024]{1,0:T(8,128)(2,1)S(1)} %copy-done.12, bf16[256,1024]{1,0:T(8,128)(2,1)S(1)} %copy-done.9, bf16[256,1024]{1,0:T(8,128)(2,1)S(1)} %collective-permute-done.4.refs_2_.refs_4_, ...), custom_call_target="tpu_custom_call" | custom-call | flops 29440000000 | bytes 65536 | tf_op jit(solution)/shard_map/grad_product/pallas_call | solution.py:295
  48.5 3.7 %project.3 = (bf16[256,1024]{1,0:T(8,128)(2,1)S(1)}, bf16[256,1024]{1,0:T(8,128)(2,1)S(1)}) custom-call(s32[2]{0:T(128)S(1)} %fusion.13.cols, bf16[256,1024]{1,0:T(8,128)(2,1)S(1)} %copy-done.18, bf16[1024,8192]{1,0:T(8,128)(2,1)} %refs_4_.3, f32[256,1024]{1,0:T(8,128)S(1)} %grad_product.2.refs_0_.refs_5_), custom_call_target="tpu_custom_call" | custom-call | flops 14720000000 | bytes 65536 | tf_op jit(solution)/shard_map/project/pallas_call | solution.py:328
  52.3 3.8 %select.66 = (bf16[256,1536]{1,0:T(8,128)(2,1)S(1)}, bf16[256,1536]{1,0:T(8,128)(2,1)}, bf16[256,1536]{1,0:T(8,128)(2,1)}, bf16[256,1536]{1,0:T(8,128)(2,1)}) custom-call(s32[9]{0:T(128)S(1)} %pad_add_fusion.places, bf16[256,1024]{1,0:T(8,128)(2,1)S(1)} %copy-done.3, bf16[256,1024]{1,0:T(8,128)(2,1)S(1)} %copy-done.13, bf16[256,1024]{1,0:T(8,128)(2,1)S(1)} %copy-done.10, ...), custom_call_target="tpu_custom_call" | custom-call | flops 11500000256 | bytes 65536 | tf_op jit(solution)/shard_map/select/pallas_call | solution.py:367
  56.1 3.2 %collective-permute-start.12 = (bf16[256,1024]{1,0:T(8,128)(2,1)S(1)}, bf16[256,1024]{1,0:T(8,128)(2,1)S(1)}, u32[]{:S(2)}, u32[]{:S(2)}) collective-permute-start(bf16[256,1024]{1,0:T(8,128)(2,1)S(1)} %get-tuple-element.58), channel_id=1, source_target_pairs={{0,3},{1,0},{2,1},{3,2},{4,7},{5,4},{6,5},{7,6},{8,11},{9,8},{10,9... | collective-permute-start | bytes 1572872 | tf_op jit(solution)/shard_map/ppermute | solution.py:42
  60.4 2.2 %collective-permute-start.14 = (bf16[256,1536]{1,0:T(8,128)(2,1)}, bf16[256,1536]{1,0:T(8,128)(2,1)S(1)}, u32[]{:S(2)}, u32[]{:S(2)}) collective-permute-start(bf16[256,1536]{1,0:T(8,128)(2,1)} %get-tuple-element.63), channel_id=1, source_target_pairs={{0,96},{8,104},{16,112},{24,120},{32,0},{40,8},{48,16},{56,24},{64... | collective-permute-start | bytes 2359304 | tf_op jit(solution)/shard_map/ppermute | solution.py:50
  62.6 1.8 %collective-permute-start.15 = (bf16[256,1536]{1,0:T(8,128)(2,1)}, bf16[256,1536]{1,0:T(8,128)(2,1)S(1)}, u32[]{:S(2)}, u32[]{:S(2)}) collective-permute-start(bf16[256,1536]{1,0:T(8,128)(2,1)} %get-tuple-element.64), channel_id=1, source_target_pairs={{0,64},{8,72},{16,80},{24,88},{32,96},{40,104},{48,112},{56,120},{... | collective-permute-start | bytes 2359304 | tf_op jit(solution)/shard_map/ppermute | solution.py:50
  64.4 3.7 %project.4 = (f32[256,1024]{1,0:T(8,128)S(1)}, bf16[256,1024]{1,0:T(8,128)(2,1)S(1)}) custom-call(s32[2]{0:T(128)S(1)} %fusion.9.cols, bf16[256,1024]{1,0:T(8,128)(2,1)S(1)} %copy-done.18, bf16[1024,8192]{1,0:T(8,128)(2,1)} %refs_4_.3, bf16[256,1536]{1,0:T(8,128)(2,1)S(1)} %get-tuple-element.53.refs_0_.g0, bf16[1024,256]{1,0:T(8,128)(2,1)S(1)} %copy-done, ...), custom_call_target="tpu_custom_call" | custom-call | flops 27599998976 | bytes 65536 | tf_op jit(solution)/shard_map/project/pallas_call | solution.py:328
  71.3 6.2 %project.5 = (bf16[256,1024]{1,0:T(8,128)(2,1)S(1)}, bf16[256,1024]{1,0:T(8,128)(2,1)S(1)}, bf16[256,1024]{1,0:T(8,128)(2,1)S(1)}, bf16[256,1024]{1,0:T(8,128)(2,1)S(1)}) custom-call(s32[4]{0:T(128)S(1)} %fusion.2.cols, bf16[256,1024]{1,0:T(8,128)(2,1)S(1)} %copy-done.19, bf16[1024,8192]{1,0:T(8,128)(2,1)} %refs_4_.3, ...), custom_call_target="tpu_custom_call" | custom-call | flops 36800000000 | bytes 65536 | tf_op jit(solution)/shard_map/project/pallas_call | solution.py:328
  77.6 2.0 %select.67 = (bf16[256,512]{1,0:T(8,128)(2,1)S(1)}, bf16[256,512]{1,0:T(8,128)(2,1)S(1)}, bf16[256,512]{1,0:T(8,128)(2,1)S(1)}, bf16[256,512]{1,0:T(8,128)(2,1)S(1)}) custom-call(s32[9]{0:T(128)S(1)} %pad_add_fusion.places, bf16[256,1024]{1,0:T(8,128)(2,1)S(1)} %copy-done.3, bf16[256,1024]{1,0:T(8,128)(2,1)S(1)} %copy-done.13, ...), custom_call_target="tpu_custom_call" | custom-call | flops 920000000 | bytes 65536 | tf_op jit(solution)/shard_map/select/pallas_call | solution.py:367
  79.6 6.9 %grad_product.3 = (bf16[256,1024]{1,0:T(8,128)(2,1)S(1)}, f32[256,1024]{1,0:T(8,128)S(1)}, bf16[192,1024]{1,0:T(8,128)(2,1)S(1)}) custom-call(s32[4]{0:T(128)S(1)} %get-tuple-element.95.cols, bf16[256,1024]{1,0:T(8,128)(2,1)S(1)} %copy-done.3, bf16[256,1024]{1,0:T(8,128)(2,1)S(1)} %collective-permute-done.6.refs_6_.refs_1_, bf16[256,1024]{1,0:T(8,128)(2,1)S(1)} %copy-done.5, ...), custom_call_target="tpu_custom_call" | custom-call | flops 920000000 | bytes 65536 | tf_op jit(solution)/shard_map/grad_product/pallas_call | solution.py:295
  87.9 2.4 %collective-permute-start.19 = (bf16[256,1024]{1,0:T(8,128)(2,1)S(1)}, bf16[256,1024]{1,0:T(8,128)(2,1)S(1)}, u32[]{:S(2)}, u32[]{:S(2)}) collective-permute-start(bf16[256,1024]{1,0:T(8,128)(2,1)S(1)} %add_convert_fusion.1.refs_1_), channel_id=1, source_target_pairs={{0,4},{1,5},{2,6},{3,7},{4,0},{5,1},{6,2},{7,3},{8,12},{9,13},{10,... | collective-permute-start | bytes 1572872 | tf_op jit(solution)/shard_map/ppermute | solution.py:46
  91.3 2.3 %collective-permute-start.24 = (bf16[256,512]{1,0:T(8,128)(2,1)S(1)}, bf16[256,512]{1,0:T(8,128)(2,1)S(1)}, u32[]{:S(2)}, u32[]{:S(2)}) collective-permute-start(bf16[256,512]{1,0:T(8,128)(2,1)S(1)} %get-tuple-element.90), channel_id=1, source_target_pairs={{0,96},{8,104},{16,112},{24,120},{32,0},{40,8},{48,16},{56,24},{64... | collective-permute-start | bytes 786440 | tf_op jit(solution)/shard_map/ppermute | solution.py:50
  93.6 2.5 %collective-permute-done.14.g2 = bf16[256,1536]{1,0:T(8,128)(2,1)S(1)} collective-permute-done((bf16[256,1536]{1,0:T(8,128)(2,1)}, bf16[256,1536]{1,0:T(8,128)(2,1)S(1)}, u32[]{:S(2)}, u32[]{:S(2)}) %collective-permute-start.14) | collective-permute-done | bytes 786464 | tf_op jit(solution)/shard_map/ppermute | solution.py:50
  97.4 4.2 %weight_sum.2 = (bf16[2,1024,384]{2,1,0:T(8,128)(2,1)S(1)}, bf16[2,1024,384]{2,1,0:T(8,128)(2,1)S(1)}) custom-call(bf16[1024,256]{1,0:T(8,128)(2,1)S(1)} %copy-done, bf16[1024,256]{1,0:T(8,128)(2,1)S(1)} %collective-permute-done.8.refs_2_.refs_4_.q1, bf16[1024,256]{1,0:T(8,128)(2,1)S(1)} %collective-permute-done.9.refs_3_.refs_5_.q2, ...), custom_call_target="tpu_custom_call" | custom-call | flops 920000000 | bytes 65536 | tf_op jit(solution)/shard_map/weight_sum/pallas_call | solution.py:398
  103.1 2.8 %collective-permute-done.20.from_core = bf16[2,1024,384]{2,1,0:T(8,128)(2,1)S(1)} collective-permute-done((bf16[2,1024,384]{2,1,0:T(8,128)(2,1)S(1)}, bf16[2,1024,384]{2,1,0:T(8,128)(2,1)S(1)}, u32[]{:S(2)}, u32[]{:S(2)}) %collective-permute-start.20) | collective-permute-done | bytes 1572896 | tf_op jit(solution)/shard_map/ppermute | solution.py:54
  106.8 1.9 %collective-permute-start.25 = (bf16[256,512]{1,0:T(8,128)(2,1)S(1)}, bf16[256,512]{1,0:T(8,128)(2,1)S(1)}, u32[]{:S(2)}, u32[]{:S(2)}) collective-permute-start(bf16[256,512]{1,0:T(8,128)(2,1)S(1)} %get-tuple-element.92), channel_id=1, source_target_pairs={{0,64},{8,72},{16,80},{24,88},{32,96},{40,104},{48,112},{56,120},{... | collective-permute-start | bytes 786440 | tf_op jit(solution)/shard_map/ppermute | solution.py:50
  108.7 5.6 %backward.1 = (bf16[256,1024]{1,0:T(8,128)(2,1)}, bf16[256,1024]{1,0:T(8,128)(2,1)}, bf16[256,1024]{1,0:T(8,128)(2,1)}) custom-call(bf16[256,1024]{1,0:T(8,128)(2,1)S(1)} %get-tuple-element.71.refs_0_.gc, f32[256,1024]{1,0:T(8,128)S(1)} %get-tuple-element.76.gq, f32[256,1024]{1,0:T(8,128)S(1)} %copy-done.7, f32[256,1024]{1,0:T(8,128)S(1)} %copy-done.6, ...), custom_call_target="tpu_custom_call" | custom-call | flops 36800000000 | bytes 65536 | tf_op jit(solution)/shard_map/backward/pallas_call | solution.py:216
  114.3 3.2 %collective-permute-start.22 = (bf16[256,1024]{1,0:T(8,128)(2,1)S(1)}, bf16[256,1024]{1,0:T(8,128)(2,1)S(1)}, u32[]{:S(2)}, u32[]{:S(2)}) collective-permute-start(bf16[256,1024]{1,0:T(8,128)(2,1)S(1)} %get-tuple-element.82), channel_id=1, source_target_pairs={{0,3},{1,0},{2,1},{3,2},{4,7},{5,4},{6,5},{7,6},{8,11},{9,8},{10,9... | collective-permute-start | bytes 1572872 | tf_op jit(solution)/shard_map/ppermute | solution.py:42
  118.6 1.9 %weight_sum.3 = (bf16[2,1024,128]{2,1,0:T(8,128)(2,1)S(1)}, bf16[2,1024,128]{2,1,0:T(8,128)(2,1)S(1)}) custom-call(bf16[1024,256]{1,0:T(8,128)(2,1)S(1)} %copy-done, bf16[1024,256]{1,0:T(8,128)(2,1)S(1)} %collective-permute-done.8.refs_2_.refs_4_.q1, bf16[1024,256]{1,0:T(8,128)(2,1)S(1)} %collective-permute-done.9.refs_3_.refs_5_.q2, ...), custom_call_target="tpu_custom_call" | custom-call | flops 920000000 | bytes 65536 | tf_op jit(solution)/shard_map/weight_sum/pallas_call | solution.py:398
  120.6 5.5 %collective-permute-done.27.from_yl = bf16[1024,384]{1,0:T(8,128)(2,1)S(1)} collective-permute-done((bf16[1024,384]{1,0:T(8,128)(2,1)S(1)}, bf16[1024,384]{1,0:T(8,128)(2,1)S(1)}, u32[]{:S(2)}, u32[]{:S(2)}) %collective-permute-start.27) | collective-permute-done | bytes 786464 | tf_op jit(solution)/shard_map/ppermute | solution.py:63
  127.0 1.9 %collective-permute-done.21 = bf16[256,1024]{1,0:T(8,128)(2,1)S(1)} collective-permute-done((bf16[256,1024]{1,0:T(8,128)(2,1)S(1)}, bf16[256,1024]{1,0:T(8,128)(2,1)S(1)}, u32[]{:S(2)}, u32[]{:S(2)}) %collective-permute-start.21) | collective-permute-done | bytes 524320 | tf_op jit(solution)/shard_map/ppermute | solution.py:42
  130.1 4.4 %collective-permute-done.28.from_yl = bf16[1024,128]{1,0:T(8,128)(2,1)S(1)} collective-permute-done((bf16[1024,128]{1,0:T(8,128)(2,1)S(1)}, bf16[1024,128]{1,0:T(8,128)(2,1)S(1)}, u32[]{:S(2)}, u32[]{:S(2)}) %collective-permute-start.28) | collective-permute-done | bytes 262176 | tf_op jit(solution)/shard_map/ppermute | solution.py:63
  (132 shorter events, 22.8 us)
Async XLA Ops:
  0.6 10.7 %copy-start.23 = (bf16[128,64]{0,1:T(8,128)(2,1)S(1)}, bf16[128,64]{0,1:T(8,128)(2,1)}, u32[]{:S(2)}) copy-start(bf16[128,64]{0,1:T(8,128)(2,1)} %param.25) | copy-start | bytes 49156
  0.7 22.7 %collective-permute-start.3 = (bf16[256,1024]{1,0:T(8,128)(2,1)}, bf16[256,1024]{1,0:T(8,128)(2,1)S(1)}, u32[]{:S(2)}, u32[]{:S(2)}) collective-permute-start(bf16[256,1024]{1,0:T(8,128)(2,1)} %refs_0_.5), channel_id=1, source_target_pairs={{0,3},{1,0},{2,1},{3,2},{4,7},{5,4},{6,5},{7,6},{8,11},{9,8},{10,9... | collective-permute-start | bytes 1572872 | tf_op jit(solution)/shard_map/ppermute | solution.py:42
  3.6 19.9 %collective-permute-start.2 = (bf16[256,1024]{1,0:T(8,128)(2,1)}, bf16[256,1024]{1,0:T(8,128)(2,1)S(1)}, u32[]{:S(2)}, u32[]{:S(2)}) collective-permute-start(bf16[256,1024]{1,0:T(8,128)(2,1)} %refs_0_.5), channel_id=1, source_target_pairs={{0,1},{1,2},{2,3},{3,0},{4,5},{5,6},{6,7},{7,4},{8,9},{9,10},{10,1... | collective-permute-start | bytes 1572872 | tf_op jit(solution)/shard_map/ppermute | solution.py:42
  3.6 16.6 %collective-permute-start.1 = (bf16[256,1024]{1,0:T(8,128)(2,1)}, bf16[256,1024]{1,0:T(8,128)(2,1)S(1)}, u32[]{:S(2)}, u32[]{:S(2)}) collective-permute-start(bf16[256,1024]{1,0:T(8,128)(2,1)} %refs_0_.5), channel_id=1, source_target_pairs={{0,4},{1,5},{2,6},{3,7},{4,0},{5,1},{6,2},{7,3},{8,12},{9,13},{10,... | collective-permute-start | bytes 1572872 | tf_op jit(solution)/shard_map/ppermute | solution.py:46
  9.9 13.5 %collective-permute-start = (bf16[176,1024]{1,0:T(8,128)(2,1)}, bf16[176,1024]{1,0:T(8,128)(2,1)S(1)}, u32[]{:S(2)}, u32[]{:S(2)}) collective-permute-start(bf16[176,1024]{1,0:T(8,128)(2,1)} %last_rows.1), channel_id=1, source_target_pairs={{0,8},{8,16},{16,24},{24,32},{32,40},{40,48},{48,56},{56,64},{64,7... | collective-permute-start | bytes 1081352 | tf_op jit(solution)/shard_map/ppermute | solution.py:59
  20.1 16.7 %collective-permute-start.5 = (bf16[256,1024]{1,0:T(8,128)(2,1)S(1)}, bf16[256,1024]{1,0:T(8,128)(2,1)S(1)}, u32[]{:S(2)}, u32[]{:S(2)}) collective-permute-start(bf16[256,1024]{1,0:T(8,128)(2,1)S(1)} %collective-permute-done.1.refs_0_.refs_3_.refs_2_), channel_id=1, source_target_pairs={{0,3},{1,0},{2,1},{3,2},{4,7},{5,4},{6,5},{7,6},{8,11},{9,8},{10,9... | collective-permute-start | bytes 1572872 | tf_op jit(solution)/shard_map/ppermute | solution.py:42
  23.4 13.4 %collective-permute-start.4 = (bf16[256,1024]{1,0:T(8,128)(2,1)S(1)}, bf16[256,1024]{1,0:T(8,128)(2,1)S(1)}, u32[]{:S(2)}, u32[]{:S(2)}) collective-permute-start(bf16[256,1024]{1,0:T(8,128)(2,1)S(1)} %collective-permute-done.1.refs_0_.refs_3_.refs_2_), channel_id=1, source_target_pairs={{0,1},{1,2},{2,3},{3,0},{4,5},{5,6},{6,7},{7,4},{8,9},{9,10},{10,1... | collective-permute-start | bytes 1572872 | tf_op jit(solution)/shard_map/ppermute | solution.py:42
  30.8 28.5 %collective-permute-start.10 = (bf16[1024,256]{1,0:T(8,128)(2,1)}, bf16[1024,256]{1,0:T(8,128)(2,1)S(1)}, u32[]{:S(2)}, u32[]{:S(2)}) collective-permute-start(bf16[1024,256]{1,0:T(8,128)(2,1)} %get-tuple-element.54.refs_1_.refs_3_.q0), channel_id=1, source_target_pairs={{0,64},{8,72},{16,80},{24,88},{32,96},{40,104},{48,112},{56,120},{... | collective-permute-start | bytes 1572872 | tf_op jit(solution)/shard_map/ppermute | solution.py:50
  34.8 25.6 %collective-permute-start.9 = (bf16[1024,256]{1,0:T(8,128)(2,1)}, bf16[1024,256]{1,0:T(8,128)(2,1)S(1)}, u32[]{:S(2)}, u32[]{:S(2)}) collective-permute-start(bf16[1024,256]{1,0:T(8,128)(2,1)} %get-tuple-element.54.refs_1_.refs_3_.q0), channel_id=1, source_target_pairs={{0,96},{8,104},{16,112},{24,120},{32,0},{40,8},{48,16},{56,24},{64... | collective-permute-start | bytes 1572872 | tf_op jit(solution)/shard_map/ppermute | solution.py:50
  35.5 27.1 %collective-permute-start.8 = (bf16[1024,256]{1,0:T(8,128)(2,1)}, bf16[1024,256]{1,0:T(8,128)(2,1)S(1)}, u32[]{:S(2)}, u32[]{:S(2)}) collective-permute-start(bf16[1024,256]{1,0:T(8,128)(2,1)} %get-tuple-element.54.refs_1_.refs_3_.q0), channel_id=1, source_target_pairs={{0,32},{8,40},{16,48},{24,56},{32,64},{40,72},{48,80},{56,88},{64,... | collective-permute-start | bytes 1572872 | tf_op jit(solution)/shard_map/ppermute | solution.py:50
  36.8 15.4 %collective-permute-start.6 = (bf16[256,1024]{1,0:T(8,128)(2,1)}, bf16[256,1024]{1,0:T(8,128)(2,1)S(1)}, u32[]{:S(2)}, u32[]{:S(2)}) collective-permute-start(bf16[256,1024]{1,0:T(8,128)(2,1)} %copy-done.11), channel_id=1, source_target_pairs={{0,1},{1,2},{2,3},{3,0},{4,5},{5,6},{6,7},{7,4},{8,9},{9,10},{10,1... | collective-permute-start | bytes 1572872 | tf_op jit(solution)/shard_map/ppermute | solution.py:42
  36.8 15.4 %collective-permute-start.7 = (bf16[256,1024]{1,0:T(8,128)(2,1)S(1)}, bf16[256,1024]{1,0:T(8,128)(2,1)S(1)}, u32[]{:S(2)}, u32[]{:S(2)}) collective-permute-start(bf16[256,1024]{1,0:T(8,128)(2,1)S(1)} %collective-permute-done.5.refs_3_.refs_5_), channel_id=1, source_target_pairs={{0,3},{1,0},{2,1},{3,2},{4,7},{5,4},{6,5},{7,6},{8,11},{9,8},{10,9... | collective-permute-start | bytes 1572872 | tf_op jit(solution)/shard_map/ppermute | solution.py:42
  52.3 12.1 %copy-start = (bf16[1024,256]{1,0:T(8,128)(2,1)S(1)}, bf16[1024,256]{1,0:T(8,128)(2,1)}, u32[]{:S(2)}) copy-start(bf16[1024,256]{1,0:T(8,128)(2,1)} %get-tuple-element.54.refs_1_.refs_3_.q0) | copy-start | bytes 1572868
  56.0 12.3 %collective-permute-start.11 = (bf16[256,1024]{1,0:T(8,128)(2,1)S(1)}, bf16[256,1024]{1,0:T(8,128)(2,1)S(1)}, u32[]{:S(2)}, u32[]{:S(2)}) collective-permute-start(bf16[256,1024]{1,0:T(8,128)(2,1)S(1)} %get-tuple-element.57.refs_8_), channel_id=1, source_target_pairs={{0,1},{1,2},{2,3},{3,0},{4,5},{5,6},{6,7},{7,4},{8,9},{9,10},{10,1... | collective-permute-start | bytes 1572872 | tf_op jit(solution)/shard_map/ppermute | solution.py:42
  56.1 13.6 %collective-permute-start.12 = (bf16[256,1024]{1,0:T(8,128)(2,1)S(1)}, bf16[256,1024]{1,0:T(8,128)(2,1)S(1)}, u32[]{:S(2)}, u32[]{:S(2)}) collective-permute-start(bf16[256,1024]{1,0:T(8,128)(2,1)S(1)} %get-tuple-element.58), channel_id=1, source_target_pairs={{0,3},{1,0},{2,1},{3,2},{4,7},{5,4},{6,5},{7,6},{8,11},{9,8},{10,9... | collective-permute-start | bytes 1572872 | tf_op jit(solution)/shard_map/ppermute | solution.py:42
  59.4 31.9 %collective-permute-start.13 = (bf16[256,1536]{1,0:T(8,128)(2,1)}, bf16[256,1536]{1,0:T(8,128)(2,1)S(1)}, u32[]{:S(2)}, u32[]{:S(2)}) collective-permute-start(bf16[256,1536]{1,0:T(8,128)(2,1)} %get-tuple-element.62), channel_id=1, source_target_pairs={{0,32},{8,40},{16,48},{24,56},{32,64},{40,72},{48,80},{56,88},{64,... | collective-permute-start | bytes 2359304 | tf_op jit(solution)/shard_map/ppermute | solution.py:50
  60.4 35.7 %collective-permute-start.14 = (bf16[256,1536]{1,0:T(8,128)(2,1)}, bf16[256,1536]{1,0:T(8,128)(2,1)S(1)}, u32[]{:S(2)}, u32[]{:S(2)}) collective-permute-start(bf16[256,1536]{1,0:T(8,128)(2,1)} %get-tuple-element.63), channel_id=1, source_target_pairs={{0,96},{8,104},{16,112},{24,120},{32,0},{40,8},{48,16},{56,24},{64... | collective-permute-start | bytes 2359304 | tf_op jit(solution)/shard_map/ppermute | solution.py:50
  62.6 34.8 %collective-permute-start.15 = (bf16[256,1536]{1,0:T(8,128)(2,1)}, bf16[256,1536]{1,0:T(8,128)(2,1)S(1)}, u32[]{:S(2)}, u32[]{:S(2)}) collective-permute-start(bf16[256,1536]{1,0:T(8,128)(2,1)} %get-tuple-element.64), channel_id=1, source_target_pairs={{0,64},{8,72},{16,80},{24,88},{32,96},{40,104},{48,112},{56,120},{... | collective-permute-start | bytes 2359304 | tf_op jit(solution)/shard_map/ppermute | solution.py:50
  68.3 18.2 %collective-permute-start.17 = (bf16[256,1024]{1,0:T(8,128)(2,1)S(1)}, bf16[256,1024]{1,0:T(8,128)(2,1)}, u32[]{:S(2)}, u32[]{:S(2)}) collective-permute-start(bf16[256,1024]{1,0:T(8,128)(2,1)S(1)} %get-tuple-element.55.refs_0_), channel_id=1, source_target_pairs={{0,3},{1,0},{2,1},{3,2},{4,7},{5,4},{6,5},{7,6},{8,11},{9,8},{10,9... | collective-permute-start | bytes 1572872 | tf_op jit(solution)/shard_map/ppermute | solution.py:42
  69.7 16.8 %collective-permute-start.16 = (bf16[256,1024]{1,0:T(8,128)(2,1)}, bf16[256,1024]{1,0:T(8,128)(2,1)S(1)}, u32[]{:S(2)}, u32[]{:S(2)}) collective-permute-start(bf16[256,1024]{1,0:T(8,128)(2,1)} %add_convert_fusion.2), channel_id=1, source_target_pairs={{0,1},{1,2},{2,3},{3,0},{4,5},{5,6},{6,7},{7,4},{8,9},{9,10},{10,1... | collective-permute-start | bytes 1572872 | tf_op jit(solution)/shard_map/ppermute | solution.py:42
  86.5 10.9 %copy-start.2 = (bf16[1024,256]{1,0:T(8,128)(2,1)S(1)}, bf16[1024,256]{1,0:T(8,128)(2,1)}, u32[]{:S(2)}) copy-start(bf16[1024,256]{1,0:T(8,128)(2,1)} %copy-done.1) | copy-start | bytes 1572868
  87.9 20.8 %collective-permute-start.19 = (bf16[256,1024]{1,0:T(8,128)(2,1)S(1)}, bf16[256,1024]{1,0:T(8,128)(2,1)S(1)}, u32[]{:S(2)}, u32[]{:S(2)}) collective-permute-start(bf16[256,1024]{1,0:T(8,128)(2,1)S(1)} %add_convert_fusion.1.refs_1_), channel_id=1, source_target_pairs={{0,4},{1,5},{2,6},{3,7},{4,0},{5,1},{6,2},{7,3},{8,12},{9,13},{10,... | collective-permute-start | bytes 1572872 | tf_op jit(solution)/shard_map/ppermute | solution.py:46
  90.3 24.0 %collective-permute-start.23 = (bf16[256,512]{1,0:T(8,128)(2,1)S(1)}, bf16[256,512]{1,0:T(8,128)(2,1)S(1)}, u32[]{:S(2)}, u32[]{:S(2)}) collective-permute-start(bf16[256,512]{1,0:T(8,128)(2,1)S(1)} %get-tuple-element.89), channel_id=1, source_target_pairs={{0,32},{8,40},{16,48},{24,56},{32,64},{40,72},{48,80},{56,88},{64,... | collective-permute-start | bytes 786440 | tf_op jit(solution)/shard_map/ppermute | solution.py:50
  91.3 26.3 %collective-permute-start.24 = (bf16[256,512]{1,0:T(8,128)(2,1)S(1)}, bf16[256,512]{1,0:T(8,128)(2,1)S(1)}, u32[]{:S(2)}, u32[]{:S(2)}) collective-permute-start(bf16[256,512]{1,0:T(8,128)(2,1)S(1)} %get-tuple-element.90), channel_id=1, source_target_pairs={{0,96},{8,104},{16,112},{24,120},{32,0},{40,8},{48,16},{56,24},{64... | collective-permute-start | bytes 786440 | tf_op jit(solution)/shard_map/ppermute | solution.py:50
  96.1 10.7 %collective-permute-start.18 = (bf16[192,1024]{1,0:T(8,128)(2,1)S(1)}, bf16[192,1024]{1,0:T(8,128)(2,1)S(1)}, u32[]{:S(2)}, u32[]{:S(2)}) collective-permute-start(bf16[192,1024]{1,0:T(8,128)(2,1)S(1)} %get-tuple-element.78), channel_id=1, source_target_pairs={{8,0},{16,8},{24,16},{32,24},{40,32},{48,40},{56,48},{64,56},{72,6... | collective-permute-start | bytes 1179656 | tf_op jit(solution)/shard_map/ppermute | solution.py:59
  101.7 4.2 %collective-permute-start.20 = (bf16[2,1024,384]{2,1,0:T(8,128)(2,1)S(1)}, bf16[2,1024,384]{2,1,0:T(8,128)(2,1)S(1)}, u32[]{:S(2)}, u32[]{:S(2)}) collective-permute-start(bf16[2,1024,384]{2,1,0:T(8,128)(2,1)S(1)} %get-tuple-element.79), channel_id=1, source_target_pairs={{0,8},{8,0},{16,24},{24,16},{32,40},{40,32},{48,56},{56,48},{64,72... | collective-permute-start | bytes 4718600 | tf_op jit(solution)/shard_map/ppermute | solution.py:54
  106.2 19.9 %collective-permute-start.27 = (bf16[1024,384]{1,0:T(8,128)(2,1)S(1)}, bf16[1024,384]{1,0:T(8,128)(2,1)S(1)}, u32[]{:S(2)}, u32[]{:S(2)}) collective-permute-start(bf16[1024,384]{1,0:T(8,128)(2,1)S(1)} %combine.2.refs_1_), channel_id=1, source_target_pairs={{0,16},{8,24},{16,0},{24,8},{32,48},{40,56},{48,32},{56,40},{64,80... | collective-permute-start | bytes 2359304 | tf_op jit(solution)/shard_map/ppermute | solution.py:63
  106.8 10.7 %collective-permute-start.25 = (bf16[256,512]{1,0:T(8,128)(2,1)S(1)}, bf16[256,512]{1,0:T(8,128)(2,1)S(1)}, u32[]{:S(2)}, u32[]{:S(2)}) collective-permute-start(bf16[256,512]{1,0:T(8,128)(2,1)S(1)} %get-tuple-element.92), channel_id=1, source_target_pairs={{0,64},{8,72},{16,80},{24,88},{32,96},{40,104},{48,112},{56,120},{... | collective-permute-start | bytes 786440 | tf_op jit(solution)/shard_map/ppermute | solution.py:50
  114.3 14.6 %collective-permute-start.21 = (bf16[256,1024]{1,0:T(8,128)(2,1)S(1)}, bf16[256,1024]{1,0:T(8,128)(2,1)S(1)}, u32[]{:S(2)}, u32[]{:S(2)}) collective-permute-start(bf16[256,1024]{1,0:T(8,128)(2,1)S(1)} %get-tuple-element.81.refs_0_), channel_id=1, source_target_pairs={{0,1},{1,2},{2,3},{3,0},{4,5},{5,6},{6,7},{7,4},{8,9},{9,10},{10,1... | collective-permute-start | bytes 1572872 | tf_op jit(solution)/shard_map/ppermute | solution.py:42
  114.3 14.6 %collective-permute-start.22 = (bf16[256,1024]{1,0:T(8,128)(2,1)S(1)}, bf16[256,1024]{1,0:T(8,128)(2,1)S(1)}, u32[]{:S(2)}, u32[]{:S(2)}) collective-permute-start(bf16[256,1024]{1,0:T(8,128)(2,1)S(1)} %get-tuple-element.82), channel_id=1, source_target_pairs={{0,3},{1,0},{2,1},{3,2},{4,7},{5,4},{6,5},{7,6},{8,11},{9,8},{10,9... | collective-permute-start | bytes 1572872 | tf_op jit(solution)/shard_map/ppermute | solution.py:42
  120.5 6.0 %collective-permute-start.26 = (bf16[2,1024,128]{2,1,0:T(8,128)(2,1)S(1)}, bf16[2,1024,128]{2,1,0:T(8,128)(2,1)S(1)}, u32[]{:S(2)}, u32[]{:S(2)}) collective-permute-start(bf16[2,1024,128]{2,1,0:T(8,128)(2,1)S(1)} %get-tuple-element.94), channel_id=1, source_target_pairs={{0,8},{8,0},{16,24},{24,16},{32,40},{40,32},{48,56},{56,48},{64,72... | collective-permute-start | bytes 1572872 | tf_op jit(solution)/shard_map/ppermute | solution.py:54
  126.6 7.9 %collective-permute-start.28 = (bf16[1024,128]{1,0:T(8,128)(2,1)S(1)}, bf16[1024,128]{1,0:T(8,128)(2,1)S(1)}, u32[]{:S(2)}, u32[]{:S(2)}) collective-permute-start(bf16[1024,128]{1,0:T(8,128)(2,1)S(1)} %combine.3), channel_id=1, source_target_pairs={{0,16},{8,24},{16,0},{24,8},{32,48},{40,56},{48,32},{56,40},{64,80... | collective-permute-start | bytes 786440 | tf_op jit(solution)/shard_map/ppermute | solution.py:63
  (30 other events, 102.0 us)
